TPU v7x, 128 devices: a whole 4x4x4 slice. The times are simulated.
128 devices in a mesh: seq: 32 (over x, z, core), head: 4 (over y).
Axes of the slice: x: 4, y: 4, z: 4, core: 2. Of those that a mesh axis runs over, the one named last changes fastest.
Arguments:
- queries: bfloat16 [16384, 4096], P(('head', 'seq')), may hold values from -6 to 6
- keys: bfloat16 [16384, 4096], P(('head', 'seq')), may hold values from -6 to 6
- values: bfloat16 [16384, 4096], P(('head', 'seq')), may hold values from -6 to 6
- key_blocks: int32 [32, 128, 48], P('seq'), may hold values from 0 to 127, as said below
- key_count: int32 [32, 128], P('seq'), may hold values from 1 to 48, as said below
Outputs:
- attended: bfloat16 [16384, 4096], P(('head', 'seq'))
Inputs may be any that keep to these rules, and one draw needn't show every extreme that they name: `key_blocks`: entries of one list are distinct; the first entry is the query block itself. `key_count`: heads differ in how many key blocks their query blocks use.
All inputs are finite; a program needn't handle non-finite values.
Results may differ from a plain program's by a relative error of at most 0.0046.
Values may be sent and summed in bfloat16 or wider, within the bound.
No kernel may reach another device: no remote copies, remote signals or barrier semaphores. Data moves between devices by JAX's collectives and lax.ppermute only.
A program may use at most 128 MiB of HBM per device.

v0:
```python
import jax
import jax.numpy as jnp
from jax import lax
from jax.sharding import PartitionSpec as P

BLOCK = 128


def select_blocks(indices, kv_flat, hdim):
    block_total = kv_flat.shape[0]
    table = jnp.arange(block_total, dtype=jnp.int32)
    flat_index = indices.reshape(-1)
    onehot = (flat_index[:, None] == table[None, :]).astype(jnp.bfloat16)
    picked = jnp.dot(onehot, kv_flat, preferred_element_type=jnp.float32).astype(jnp.bfloat16)
    half = kv_flat.shape[1] // 2
    key_rows = picked[:, :half].reshape(indices.shape + (BLOCK, hdim))
    val_rows = picked[:, half:].reshape(indices.shape + (BLOCK, hdim))
    return (key_rows, val_rows)


def padded_attention(q_rows, kv_flat, lists, counts, scale):
    q_count = lists.shape[0]
    listed_most = lists.shape[1]
    hdim = q_rows.shape[1]
    group = 1
    for cand in range(1, q_count + 1):
        if q_count % cand == 0 and cand * BLOCK <= 512:
            group = cand
    q_grouped = q_rows.reshape(q_count // group, group, BLOCK, hdim)
    list_grouped = lists.reshape(q_count // group, group, listed_most)
    count_grouped = counts.reshape(q_count // group, group)
    slot_block = jnp.arange(listed_most * BLOCK, dtype=jnp.int32) // BLOCK

    def one_group(inner):
        q_part, list_part, count_part = inner
        key_sel, val_sel = select_blocks(list_part, kv_flat, hdim)
        key_rows = key_sel.reshape(group, listed_most * BLOCK, hdim)
        val_rows = val_sel.reshape(group, listed_most * BLOCK, hdim)
        score = (
            jnp.einsum("qth,qkh->qtk", q_part, key_rows, preferred_element_type=jnp.float32) * scale
        )
        valid = slot_block[None, None, :] < count_part[:, None, None]
        score = jnp.where(valid, score, -jnp.inf)
        top = jnp.max(score, axis=2, keepdims=True)
        weight = jnp.exp(score - top)
        total = jnp.sum(weight, axis=2, keepdims=True)
        weight_b = weight.astype(jnp.bfloat16)
        summed = jnp.einsum("qtk,qkh->qth", weight_b, val_rows, preferred_element_type=jnp.float32)
        return (summed / total).astype(jnp.bfloat16)

    result = lax.map(one_group, (q_grouped, list_grouped, count_grouped))
    return result.reshape(q_count * BLOCK, hdim)


def local(queries, keys, values, key_blocks, key_count):
    seq_count = lax.axis_size("seq")
    tok_dev, width = queries.shape
    hdim = width // seq_count
    scale = 1.0 / hdim**0.5
    q_mine = lax.all_to_all(queries, "seq", split_axis=1, concat_axis=0, tiled=True)
    k_group, v_group = (
        lax.all_gather(keys[None], "head", axis=0, tiled=True),
        lax.all_gather(values[None], "head", axis=0, tiled=True),
    )
    k_moved, v_moved = (
        lax.all_to_all(k_group, "seq", split_axis=2, concat_axis=1, tiled=True),
        lax.all_to_all(v_group, "seq", split_axis=2, concat_axis=1, tiled=True),
    )
    k_all = k_moved.reshape(-1, hdim)
    v_all = v_moved.reshape(-1, hdim)
    block_total = k_all.shape[0] // BLOCK
    kv_flat = jnp.concatenate(
        (k_all.reshape(block_total, BLOCK * hdim), v_all.reshape(block_total, BLOCK * hdim)), axis=1
    )
    q_count = q_mine.shape[0] // BLOCK
    first_block = lax.axis_index("head") * q_count
    lists = lax.dynamic_slice_in_dim(key_blocks[0], first_block, q_count, 0)
    counts = lax.dynamic_slice_in_dim(key_count[0], first_block, q_count, 0)
    result = padded_attention(q_mine, kv_flat, lists, counts, scale)
    return lax.all_to_all(result, "seq", split_axis=0, concat_axis=1, tiled=True)


def solution(mesh):
    placed = (
        P(("head", "seq"), None),
        P(("head", "seq"), None),
        P(("head", "seq"), None),
        P("seq", None, None),
        P("seq", None),
    )
    return jax.shard_map(
        local, mesh=mesh, in_specs=placed, out_specs=P(("head", "seq"), None), check_vma=False
    )
```

profile of v0, /device:TPU:0, one launch (start us, length us, event | category | flops | bytes accessed | tf_op | source)
XLA Modules:
  0.0 707.2 jit_solution(17578829605792613730)
XLA Ops:
  8.0 51.8 %all-gather.7.cloned.1.call-done = bf16[512,4096]{1,0:T(8,128)(2,1)} async-done(((bf16[128,4096]{1,0:T(8,128)(2,1)}), bf16[512,4096]{1,0:T(8,128)(2,1)}) %all-gather.7.cloned.1.call-update) | async-done | bytes 4194320 | tf_op jit(solution)/shard_map/all_gather | solution.py:63
  74.6 35.5 %all-gather.5.cloned.1.call-done = bf16[512,4096]{1,0:T(8,128)(2,1)} async-done(((bf16[128,4096]{1,0:T(8,128)(2,1)}), bf16[512,4096]{1,0:T(8,128)(2,1)}) %all-gather.5.cloned.1.call-update) | async-done | bytes 4194320 | tf_op jit(solution)/shard_map/all_gather | solution.py:62
  146.7 40.1 %all-to-all-done.1 = bf16[4,128,4096]{1,0,2:T(4,128)(2,1)} async-done(((bf16[4,128,4096]{1,0,2:T(4,128)(2,1)}), bf16[4,128,4096]{1,0,2:T(4,128)(2,1)}, u32[]{:S(2)}, u32[]{:S(2)}) %all-to-all-start.1) | async-done | bytes 4194336 | tf_op jit(solution)/shard_map/all_to_all | solution.py:66
  204.3 12.7 %copy_bitcast_fusion = (bf16[128,16384]{1,0:T(8,128)(2,1)}, bf16[128,16384]{1,0:T(8,128)(2,1)}) fusion(bf16[16,8,128,128]{3,2,1,0:T(8,128)(2,1)} %bitcast.57, bf16[16,8,128,128]{3,2,1,0:T(8,128)(2,1)} %bitcast.58), kind=kLoop, calls=%fused_computation.36 | loop fusion | bytes 16777216 | tf_op jit(solution)/shard_map/reshape;reshape | solution.py:73
  224.4 449.8 %while.11 = (s32[]{:T(128)}, bf16[8,4,128,128]{3,2,1,0:T(8,128)(2,1)S(1)}, s32[8,4]{1,0:T(8,128)S(1)}, bf16[8,4,128,128]{3,2,1,0:T(8,128)(2,1)S(1)}, s32[8,4,48]...) while((s32[]{:T(128)}, bf16[8,4,128,128]{3,2,1,0:T(8,128)(2,1)S(1)}, ...), condition=%wide.region_3.4_spmd.clone, body=%wide.region_0.3_spmd.clone.sunk | while | flops 3262348288 | bytes 122058640 | solution.py:51
  224.7 11.4 %convolution_convert_fusion.2 = bf16[192,32768]{1,0:T(8,128)(2,1)} fusion(bf16[128,32768]{1,0:T(8,128)(2,1)} %get-tuple-element.139, s32[192]{0:T(256)S(1)} %eq.34), kind=kOutput, calls=%fused_computation.1.clone.1 | convolution fusion | flops 1616928768 | bytes 20972288 | tf_op jit(solution)/shard_map/while/body/eval_jaxpr/dot_general | solution.py:14
  256.7 10.4 %reshape.84 = bf16[4,6144,128]{2,1,0:T(8,128)(2,1)} reshape(bf16[192,16384]{1,0:T(8,128)(2,1)} %get-tuple-element.117) | data formatting | bytes 12582912 | tf_op jit(solution)/shard_map/while/body/eval_jaxpr/reshape;while/body/eval_jaxpr/reshape | solution.py:37
  280.9 11.4 %convolution_convert_fusion.2 = bf16[192,32768]{1,0:T(8,128)(2,1)} fusion(bf16[128,32768]{1,0:T(8,128)(2,1)} %get-tuple-element.139, s32[192]{0:T(256)S(1)} %eq.34), kind=kOutput, calls=%fused_computation.1.clone.1 | convolution fusion | flops 1616928768 | bytes 20972288 | tf_op jit(solution)/shard_map/while/body/eval_jaxpr/dot_general | solution.py:14
  302.6 10.4 %reshape.83 = bf16[4,6144,128]{2,1,0:T(8,128)(2,1)} reshape(bf16[192,16384]{1,0:T(8,128)(2,1)} %get-tuple-element.116) | data formatting | bytes 12582912 | tf_op jit(solution)/shard_map/while/body/eval_jaxpr/reshape;while/body/eval_jaxpr/reshape | solution.py:38
  313.0 10.4 %reshape.84 = bf16[4,6144,128]{2,1,0:T(8,128)(2,1)} reshape(bf16[192,16384]{1,0:T(8,128)(2,1)} %get-tuple-element.117) | data formatting | bytes 12582912 | tf_op jit(solution)/shard_map/while/body/eval_jaxpr/reshape;while/body/eval_jaxpr/reshape | solution.py:37
  337.1 11.4 %convolution_convert_fusion.2 = bf16[192,32768]{1,0:T(8,128)(2,1)} fusion(bf16[128,32768]{1,0:T(8,128)(2,1)} %get-tuple-element.139, s32[192]{0:T(256)S(1)} %eq.34), kind=kOutput, calls=%fused_computation.1.clone.1 | convolution fusion | flops 1616928768 | bytes 20972288 | tf_op jit(solution)/shard_map/while/body/eval_jaxpr/dot_general | solution.py:14
  369.2 10.4 %reshape.84 = bf16[4,6144,128]{2,1,0:T(8,128)(2,1)} reshape(bf16[192,16384]{1,0:T(8,128)(2,1)} %get-tuple-element.117) | data formatting | bytes 12582912 | tf_op jit(solution)/shard_map/while/body/eval_jaxpr/reshape;while/body/eval_jaxpr/reshape | solution.py:37
  393.3 11.4 %convolution_convert_fusion.2 = bf16[192,32768]{1,0:T(8,128)(2,1)} fusion(bf16[128,32768]{1,0:T(8,128)(2,1)} %get-tuple-element.139, s32[192]{0:T(256)S(1)} %eq.34), kind=kOutput, calls=%fused_computation.1.clone.1 | convolution fusion | flops 1616928768 | bytes 20972288 | tf_op jit(solution)/shard_map/while/body/eval_jaxpr/dot_general | solution.py:14
  415.0 10.4 %reshape.83 = bf16[4,6144,128]{2,1,0:T(8,128)(2,1)} reshape(bf16[192,16384]{1,0:T(8,128)(2,1)} %get-tuple-element.116) | data formatting | bytes 12582912 | tf_op jit(solution)/shard_map/while/body/eval_jaxpr/reshape;while/body/eval_jaxpr/reshape | solution.py:38
  425.4 10.4 %reshape.84 = bf16[4,6144,128]{2,1,0:T(8,128)(2,1)} reshape(bf16[192,16384]{1,0:T(8,128)(2,1)} %get-tuple-element.117) | data formatting | bytes 12582912 | tf_op jit(solution)/shard_map/while/body/eval_jaxpr/reshape;while/body/eval_jaxpr/reshape | solution.py:37
  449.6 11.4 %convolution_convert_fusion.2 = bf16[192,32768]{1,0:T(8,128)(2,1)} fusion(bf16[128,32768]{1,0:T(8,128)(2,1)} %get-tuple-element.139, s32[192]{0:T(256)S(1)} %eq.34), kind=kOutput, calls=%fused_computation.1.clone.1 | convolution fusion | flops 1616928768 | bytes 20972288 | tf_op jit(solution)/shard_map/while/body/eval_jaxpr/dot_general | solution.py:14
  481.6 10.4 %reshape.84 = bf16[4,6144,128]{2,1,0:T(8,128)(2,1)} reshape(bf16[192,16384]{1,0:T(8,128)(2,1)} %get-tuple-element.117) | data formatting | bytes 12582912 | tf_op jit(solution)/shard_map/while/body/eval_jaxpr/reshape;while/body/eval_jaxpr/reshape | solution.py:37
  505.8 11.4 %convolution_convert_fusion.2 = bf16[192,32768]{1,0:T(8,128)(2,1)} fusion(bf16[128,32768]{1,0:T(8,128)(2,1)} %get-tuple-element.139, s32[192]{0:T(256)S(1)} %eq.34), kind=kOutput, calls=%fused_computation.1.clone.1 | convolution fusion | flops 1616928768 | bytes 20972288 | tf_op jit(solution)/shard_map/while/body/eval_jaxpr/dot_general | solution.py:14
  537.9 10.4 %reshape.84 = bf16[4,6144,128]{2,1,0:T(8,128)(2,1)} reshape(bf16[192,16384]{1,0:T(8,128)(2,1)} %get-tuple-element.117) | data formatting | bytes 12582912 | tf_op jit(solution)/shard_map/while/body/eval_jaxpr/reshape;while/body/eval_jaxpr/reshape | solution.py:37
  562.0 11.4 %convolution_convert_fusion.2 = bf16[192,32768]{1,0:T(8,128)(2,1)} fusion(bf16[128,32768]{1,0:T(8,128)(2,1)} %get-tuple-element.139, s32[192]{0:T(256)S(1)} %eq.34), kind=kOutput, calls=%fused_computation.1.clone.1 | convolution fusion | flops 1616928768 | bytes 20972288 | tf_op jit(solution)/shard_map/while/body/eval_jaxpr/dot_general | solution.py:14
  594.1 10.4 %reshape.84 = bf16[4,6144,128]{2,1,0:T(8,128)(2,1)} reshape(bf16[192,16384]{1,0:T(8,128)(2,1)} %get-tuple-element.117) | data formatting | bytes 12582912 | tf_op jit(solution)/shard_map/while/body/eval_jaxpr/reshape;while/body/eval_jaxpr/reshape | solution.py:37
  618.3 11.4 %convolution_convert_fusion.2 = bf16[192,32768]{1,0:T(8,128)(2,1)} fusion(bf16[128,32768]{1,0:T(8,128)(2,1)} %get-tuple-element.139, s32[192]{0:T(256)S(1)} %eq.34), kind=kOutput, calls=%fused_computation.1.clone.1 | convolution fusion | flops 1616928768 | bytes 20972288 | tf_op jit(solution)/shard_map/while/body/eval_jaxpr/dot_general | solution.py:14
  650.3 10.4 %reshape.84 = bf16[4,6144,128]{2,1,0:T(8,128)(2,1)} reshape(bf16[192,16384]{1,0:T(8,128)(2,1)} %get-tuple-element.117) | data formatting | bytes 12582912 | tf_op jit(solution)/shard_map/while/body/eval_jaxpr/reshape;while/body/eval_jaxpr/reshape | solution.py:37
  674.3 24.1 %all_to_all.65 = bf16[32,128,128]{2,1,0:T(8,128)(2,1)S(1)} all-to-all(bf16[32,128,128]{2,1,0:T(8,128)(2,1)S(1)} %bitcast.63), channel_id=1, replica_groups=mesh['seq'=32,'head'=4] {'seq'}, dimensions={0} | all-to-all | bytes 2097152 | tf_op jit(solution)/shard_map/all_to_all | solution.py:80
  (110 shorter events, 333.9 us)
Async XLA Ops:
  6.5 127.8 %copy-start = (bf16[128,4096]{1,0:T(8,128)(2,1)S(1)}, bf16[128,4096]{1,0:T(8,128)(2,1)}, u32[]{:S(2)}) copy-start(bf16[128,4096]{1,0:T(8,128)(2,1)} %param.7) | copy-start | bytes 3145732
  6.5 53.3 %all-gather.7.cloned.1.call-start = ((), (), s32[]{:S(2)}) async-start(), calls=%async_computation.5 | async-start | bytes 5242880 | tf_op jit(solution)/shard_map/all_gather | solution.py:63
  7.3 102.8 %all-gather.5.cloned.1.call-start = ((), (), s32[]{:S(2)}) async-start(), calls=%async_computation.4 | async-start | bytes 5242880 | tf_op jit(solution)/shard_map/all_gather | solution.py:62
  67.3 60.1 %all-to-all-start.2 = ((bf16[4,128,4096]{1,0,2:T(4,128)(2,1)}), bf16[4,128,4096]{1,0,2:T(4,128)(2,1)}, u32[]{:S(2)}, u32[]{:S(2)}) async-start(bf16[4,128,4096]{1,0,2:T(4,128)(2,1)} %copy.32), calls=%async_computation.2 | async-start | bytes 8388608 | tf_op jit(solution)/shard_map/all_to_all | solution.py:67
  110.1 23.9 %copy-start.3 = (s32[1,128]{1,0:T(1,128)S(1)}, s32[1,128]{1,0:T(1,128)}, u32[]{:S(2)}) copy-start(s32[1,128]{1,0:T(1,128)} %param.11) | copy-start | bytes 1540
  110.1 24.1 %copy-start.2 = (s32[1,128,48]{1,2,0:T(8,128)S(1)}, s32[1,128,48]{1,2,0:T(8,128)}, u32[]{:S(2)}) copy-start(s32[1,128,48]{1,2,0:T(8,128)} %param.10) | copy-start | bytes 73732
  127.4 59.4 %all-to-all-start.1 = ((bf16[4,128,4096]{1,0,2:T(4,128)(2,1)}), bf16[4,128,4096]{1,0,2:T(4,128)(2,1)}, u32[]{:S(2)}, u32[]{:S(2)}) async-start(bf16[4,128,4096]{1,0,2:T(4,128)(2,1)} %copy.29), calls=%async_computation.1 | async-start | bytes 8388608 | tf_op jit(solution)/shard_map/all_to_all | solution.py:66
  186.8 37.6 %all-to-all-start = ((bf16[128,32,128]{2,0,1:T(8,128)(2,1)}), bf16[128,32,128]{2,0,1:T(8,128)(2,1)S(1)}, u32[]{:S(2)}, u32[]{:S(2)}) async-start(bf16[128,32,128]{2,0,1:T(8,128)(2,1)} %copy_bitcast_fusion.2), calls=%async_computation | async-start | bytes 2097152 | tf_op jit(solution)/shard_map/all_to_all | solution.py:60
  674.3 26.1 %copy-start.1 = (bf16[128,4096]{1,0:T(8,128)(2,1)S(1)}, bf16[128,4096]{1,0:T(8,128)(2,1)}, u32[]{:S(2)}) copy-start(bf16[128,4096]{1,0:T(8,128)(2,1)} %param.7) | copy-start | bytes 3145732
Sparse Core Ops, SparseCore 0:
  9.0 50.7 all-gather.6
  61.5 48.5 all-gather.4
where the time goes:
time: 714 us; the launch traced here: 707 us
  local copies, waits for them, and re-layouts  303 us (42%)
  matrix products  173 us (24%)
  waiting for transfers between devices  139 us (19%)
  other arithmetic  34 us (5%)
  blocking collectives  24.1 us (3%)
  starting transfers between devices  20.5 us (3%)
  between operations  13.5 us (2%)
    dot_general x8, matrix products, select_blocks(): jnp.dot(onehot, kv_flat, preferred_element_type=jnp.float32)  90.9 us
    reshape x8, local copies, waits for them, and re-layouts, one_group(): key_rows = key_sel.reshape(group, listed_most * BLOCK, hdim)  83.5 us
    reshape x8, local copies, waits for them, and re-layouts, one_group(): val_rows = val_sel.reshape(group, listed_most * BLOCK, hdim)  83.3 us
    slice x8, local copies, waits for them, and re-layouts, select_blocks(): key_rows = picked[:, :half].reshape(indices.shape + (BLOCK, hdim))  82.4 us
    all_gather x1, waiting for transfers between devices, local(): lax.all_gather(values[None], 'head', axis=0, tiled=True)  51.8 us
    dot_general x8, matrix products, one_group(): jnp.einsum('qtk,qkh->qth', weight_b, val_rows, preferred_element_type=jnp...  49.6 us
    all_to_all x1, waiting for transfers between devices, local(): lax.all_to_all(k_group, 'seq', split_axis=2, concat_axis=1, tiled=True)  40.1 us
    all_gather x1, waiting for transfers between devices, local(): lax.all_gather(keys[None], 'head', axis=0, tiled=True)  35.5 us
  transfers between devices with their start and end apart: 5, of which 4 were waited for; matrix products, arithmetic and copies ran while one was open for 8% of the time, Pallas kernels for 0%

commit v1 on v0

v1 whole, which is shorter than its diff:
```python
import functools

import jax
import jax.numpy as jnp
from jax import lax
from jax.experimental import pallas as pl
from jax.experimental.pallas import tpu as pltpu
from jax.sharding import PartitionSpec as P

BLOCK = 128
HDIM = 128
LOG2E = 1.4426950408889634


def pack_kernel(q_ref, k_ref, v_ref, qo_ref, ko_ref, vo_ref):
    for h in range(qo_ref.shape[0]):
        cols = slice(h * HDIM, (h + 1) * HDIM)
        qo_ref[h] = q_ref[:, cols]
        ko_ref[h] = k_ref[:, cols]
        vo_ref[h] = v_ref[:, cols].T


def pack(queries, keys, values):
    tok, width = queries.shape
    heads = width // HDIM
    per = 8
    flat = pl.BlockSpec((tok, per * HDIM), lambda i: (0, i))
    blocks = pl.BlockSpec((per, tok, HDIM), lambda i: (i, 0, 0))
    out = jax.ShapeDtypeStruct((heads, tok, HDIM), queries.dtype)
    return pl.pallas_call(
        pack_kernel,
        grid=(heads // per,),
        in_specs=[flat] * 3,
        out_specs=[blocks] * 3,
        out_shape=[out] * 3,
    )(queries, keys, values)


def unpack_kernel(x_ref, o_ref):
    for h in range(x_ref.shape[0]):
        o_ref[:, h * HDIM : (h + 1) * HDIM] = x_ref[h]


def unpack(x):
    heads, tok, hdim = x.shape
    per = 8
    return pl.pallas_call(
        unpack_kernel,
        grid=(heads // per,),
        in_specs=[pl.BlockSpec((per, tok, hdim), lambda i: (i, 0, 0))],
        out_specs=pl.BlockSpec((tok, per * hdim), lambda i: (0, i)),
        out_shape=jax.ShapeDtypeStruct((tok, heads * hdim), x.dtype),
    )(x)


def attention_kernel(group, most, lists, counts, q_ref, k_ref, vt_ref, o_ref):
    factor = LOG2E / HDIM**0.5

    def query_block(b, _):
        q = q_ref[b]
        count = counts[b]

        def chunk(c, carry):
            top, total, acc = carry
            scores, places, active = [], [], []
            for g in range(group):
                j = c * group + g
                place = lists[b * most + jnp.minimum(j, count - 1)]
                places.append(place)
                active.append(j < count)
                scores.append(
                    lax.dot_general(
                        k_ref[place], q, (((1,), (1,)), ((), ())), preferred_element_type=jnp.float32
                    )
                )
            largest = functools.reduce(jnp.maximum, scores)
            new_top = jnp.maximum(top, jnp.max(largest, axis=0, keepdims=True) * factor)
            shrink = jnp.exp2(top - new_top)
            total = total * shrink
            acc = acc * shrink
            for g in range(group):
                base = jnp.where(active[g], new_top, jnp.inf)
                weight = jnp.exp2(scores[g] * factor - base)
                total = total + weight.reshape(BLOCK // 8, 8, BLOCK).sum(axis=0)
                acc = acc + lax.dot_general(
                    vt_ref[places[g]],
                    weight.astype(jnp.bfloat16),
                    (((1,), (0,)), ((), ())),
                    preferred_element_type=jnp.float32,
                )
            return new_top, total, acc

        first = (
            jnp.full((1, BLOCK), -jnp.inf, jnp.float32),
            jnp.zeros((8, BLOCK), jnp.float32),
            jnp.zeros((HDIM, BLOCK), jnp.float32),
        )
        _, total, acc = lax.fori_loop(0, (count + group - 1) // group, chunk, first)
        out = acc / jnp.sum(total, axis=0, keepdims=True)
        o_ref[b] = out.T.astype(jnp.bfloat16)
        return 0

    lax.fori_loop(0, q_ref.shape[0], query_block, 0)


def attention(lists, counts, q, k, vt, group=8):
    whole = lambda a: pl.BlockSpec(a.shape, lambda i, *_: (0, 0, 0))
    return pl.pallas_call(
        functools.partial(attention_kernel, group, lists.shape[1]),
        grid_spec=pltpu.PrefetchScalarGridSpec(
            num_scalar_prefetch=2,
            grid=(1,),
            in_specs=[whole(q), whole(k), whole(vt)],
            out_specs=whole(q),
        ),
        out_shape=jax.ShapeDtypeStruct(q.shape, jnp.bfloat16),
        compiler_params=pltpu.CompilerParams(vmem_limit_bytes=48 << 20),
    )(lists.reshape(-1), counts, q, k, vt)


def local(queries, keys, values, key_blocks, key_count):
    swap = lambda a: lax.all_to_all(a, "seq", split_axis=0, concat_axis=0, tiled=True)
    gather = lambda a: lax.all_gather(a, "head", axis=0, tiled=True)
    q, k, vt = pack(queries, keys, values)
    k_all = gather(swap(k))
    vt_all = gather(swap(vt))
    q_mine = swap(q)
    q_count = q_mine.shape[0]
    first_block = lax.axis_index("head") * q_count
    lists = lax.dynamic_slice_in_dim(key_blocks[0], first_block, q_count, 0)
    counts = lax.dynamic_slice_in_dim(key_count[0], first_block, q_count, 0)
    result = attention(lists, counts, q_mine, k_all, vt_all)
    return unpack(swap(result))


def solution(mesh):
    placed = (
        P(("head", "seq"), None),
        P(("head", "seq"), None),
        P(("head", "seq"), None),
        P("seq", None, None),
        P("seq", None),
    )
    return jax.shard_map(
        local, mesh=mesh, in_specs=placed, out_specs=P(("head", "seq"), None), check_vma=False
    )
```

time: 714 us -> 261 us (0.37)
  the two profiles are of different devices: /device:TPU:0 before, /device:TPU:25 now
where the time goes in v1:
time: 261 us; the launch traced here: 260 us
  blocking collectives  117 us (45%)
  waiting for transfers between devices  68.5 us (26%)
  Pallas kernels  56.2 us (22%)
  between operations  13.4 us (5%)
  starting transfers between devices  3.99 us (2%)
    all_to_all x3, blocking collectives, local(): lax.all_to_all(a, 'seq', split_axis=0, concat_axis=0, tiled=True)  117 us
    all_gather x2, waiting for transfers between devices, local(): gather = lambda a: lax.all_gather(a, 'head', axis=0, tiled=True)  51.9 us
    pallas_call x1, Pallas kernels, attention(): pl.pallas_call(functools.partial(attention_kernel, group, lists.shape[1])...  48.6 us
    all_to_all x1, waiting for transfers between devices, local(): lax.all_to_all(a, 'seq', split_axis=0, concat_axis=0, tiled=True)  16.6 us
  transfers between devices with their start and end apart: 3, of which 3 were waited for; matrix products, arithmetic and copies ran while one was open for 0% of the time, Pallas kernels for 0%

profile of v1, /device:TPU:25, one launch (start us, length us, event | category | flops | bytes accessed | tf_op | source)
XLA Modules:
  0.0 259.5 jit_solution(17407270795705322887)
XLA Ops:
  6.5 0.0 copy-start
  6.5 0.0 all-gather.3.cloned.1.call-start
  6.5 4.2 %shard_map.55 = (bf16[32,128,128]{2,1,0:T(8,128)(2,1)}, bf16[32,128,128]{2,1,0:T(8,128)(2,1)}, bf16[32,128,128]{2,1,0:T(8,128)(2,1)}) custom-call(bf16[128,4096]{1,0:T(8,128)(2,1)} %q_ref.1, bf16[128,4096]{1,0:T(8,128)(2,1)} %k_ref.1, bf16[128,4096]{1,0:T(8,128)(2,1)} %v_ref.1), custom_call_target="tpu_custom_call" | custom-call | tf_op jit(solution)/shard_map/pallas_call | solution.py:30
  10.7 0.0 copy-start.1
  10.7 25.8 %all_to_all.20 = bf16[32,128,128]{2,1,0:T(8,128)(2,1)} all-to-all(bf16[32,128,128]{2,1,0:T(8,128)(2,1)} %get-tuple-element.9), channel_id=1, replica_groups=mesh['seq'=32,'head'=4] {'seq'}, dimensions={0} | all-to-all | bytes 2097152 | tf_op jit(solution)/shard_map/all_to_all | solution.py:122
  36.5 0.0 all-gather.3.cloned.1.call-update
  36.5 0.0 all-gather.5.cloned.1.call-start
  36.6 21.4 %all_to_all.21 = bf16[32,128,128]{2,1,0:T(8,128)(2,1)} all-to-all(bf16[32,128,128]{2,1,0:T(8,128)(2,1)} %get-tuple-element.10), channel_id=1, replica_groups=mesh['seq'=32,'head'=4] {'seq'}, dimensions={0} | all-to-all | bytes 2097152 | tf_op jit(solution)/shard_map/all_to_all | solution.py:122
  58.0 0.0 all-gather.5.cloned.1.call-update
  58.0 3.9 %all-to-all-start = ((bf16[32,128,128]{2,1,0:T(8,128)(2,1)}), bf16[32,128,128]{2,1,0:T(8,128)(2,1)S(1)}, u32[]{:S(2)}, u32[]{:S(2)}) async-start(bf16[32,128,128]{2,1,0:T(8,128)(2,1)} %get-tuple-element.8), calls=%async_computation | async-start | bytes 2097152 | tf_op jit(solution)/shard_map/all_to_all | solution.py:122
  62.0 0.0 copy-done
  62.0 0.1 constant_dynamic-slice_fusion
  62.1 0.1 copy.7
  62.1 0.1 reshape.6.lists
  62.2 0.0 copy-done.1
  62.2 0.1 dynamic-slice_bitcast_fusion.counts
  62.3 16.6 %all-to-all-done.q_ref = bf16[32,128,128]{2,1,0:T(8,128)(2,1)S(1)} async-done(((bf16[32,128,128]{2,1,0:T(8,128)(2,1)}), bf16[32,128,128]{2,1,0:T(8,128)(2,1)S(1)}, u32[]{:S(2)}, u32[]{:S(2)}) %all-to-all-start) | async-done | bytes 1048608 | tf_op jit(solution)/shard_map/all_to_all | solution.py:122
  78.9 1.6 all-gather.3.cloned.1.call-done.k_ref
  80.5 50.3 %all-gather.5.cloned.1.call-done.vt_ref = bf16[128,128,128]{2,1,0:T(8,128)(2,1)} async-done(((bf16[32,128,128]{2,1,0:T(8,128)(2,1)}), bf16[128,128,128]{2,1,0:T(8,128)(2,1)}) %all-gather.5.cloned.1.call-update) | async-done | bytes 4194320 | tf_op jit(solution)/shard_map/all_gather | solution.py:123
  130.8 48.6 %shard_map.56 = bf16[32,128,128]{2,1,0:T(8,128)(2,1)S(1)} custom-call(s32[1536]{0:T(1024)S(1)} %reshape.6.lists, s32[32]{0:T(128)S(1)} %dynamic-slice_bitcast_fusion.counts, bf16[32,128,128]{2,1,0:T(8,128)(2,1)S(1)} %all-to-all-done.q_ref, bf16[128,128,128]{2,1,0:T(8,128)(2,1)} %all-gather.3.cloned.1.call-done.k_ref, ...), custom_call_target="tpu_custom_call" | custom-call | tf_op jit(solution)/shard_map/pallas_call | solution.py:108
  179.4 69.8 %all_to_all.22.x_ref = bf16[32,128,128]{2,1,0:T(8,128)(2,1)} all-to-all(bf16[32,128,128]{2,1,0:T(8,128)(2,1)S(1)} %shard_map.56), channel_id=1, replica_groups=mesh['seq'=32,'head'=4] {'seq'}, dimensions={0} | all-to-all | bytes 2097152 | tf_op jit(solution)/shard_map/all_to_all | solution.py:122
  249.2 3.5 %shard_map.57 = bf16[128,4096]{1,0:T(8,128)(2,1)} custom-call(bf16[32,128,128]{2,1,0:T(8,128)(2,1)} %all_to_all.22.x_ref), custom_call_target="tpu_custom_call" | custom-call | tf_op jit(solution)/shard_map/pallas_call | solution.py:47
Async XLA Ops:
  6.5 55.4 %copy-start = (s32[1,128,48]{1,2,0:T(8,128)S(1)}, s32[1,128,48]{1,2,0:T(8,128)}, u32[]{:S(2)}) copy-start(s32[1,128,48]{1,2,0:T(8,128)} %param.8) | copy-start | bytes 73732
  6.5 74.0 %all-gather.3.cloned.1.call-start = ((), (), s32[]{:S(2)}) async-start(), calls=%async_computation.4 | async-start | bytes 5242880 | tf_op jit(solution)/shard_map/all_gather | solution.py:123
  10.7 51.5 %copy-start.1 = (s32[1,128]{1,0:T(1,128)S(1)}, s32[1,128]{1,0:T(1,128)}, u32[]{:S(2)}) copy-start(s32[1,128]{1,0:T(1,128)} %param.9) | copy-start | bytes 1540
  36.5 94.3 %all-gather.5.cloned.1.call-start = ((), (), s32[]{:S(2)}) async-start(), calls=%async_computation.5 | async-start | bytes 5242880 | tf_op jit(solution)/shard_map/all_gather | solution.py:123
  58.0 20.9 %all-to-all-start = ((bf16[32,128,128]{2,1,0:T(8,128)(2,1)}), bf16[32,128,128]{2,1,0:T(8,128)(2,1)S(1)}, u32[]{:S(2)}, u32[]{:S(2)}) async-start(bf16[32,128,128]{2,1,0:T(8,128)(2,1)} %get-tuple-element.8), calls=%async_computation | async-start | bytes 2097152 | tf_op jit(solution)/shard_map/all_to_all | solution.py:122
Sparse Core Ops, SparseCore 0:
  36.6 43.8 all-gather.2
  82.2 48.5 all-gather.4

commit v2 on v0

v2 whole, which is shorter than its diff:
```python
import functools

import jax
import jax.numpy as jnp
from jax import lax
from jax.experimental import pallas as pl
from jax.experimental.pallas import tpu as pltpu
from jax.sharding import PartitionSpec as P

BLOCK = 128
HDIM = 128
LOG2E = 1.4426950408889634
FACTOR = LOG2E / HDIM**0.5
GROUP = 8
PLACES = 16
VMEM = 48 << 20


def pack_kv_kernel(k_ref, v_ref, o_ref):
    for h in range(o_ref.shape[0] * o_ref.shape[1]):
        cols = slice(h * HDIM, (h + 1) * HDIM)
        o_ref[h % 2, h // 2, 0] = k_ref[:, cols]
        o_ref[h % 2, h // 2, 1] = v_ref[:, cols].T


def pack_q_kernel(q_ref, o_ref):
    for h in range(o_ref.shape[0] * o_ref.shape[1]):
        o_ref[h % 2, h // 2] = q_ref[:, h * HDIM : (h + 1) * HDIM]


def unpack_kernel(x_ref, o_ref):
    for h in range(x_ref.shape[0] * x_ref.shape[1]):
        o_ref[:, h * HDIM : (h + 1) * HDIM] = x_ref[h % 2, h // 2]


STEP = 4
FLAT = pl.BlockSpec((BLOCK, 2 * STEP * HDIM), lambda i: (0, i))
PACKED = pl.BlockSpec((2, STEP, BLOCK, HDIM), lambda i: (0, i, 0, 0))


def pack_kv(keys, values):
    return pl.pallas_call(
        pack_kv_kernel,
        grid=(PLACES // STEP,),
        in_specs=[FLAT, FLAT],
        out_specs=pl.BlockSpec((2, STEP, 2, BLOCK, HDIM), lambda i: (0, i, 0, 0, 0)),
        out_shape=jax.ShapeDtypeStruct((2, PLACES, 2, BLOCK, HDIM), keys.dtype),
    )(keys, values)


def pack_q(queries):
    return pl.pallas_call(
        pack_q_kernel,
        grid=(PLACES // STEP,),
        in_specs=[FLAT],
        out_specs=PACKED,
        out_shape=jax.ShapeDtypeStruct((2, PLACES, BLOCK, HDIM), queries.dtype),
    )(queries)


def unpack(x):
    return pl.pallas_call(
        unpack_kernel,
        grid=(PLACES // STEP,),
        in_specs=[PACKED],
        out_specs=FLAT,
        out_shape=jax.ShapeDtypeStruct((BLOCK, 2 * PLACES * HDIM), x.dtype),
    )(x)


def attention_kernel(
    first, last, chunks, lists, counts, q_hbm, own_hbm, other_hbm, *rest
):
    rest = list(rest)
    if not first:
        acc_in, top_in, total_in = (rest.pop(0) for _ in range(3))
    if last:
        o_ref = rest.pop(0)
        acc_ref, top_ref, total_ref = rest[6:9]
    else:
        acc_ref, top_ref, total_ref = (rest.pop(0) for _ in range(3))
    s0, s1, p0, p1, q_ref, kv_ref = rest[:6]
    sems = rest[-1]
    nq = q_hbm.shape[0]
    half = own_hbm.shape[0]
    most = lists.shape[0] // (nq + 1)

    copies = [
        (q_hbm, q_ref),
        (own_hbm, kv_ref.at[pl.ds(0, half)]),
        (other_hbm, kv_ref.at[pl.ds(half, half)]),
    ]
    if not first:
        copies += [(acc_in, acc_ref), (top_in, top_ref), (total_in, total_ref)]
    copies = [
        pltpu.make_async_copy(src, dst, sems.at[i]) for i, (src, dst) in enumerate(copies)
    ]
    for copy in copies:
        copy.start()
    if first:
        acc_ref[...] = jnp.zeros_like(acc_ref)
        top_ref[...] = jnp.full_like(top_ref, -jnp.inf)
        total_ref[...] = jnp.zeros_like(total_ref)
    for copy in copies:
        copy.wait()

    def where(t):
        code = chunks[t + 1]
        return code // 8, code % 8

    def places(b, c):
        end = jnp.maximum(counts[b] - 1, 0)
        return [lists[b * most + jnp.minimum(c * GROUP + g, end)] for g in range(GROUP)]

    def scores(b, chosen, dst):
        rows = jnp.concatenate([kv_ref[i, 0] for i in chosen], axis=0)
        q = q_ref[jnp.minimum(b, nq - 1)]
        s = lax.dot_general(rows, q, (((1,), (1,)), ((), ())), preferred_element_type=jnp.float32)
        dst[...] = s
        return jnp.max(s.reshape(GROUP * BLOCK // 8, 8, BLOCK), axis=0)

    def weights(b, c, largest, src, dst, top, total):
        count = counts[b]
        top = jnp.where(c == 0, top_ref[b], top)
        total = jnp.where(c == 0, total_ref[b], total)
        new_top = jnp.maximum(top, jnp.max(largest, axis=0, keepdims=True) * FACTOR)
        shrink = jnp.exp2(top - new_top)
        total = total * shrink
        for g in range(GROUP):
            rows = slice(g * BLOCK, (g + 1) * BLOCK)
            base = jnp.where(c * GROUP + g < count, new_top, jnp.inf)
            weight = jnp.exp2(src[rows, :] * FACTOR - base)
            total = total + jnp.sum(weight.reshape(BLOCK // 8, 8, BLOCK), axis=0)
            dst[rows, :] = weight.astype(jnp.bfloat16)
        top_ref[b] = new_top
        total_ref[b] = total
        return new_top, total, shrink

    def weighted(b, chosen, shrink, src):
        cols = jnp.concatenate([kv_ref[i, 1] for i in chosen], axis=1)
        acc_ref[b] = acc_ref[b] * shrink + jnp.dot(
            cols, src[...], preferred_element_type=jnp.float32
        )

    steps = chunks[0]
    score_bufs, weight_bufs = (s0, s1), (p0, p1)
    b0, c0 = where(0)
    places0 = places(b0, c0)
    largest0 = scores(b0, places0, s0)
    b1, c1 = where(1)
    places1 = places(b1, c1)
    largest1 = scores(b1, places1, s1)
    top, total, shrink0 = weights(
        b0,
        c0,
        largest0,
        s0,
        p0,
        jnp.full((1, BLOCK), -jnp.inf, jnp.float32),
        jnp.zeros((8, BLOCK), jnp.float32),
    )

    def body(i, carry):
        b0, shrink0, b1, c1, largest1, top, total = carry[:7]
        places0, places1 = list(carry[7 : 7 + GROUP]), list(carry[7 + GROUP :])
        for u in range(2):
            b2, c2 = where(2 * i + u + 2)
            places2 = places(b2, c2)
            largest2 = scores(b2, places2, score_bufs[u])
            top, total, shrink1 = weights(
                b1, c1, largest1, score_bufs[1 - u], weight_bufs[1 - u], top, total
            )
            weighted(b0, places0, shrink0, weight_bufs[u])
            b0, shrink0, places0 = b1, shrink1, places1
            b1, c1, largest1, places1 = b2, c2, largest2, places2
        return (b0, shrink0, b1, c1, largest1, top, total, *places0, *places1)

    lax.fori_loop(
        0,
        (steps + 1) // 2,
        body,
        (b0, shrink0, b1, c1, largest1, top, total, *places0, *places1),
    )

    if last:

        def finish(b, _):
            out = acc_ref[b] / jnp.sum(total_ref[b], axis=0, keepdims=True)
            o_ref[b] = out.T.astype(jnp.bfloat16)
            return 0

        lax.fori_loop(0, nq, finish, 0, unroll=4)


def attention(tables, q, own, other, state, last):
    chunks, lists, counts = tables
    nq = q.shape[0]
    first = state is None
    hbm = pl.BlockSpec(memory_space=pl.ANY)
    shapes = [(nq + 1, HDIM, BLOCK), (nq + 1, 1, BLOCK), (nq + 1, 8, BLOCK)]
    whole = lambda s: pl.BlockSpec(s, lambda i, *_: (0, 0, 0))
    scratch = [
        pltpu.VMEM((GROUP * BLOCK, BLOCK), jnp.float32),
        pltpu.VMEM((GROUP * BLOCK, BLOCK), jnp.float32),
        pltpu.VMEM((GROUP * BLOCK, BLOCK), jnp.bfloat16),
        pltpu.VMEM((GROUP * BLOCK, BLOCK), jnp.bfloat16),
        pltpu.VMEM(q.shape, q.dtype),
        pltpu.VMEM((2 * own.shape[0],) + own.shape[1:], own.dtype),
    ]
    if last:
        scratch += [pltpu.VMEM(s, jnp.float32) for s in shapes]
        out_shape = jax.ShapeDtypeStruct(q.shape, jnp.bfloat16)
        out_specs = whole(q.shape)
    else:
        out_shape = [jax.ShapeDtypeStruct(s, jnp.float32) for s in shapes]
        out_specs = [whole(s) for s in shapes]
    scratch += [pltpu.SemaphoreType.DMA((6,))]
    args = [q, own, other] + ([] if first else list(state))
    return pl.pallas_call(
        functools.partial(attention_kernel, first, last),
        grid_spec=pltpu.PrefetchScalarGridSpec(
            num_scalar_prefetch=3,
            grid=(1,),
            in_specs=[hbm] * len(args),
            out_specs=out_specs,
            scratch_shapes=scratch,
        ),
        out_shape=out_shape,
        compiler_params=pltpu.CompilerParams(vmem_limit_bytes=VMEM),
        cost_estimate=pl.CostEstimate(
            flops=20_000_000_000, bytes_accessed=16 << 20, transcendentals=0
        ),
    )(chunks, lists, counts, *args)


def make_tables(match, place):
    nq, most = match.shape
    at = jnp.arange(most, dtype=jnp.int32)
    before = (at[:, None] < at[None, :])[None] & match[:, :, None]
    pos = jnp.sum(before.astype(jnp.int32), axis=1)
    hit = (pos[:, :, None] == at[None, None, :]) & match[:, :, None]
    lists = jnp.sum(jnp.where(hit, place[:, :, None], 0), axis=1)
    counts = jnp.sum(match.astype(jnp.int32), axis=1)
    steps = (counts + GROUP - 1) // GROUP
    row = jnp.arange(nq, dtype=jnp.int32)
    ends = jnp.sum(jnp.where(row[:, None] <= row[None, :], steps[:, None], 0), axis=0)
    t = jnp.arange(nq * ((most + GROUP - 1) // GROUP) + 3, dtype=jnp.int32)
    b = jnp.sum((t[:, None] >= ends[None, :]).astype(jnp.int32), axis=1)
    start = jnp.sum(jnp.where(row[None, :] < b[:, None], steps[None, :], 0), axis=1)
    c = jnp.where(b < nq, t - start, 0)
    chunks = jnp.concatenate([ends[-1:], b * 8 + c])
    lists = jnp.pad(lists, ((0, 1), (0, 0))).reshape(-1)
    return chunks, lists, jnp.pad(counts, (0, 1))


def local(queries, keys, values, key_blocks, key_count):
    seq_count, head_count = lax.axis_size("seq"), lax.axis_size("head")
    y = lax.axis_index("head")
    core = lax.axis_index("seq") % 2

    index = lambda place, c, yy: (place * 2 + c) * head_count + yy
    groups = [
        [index(place, c, yy) for yy in ys for place in range(PLACES)]
        for c in range(2)
        for ys in ((0, 3), (1, 2))
    ]
    swap = lambda a: lax.all_to_all(
        a, ("seq", "head"), 0, 0, axis_index_groups=groups, tiled=True
    )
    to_core = lambda a: lax.ppermute(a, "seq", [(i, i ^ 1) for i in range(seq_count)])
    to_pair = lambda a: lax.ppermute(a, "head", [(i, i ^ 1) for i in range(head_count)])

    odd = (y >= 2).astype(jnp.int32)
    mine = jnp.concatenate([key_blocks[0], key_count[0][:, None]], axis=1)
    mine = jnp.where(core == odd, mine, to_core(mine))
    outer = (y == 0) | (y == 3)
    mine = mine.reshape(head_count, PLACES, 2, -1)
    mine = lax.dynamic_index_in_dim(mine, core, 2, keepdims=False)
    mine = jnp.where(outer, mine[0::3], mine[1:3]).reshape(2 * PLACES, -1)
    blocks, count = mine[:, :-1], mine[:, -1]
    active = jnp.arange(blocks.shape[1], dtype=jnp.int32)[None, :] < count[:, None]
    block_y = blocks // 32
    block_core = (blocks % 2) ^ core
    block_place = (blocks // 2) % PLACES
    near = ((block_y == 0) | (block_y == 3)) == outer
    second = block_y // 2
    near_tables = make_tables(
        active & near, (block_core * 2 + second) * PLACES + block_place
    )
    far_place = block_core * PLACES + block_place
    far_tables = [make_tables(active & ~near & (second == i), far_place) for i in range(2)]

    kv = swap(pack_kv(keys, values).reshape(2 * PLACES, 2, BLOCK, HDIM))
    kv_far = [to_pair(kv[i * PLACES : (i + 1) * PLACES]) for i in range(2)]
    q = swap(pack_q(queries).reshape(2 * PLACES, BLOCK, HDIM))
    state = attention(near_tables, q, kv, to_core(kv), None, False)
    state, far = lax.optimization_barrier((state, kv_far[0]))
    state = attention(far_tables[0], q, far, to_core(far), state, False)
    state, far = lax.optimization_barrier((state, kv_far[1]))
    out = attention(far_tables[1], q, far, to_core(far), state, True)
    return unpack(swap(out).reshape(2, PLACES, BLOCK, HDIM))


def solution(mesh):
    placed = (
        P(("head", "seq"), None),
        P(("head", "seq"), None),
        P(("head", "seq"), None),
        P("seq", None, None),
        P("seq", None),
    )
    return jax.shard_map(
        local, mesh=mesh, in_specs=placed, out_specs=P(("head", "seq"), None), check_vma=False
    )
```

time: 714 us -> 162 us (0.23)
  local copies, waits for them, and re-layouts: 303 us -> 5.22 us
  matrix products: 173 us -> 0 us
  waiting for transfers between devices: 139 us -> 50.4 us
  Pallas kernels: 0 us -> 53.2 us
  other arithmetic: 34 us -> 6.86 us
  between operations: 13.5 us -> 0.27 us
    dot_general x24 -> x0, matrix products: 173 us -> none  [the longest x8 90.9 us: select_blocks(): jnp.dot(onehot, kv_flat, preferred_element_type=jnp.float32)]
    reshape x17 -> x3, local copies, waits for them, and re-layouts: 167 us -> 0.22 us  [make_tables(): lists = jnp.pad(lists, ((0, 1), (0, 0))).reshape(-1)]
    all_gather x2 -> x0, waiting for transfers between devices: 87.3 us -> none  [the longest x1 51.8 us: local(): lax.all_gather(values[None], 'head', axis=0, tiled=True)]
    slice x8 -> x6, local copies, waits for them, and re-layouts: 82.4 us -> 3.48 us  [the longest x3 1.83 us: make_tables(): chunks = jnp.concatenate([ends[-1:], b * 8 + c])]
    pallas_call x0 -> x6, Pallas kernels: none -> 53.2 us  [the longest x3 42.3 us: attention(): pl.pallas_call(functools.partial(attention_kernel, first, last), grid_spe...]
    all_to_all x7 -> x0, local copies, waits for them, and re-layouts: 25.3 us -> none  [the longest x2 11.1 us: local(): lax.all_to_all(k_group, 'seq', split_axis=2, concat_axis=1, tiled=True)]
    reduce_sum x8 -> x14, other arithmetic: 25.8 us -> 4.52 us  [the longest x2 2.36 us: make_tables(): lists = jnp.sum(jnp.where(hit, place[:, :, None], 0), axis=1)]
    all_gather x2 -> x0, local copies, waits for them, and re-layouts: 15 us -> none  [the longest x1 7.55 us: local(): lax.all_gather(keys[None], 'head', axis=0, tiled=True)]
  transfers between devices with their start and end apart: 5 -> 8, of which waited for: 4 -> 4; matrix products, arithmetic and copies ran while one was open for 8% -> 7% of each run, Pallas kernels for 0% -> 21%
where the time goes in v2:
time: 162 us
  Pallas kernels  53.2 us (33%)
  waiting for transfers between devices  50.4 us (31%)
  blocking collectives  26.6 us (16%)
  starting transfers between devices  19 us (12%)
  other arithmetic  6.86 us (4%)
  local copies, waits for them, and re-layouts  5.22 us (3%)
    pallas_call x3, Pallas kernels, attention(): pl.pallas_call(functools.partial(attention_kernel, first, last), grid_spe...  42.3 us
    all_to_all x2, waiting for transfers between devices, local(): lax.all_to_all(a, ('seq', 'head'), 0, 0, axis_index_groups=groups, tiled=...  36.5 us
    all_to_all x1, blocking collectives, local(): lax.all_to_all(a, ('seq', 'head'), 0, 0, axis_index_groups=groups, tiled=...  26.6 us
    all_to_all x2, starting transfers between devices, local(): lax.all_to_all(a, ('seq', 'head'), 0, 0, axis_index_groups=groups, tiled=...  17.2 us
    ppermute x2, waiting for transfers between devices, local(): lax.ppermute(a, 'head', [(i, i ^ 1) for i in range(head_count)])  12.7 us
    pallas_call x1, Pallas kernels, pack_kv(): pl.pallas_call(pack_kv_kernel, grid=(PLACES // STEP,), in_specs=[FLAT, FL...  4.04 us
    pallas_call x1, Pallas kernels, unpack(): pl.pallas_call(unpack_kernel, grid=(PLACES // STEP,), in_specs=[PACKED],...  3.46 us
    pallas_call x1, Pallas kernels, pack_q(): pl.pallas_call(pack_q_kernel, grid=(PLACES // STEP,), in_specs=[FLAT], ou...  3.42 us
  transfers between devices with their start and end apart: 8, of which 4 were waited for; matrix products, arithmetic and copies ran while one was open for 7% of the time, Pallas kernels for 21%

profile of v2, /device:TPU:0, one launch (start us, length us, event | category | flops | bytes accessed | tf_op | source)
XLA Modules:
  0.0 161.6 jit_solution(5599984004510077202)
XLA Ops:
  0.0 4.0 %shard_map.56 = bf16[2,16,2,128,128]{4,3,2,1,0:T(8,128)(2,1)} custom-call(bf16[128,4096]{1,0:T(8,128)(2,1)} %k_ref.1, bf16[128,4096]{1,0:T(8,128)(2,1)} %v_ref.1), custom_call_target="tpu_custom_call" | custom-call | tf_op jit(solution)/shard_map/pallas_call | solution.py:42
  4.0 10.8 %all-to-all-start.1 = ((bf16[32,2,128,128]{3,2,1,0:T(8,128)(2,1)}), bf16[32,2,128,128]{3,2,1,0:T(8,128)(2,1)S(1)}, u32[]{:S(2)}, u32[]{:S(2)}) async-start(bf16[32,2,128,128]{3,2,1,0:T(8,128)(2,1)} %bitcast.9), calls=%async_computation.1 | async-start | bytes 4194304 | tf_op jit(solution)/shard_map/all_to_all | solution.py:267
  15.1 3.4 %shard_map.55 = bf16[2,16,128,128]{3,2,1,0:T(8,128)(2,1)} custom-call(bf16[128,4096]{1,0:T(8,128)(2,1)} %q_ref.1), custom_call_target="tpu_custom_call" | custom-call | tf_op jit(solution)/shard_map/pallas_call | solution.py:52
  18.7 25.6 %all-to-all-done.1.own_hbm = bf16[32,2,128,128]{3,2,1,0:T(8,128)(2,1)S(1)} async-done(((bf16[32,2,128,128]{3,2,1,0:T(8,128)(2,1)}), bf16[32,2,128,128]{3,2,1,0:T(8,128)(2,1)S(1)}, u32[]{:S(2)}, u32[]{:S(2)}) %all-to-all-start.1) | async-done | bytes 2097184 | tf_op jit(solution)/shard_map/all_to_all | solution.py:267
  44.3 6.4 %all-to-all-start = ((bf16[32,128,128]{2,1,0:T(8,128)(2,1)}), bf16[32,128,128]{2,1,0:T(8,128)(2,1)S(1)}, u32[]{:S(2)}, u32[]{:S(2)}) async-start(bf16[32,128,128]{2,1,0:T(8,128)(2,1)} %bitcast.10), calls=%async_computation | async-start | bytes 2097152 | tf_op jit(solution)/shard_map/all_to_all | solution.py:267
  51.3 1.0 convert_reduce_fusion
  52.4 0.7 slice.37
  53.1 0.9 select_reduce_fusion
  54.3 0.8 pad_add_fusion.3.chunks
  55.0 1.4 fusion.17
  56.5 10.9 %all-to-all-done.q_hbm = bf16[32,128,128]{2,1,0:T(8,128)(2,1)S(1)} async-done(((bf16[32,128,128]{2,1,0:T(8,128)(2,1)}), bf16[32,128,128]{2,1,0:T(8,128)(2,1)S(1)}, u32[]{:S(2)}, u32[]{:S(2)}) %all-to-all-start) | async-done | bytes 1048608 | tf_op jit(solution)/shard_map/all_to_all | solution.py:267
  67.4 19.2 %shard_map.57 = (f32[33,128,128]{2,1,0:T(8,128)}, f32[33,1,128]{2,1,0:T(1,128)S(1)}, f32[33,8,128]{2,1,0:T(8,128)S(1)}) custom-call(s32[196]{0:T(256)S(1)} %pad_add_fusion.3.chunks, s32[1584]{0:T(1024)S(1)} %reshape.164.lists, s32[33]{0:T(128)S(1)} %pad.25.counts, bf16[32,128,128]{2,1,0:T(8,128)(2,1)S(1)} %all-to-all-done.q_hbm, ...), custom_call_target="tpu_custom_call" | custom-call | flops 20000000000 | bytes 16777216 | tf_op jit(solution)/shard_map/pallas_call | solution.py:219
  86.6 1.6 %collective-permute-start.3 = (bf16[16,2,128,128]{3,2,1,0:T(8,128)(2,1)}, bf16[16,2,128,128]{3,2,1,0:T(8,128)(2,1)}, u32[]{:S(2)}, u32[]{:S(2)}) collective-permute-start(bf16[16,2,128,128]{3,2,1,0:T(8,128)(2,1)} %collective-permute-done.2.own_hbm), channel_id=1, source_target_pairs={{0,4},{4,0},{8,12},{12,8},{16,20},{20,16},{24,28},{28,24},{32,36},... | collective-permute-start | bytes 3145736 | tf_op jit(solution)/shard_map/ppermute | solution.py:270
  88.9 1.5 select_reduce_fusion.1
  90.7 0.7 pad_add_fusion.2.chunks
  91.5 11.2 %shard_map.58 = (f32[33,128,128]{2,1,0:T(8,128)S(1)}, f32[33,1,128]{2,1,0:T(1,128)S(1)}, f32[33,8,128]{2,1,0:T(8,128)S(1)}) custom-call(s32[196]{0:T(256)S(1)} %pad_add_fusion.2.chunks, s32[1584]{0:T(1024)S(1)} %reshape.163.lists, s32[33]{0:T(128)S(1)} %pad.23.counts, bf16[32,128,128]{2,1,0:T(8,128)(2,1)S(1)} %all-to-all-done.q_hbm, ...), custom_call_target="tpu_custom_call" | custom-call | flops 20000000000 | bytes 16777216 | tf_op jit(solution)/shard_map/pallas_call | solution.py:219
  102.7 1.3 copy-done
  104.0 12.7 %collective-permute-done.4.own_hbm = bf16[16,2,128,128]{3,2,1,0:T(8,128)(2,1)S(1)} collective-permute-done((bf16[16,2,128,128]{3,2,1,0:T(8,128)(2,1)}, bf16[16,2,128,128]{3,2,1,0:T(8,128)(2,1)S(1)}, u32[]{:S(2)}, u32[]{:S(2)}) %collective-permute-start.4) | collective-permute-done | bytes 1048608 | tf_op jit(solution)/shard_map/ppermute | solution.py:271
  116.9 0.6 slice.35
  117.7 0.7 pad_add_fusion.1.chunks
  118.5 1.1 collective-permute-done.5.other_hbm
  119.6 11.9 %shard_map.59 = bf16[32,128,128]{2,1,0:T(8,128)(2,1)S(1)} custom-call(s32[196]{0:T(256)S(1)} %pad_add_fusion.1.chunks, s32[1584]{0:T(1024)S(1)} %reshape.161.lists, s32[33]{0:T(128)S(1)} %pad.21.counts, bf16[32,128,128]{2,1,0:T(8,128)(2,1)S(1)} %all-to-all-done.q_hbm, bf16[16,2,128,128]{3,2,1,0:T(8,128)(2,1)S(1)} %collective-permute-done.4.own_hbm, ...), custom_call_target="tpu_custom_call" | custom-call | flops 20000000000 | bytes 16777216 | tf_op jit(solution)/shard_map/pallas_call | solution.py:219
  131.5 26.6 %all_to_all.15 = bf16[32,128,128]{2,1,0:T(8,128)(2,1)} all-to-all(bf16[32,128,128]{2,1,0:T(8,128)(2,1)S(1)} %shard_map.59), channel_id=1, replica_groups={{0,8,16,24,32,40,48,56,64,72,80,88,96,104,112,120,3,11,19,27,35,43,51,5..., dimensions={0} | all-to-all | bytes 2097152 | tf_op jit(solution)/shard_map/all_to_all | solution.py:267
  158.1 3.5 %shard_map.60 = bf16[128,4096]{1,0:T(8,128)(2,1)} custom-call(bf16[2,16,128,128]{3,2,1,0:T(8,128)(2,1)} %bitcast.11), custom_call_target="tpu_custom_call" | custom-call | tf_op jit(solution)/shard_map/pallas_call | solution.py:62
  (49 shorter events, 2.7 us)
Async XLA Ops:
  4.0 10.8 %copy-start.1 = (s32[1,128,48]{1,2,0:T(8,128)S(1)}, s32[1,128,48]{1,2,0:T(8,128)}, u32[]{:S(2)}) copy-start(s32[1,128,48]{1,2,0:T(8,128)} %param.8) | copy-start | bytes 73732
  4.0 10.8 %copy-start.2 = (s32[1,128]{1,0:T(1,128)S(1)}, s32[1,128]{1,0:T(1,128)}, u32[]{:S(2)}) copy-start(s32[1,128]{1,0:T(1,128)} %param.9) | copy-start | bytes 1540
  4.0 40.2 %all-to-all-start.1 = ((bf16[32,2,128,128]{3,2,1,0:T(8,128)(2,1)}), bf16[32,2,128,128]{3,2,1,0:T(8,128)(2,1)S(1)}, u32[]{:S(2)}, u32[]{:S(2)}) async-start(bf16[32,2,128,128]{3,2,1,0:T(8,128)(2,1)} %bitcast.9), calls=%async_computation.1 | async-start | bytes 4194304 | tf_op jit(solution)/shard_map/all_to_all | solution.py:267
  15.0 3.6 %collective-permute-start = (s32[128,49]{1,0:T(8,128)S(1)}, s32[128,49]{1,0:T(8,128)S(1)}, u32[]{:S(2)}, u32[]{:S(2)}) collective-permute-start(s32[128,49]{1,0:T(8,128)S(1)} %copy.18), channel_id=1, source_target_pairs={{0,4},{4,0},{8,12},{12,8},{16,20},{20,16},{24,28},{28,24},{32,36},... | collective-permute-start | bytes 75272 | tf_op jit(solution)/shard_map/ppermute | solution.py:270
  44.3 23.1 %all-to-all-start = ((bf16[32,128,128]{2,1,0:T(8,128)(2,1)}), bf16[32,128,128]{2,1,0:T(8,128)(2,1)S(1)}, u32[]{:S(2)}, u32[]{:S(2)}) async-start(bf16[32,128,128]{2,1,0:T(8,128)(2,1)} %bitcast.10), calls=%async_computation | async-start | bytes 2097152 | tf_op jit(solution)/shard_map/all_to_all | solution.py:267
  50.6 16.8 %collective-permute-start.1 = (bf16[32,2,128,128]{3,2,1,0:T(8,128)(2,1)S(1)}, bf16[32,2,128,128]{3,2,1,0:T(8,128)(2,1)}, u32[]{:S(2)}, u32[]{:S(2)}) collective-permute-start(bf16[32,2,128,128]{3,2,1,0:T(8,128)(2,1)S(1)} %all-to-all-done.1.own_hbm), channel_id=1, source_target_pairs={{0,4},{4,0},{8,12},{12,8},{16,20},{20,16},{24,28},{28,24},{32,36},... | collective-permute-start | bytes 6291464 | tf_op jit(solution)/shard_map/ppermute | solution.py:270
  56.5 30.1 %collective-permute-start.2 = (bf16[16,2,128,128]{3,2,1,0:T(8,128)(2,1)}, bf16[16,2,128,128]{3,2,1,0:T(8,128)(2,1)}, u32[]{:S(2)}, u32[]{:S(2)}) collective-permute-start(bf16[16,2,128,128]{3,2,1,0:T(8,128)(2,1)} %get-tuple-element.50), channel_id=1, source_target_pairs={{0,1},{1,0},{2,3},{3,2},{4,5},{5,4},{6,7},{7,6},{8,9},{9,8},{10,11... | collective-permute-start | bytes 3145736 | tf_op jit(solution)/shard_map/ppermute | solution.py:271
  86.6 4.9 %collective-permute-start.3 = (bf16[16,2,128,128]{3,2,1,0:T(8,128)(2,1)}, bf16[16,2,128,128]{3,2,1,0:T(8,128)(2,1)}, u32[]{:S(2)}, u32[]{:S(2)}) collective-permute-start(bf16[16,2,128,128]{3,2,1,0:T(8,128)(2,1)} %collective-permute-done.2.own_hbm), channel_id=1, source_target_pairs={{0,4},{4,0},{8,12},{12,8},{16,20},{20,16},{24,28},{28,24},{32,36},... | collective-permute-start | bytes 3145736 | tf_op jit(solution)/shard_map/ppermute | solution.py:270
  91.5 25.3 %collective-permute-start.4 = (bf16[16,2,128,128]{3,2,1,0:T(8,128)(2,1)}, bf16[16,2,128,128]{3,2,1,0:T(8,128)(2,1)S(1)}, u32[]{:S(2)}, u32[]{:S(2)}) collective-permute-start(bf16[16,2,128,128]{3,2,1,0:T(8,128)(2,1)} %get-tuple-element.49), channel_id=1, source_target_pairs={{0,1},{1,0},{2,3},{3,2},{4,5},{5,4},{6,7},{7,6},{8,9},{9,8},{10,11... | collective-permute-start | bytes 3145736 | tf_op jit(solution)/shard_map/ppermute | solution.py:271
  102.7 1.4 copy-start
  116.8 2.8 %collective-permute-start.5 = (bf16[16,2,128,128]{3,2,1,0:T(8,128)(2,1)S(1)}, bf16[16,2,128,128]{3,2,1,0:T(8,128)(2,1)}, u32[]{:S(2)}, u32[]{:S(2)}) collective-permute-start(bf16[16,2,128,128]{3,2,1,0:T(8,128)(2,1)S(1)} %collective-permute-done.4.own_hbm), channel_id=1, source_target_pairs={{0,4},{4,0},{8,12},{12,8},{16,20},{20,16},{24,28},{28,24},{32,36},... | collective-permute-start | bytes 3145736 | tf_op jit(solution)/shard_map/ppermute | solution.py:270

commit v3 on v2

--- a/solution.py
+++ b/solution.py
@@ -34,6 +34,7 @@
 
 
 STEP = 4
+CUT = 12
 FLAT = pl.BlockSpec((BLOCK, 2 * STEP * HDIM), lambda i: (0, i))
 PACKED = pl.BlockSpec((2, STEP, BLOCK, HDIM), lambda i: (0, i, 0, 0))
 
@@ -228,7 +229,7 @@
         out_shape=out_shape,
         compiler_params=pltpu.CompilerParams(vmem_limit_bytes=VMEM),
         cost_estimate=pl.CostEstimate(
-            flops=20_000_000_000, bytes_accessed=16 << 20, transcendentals=0
+            flops=1_000_000, bytes_accessed=1, transcendentals=0
         ),
     )(chunks, lists, counts, *args)
 
@@ -283,16 +284,22 @@
     block_core = (blocks % 2) ^ core
     block_place = (blocks // 2) % PLACES
     near = ((block_y == 0) | (block_y == 3)) == outer
-    second = block_y // 2
-    near_tables = make_tables(
-        active & near, (block_core * 2 + second) * PLACES + block_place
-    )
-    far_place = block_core * PLACES + block_place
-    far_tables = [make_tables(active & ~near & (second == i), far_place) for i in range(2)]
+    block_at = (block_y // 2) * PLACES + block_place
+    size = 2 * PLACES
+    near_tables = make_tables(active & near, block_core * size + block_at)
+    far_tables = [
+        make_tables(active & ~near & (block_at < CUT), block_core * CUT + block_at),
+        make_tables(
+            active & ~near & (block_at >= CUT), block_core * (size - CUT) + block_at - CUT
+        ),
+    ]
 
     kv = swap(pack_kv(keys, values).reshape(2 * PLACES, 2, BLOCK, HDIM))
-    kv_far = [to_pair(kv[i * PLACES : (i + 1) * PLACES]) for i in range(2)]
-    q = swap(pack_q(queries).reshape(2 * PLACES, BLOCK, HDIM))
+    kv_far = [to_pair(kv[:CUT]), to_pair(kv[CUT:])]
+    q, near_tables, far_tables = lax.optimization_barrier(
+        (pack_q(queries), near_tables, far_tables)
+    )
+    q = swap(q.reshape(2 * PLACES, BLOCK, HDIM))
     state = attention(near_tables, q, kv, to_core(kv), None, False)
     state, far = lax.optimization_barrier((state, kv_far[0]))
     state = attention(far_tables[0], q, far, to_core(far), state, False)

time: 162 us -> 154 us (0.951)
  Pallas kernels: 53.2 us -> 41.3 us
  blocking collectives: 26.6 us -> 33.9 us
  waiting for transfers between devices: 50.4 us -> 46.2 us
    pallas_call x3, Pallas kernels: 42.3 us -> 30.4 us  [attention(): pl.pallas_call(functools.partial(attention_kernel, first, last), grid_spe...]
    all_to_all x1, blocking collectives: 26.6 us -> 33.9 us  [local(): lax.all_to_all(a, ('seq', 'head'), 0, 0, axis_index_groups=groups, tiled=...]
    ppermute x2, waiting for transfers between devices: 12.7 us -> 5.96 us  [local(): lax.ppermute(a, 'head', [(i, i ^ 1) for i in range(head_count)])]
    ppermute x4, waiting for transfers between devices: 1.1 us -> 5.73 us  [local(): lax.ppermute(a, 'seq', [(i, i ^ 1) for i in range(seq_count)])]
    ppermute x2, starting transfers between devices: 0.03 us -> 2.03 us  [local(): lax.ppermute(a, 'head', [(i, i ^ 1) for i in range(head_count)])]
    all_to_all x2, waiting for transfers between devices: 36.5 us -> 34.5 us  [local(): lax.all_to_all(a, ('seq', 'head'), 0, 0, axis_index_groups=groups, tiled=...]
    ppermute x4, starting transfers between devices: 1.81 us -> 0.17 us  [local(): lax.ppermute(a, 'seq', [(i, i ^ 1) for i in range(seq_count)])]
  transfers between devices with their start and end apart: 8 -> 8, of which waited for: 4 -> 5; matrix products, arithmetic and copies ran while one was open for 7% -> 7% of each run, Pallas kernels for 21% -> 18%
where the time goes in v3:
time: 154 us
  waiting for transfers between devices  46.2 us (30%)
  Pallas kernels  41.3 us (27%)
  blocking collectives  33.9 us (22%)
  starting transfers between devices  19 us (12%)
  other arithmetic  7.69 us (5%)
  local copies, waits for them, and re-layouts  5.9 us (4%)
    all_to_all x2, waiting for transfers between devices, local(): lax.all_to_all(a, ('seq', 'head'), 0, 0, axis_index_groups=groups, tiled=...  34.5 us
    all_to_all x1, blocking collectives, local(): lax.all_to_all(a, ('seq', 'head'), 0, 0, axis_index_groups=groups, tiled=...  33.9 us
    pallas_call x3, Pallas kernels, attention(): pl.pallas_call(functools.partial(attention_kernel, first, last), grid_spe...  30.4 us
    all_to_all x2, starting transfers between devices, local(): lax.all_to_all(a, ('seq', 'head'), 0, 0, axis_index_groups=groups, tiled=...  16.8 us
    ppermute x2, waiting for transfers between devices, local(): lax.ppermute(a, 'head', [(i, i ^ 1) for i in range(head_count)])  5.96 us
    ppermute x4, waiting for transfers between devices, local(): lax.ppermute(a, 'seq', [(i, i ^ 1) for i in range(seq_count)])  5.73 us
    pallas_call x1, Pallas kernels, pack_kv(): pl.pallas_call(pack_kv_kernel, grid=(PLACES // STEP,), in_specs=[FLAT, FL...  4.05 us
    pallas_call x1, Pallas kernels, unpack(): pl.pallas_call(unpack_kernel, grid=(PLACES // STEP,), in_specs=[PACKED],...  3.46 us
  transfers between devices with their start and end apart: 8, of which 5 were waited for; matrix products, arithmetic and copies ran while one was open for 7% of the time, Pallas kernels for 18%

profile of v3, /device:TPU:0, one launch (start us, length us, event | category | flops | bytes accessed | tf_op | source)
XLA Modules:
  0.0 154.3 jit_solution(54241824892693513)
XLA Ops:
  0.0 0.8 pad_add_fusion
  1.0 4.1 %shard_map.56 = bf16[2,16,2,128,128]{4,3,2,1,0:T(8,128)(2,1)} custom-call(bf16[128,4096]{1,0:T(8,128)(2,1)} %k_ref.1, bf16[128,4096]{1,0:T(8,128)(2,1)} %v_ref.1), custom_call_target="tpu_custom_call" | custom-call | tf_op jit(solution)/shard_map/pallas_call | solution.py:43
  5.0 10.7 %all-to-all-start.1 = ((bf16[32,2,128,128]{3,2,1,0:T(8,128)(2,1)}), bf16[32,2,128,128]{3,2,1,0:T(8,128)(2,1)S(1)}, u32[]{:S(2)}, u32[]{:S(2)}) async-start(bf16[32,2,128,128]{3,2,1,0:T(8,128)(2,1)} %bitcast.9), calls=%async_computation.1 | async-start | bytes 4194304 | tf_op jit(solution)/shard_map/all_to_all | solution.py:268
  15.7 3.4 %shard_map.55 = bf16[2,16,128,128]{3,2,1,0:T(8,128)(2,1)} custom-call(bf16[128,4096]{1,0:T(8,128)(2,1)} %q_ref.1), custom_call_target="tpu_custom_call" | custom-call | tf_op jit(solution)/shard_map/pallas_call | solution.py:53
  20.6 1.0 convert_reduce_fusion
  21.6 0.9 select_reduce_fusion.2
  23.3 1.7 %select_reduce_fusion = (s32[32,48]{1,0:T(8,128)S(1)}, s32[32,48]{1,0:T(8,128)S(1)}) fusion(s32[32,48]{1,0:T(8,128)S(1)} %get-tuple-element.56, s32[32,48]{1,0:T(8,128)S(1)} %get-tuple-element.53, pred[32,48]{1,0:T(8,128)(4,1)S(1)} %get-tuple-element.70, s32[32,48]{1,0:T(8,128)S(1)} %get-tuple-element.67, pred[32,48]{1,0:T(8,128)(4,1)S(1)} %get-tuple-element.64, ...), kind=kLoop, calls=%fused_computation | loop fusion | flops 586752 | bytes 39936 | tf_op jit(solution)/shard_map/reduce_sum | solution.py:243
  26.2 20.5 %all-to-all-done.1.own_hbm = bf16[32,2,128,128]{3,2,1,0:T(8,128)(2,1)S(1)} async-done(((bf16[32,2,128,128]{3,2,1,0:T(8,128)(2,1)}), bf16[32,2,128,128]{3,2,1,0:T(8,128)(2,1)S(1)}, u32[]{:S(2)}, u32[]{:S(2)}) %all-to-all-start.1) | async-done | bytes 2097184 | tf_op jit(solution)/shard_map/all_to_all | solution.py:268
  46.6 0.7 pad_add_fusion.1.chunks
  48.3 0.7 pad_add_fusion.3.chunks
  49.0 6.1 %all-to-all-start = ((bf16[32,128,128]{2,1,0:T(8,128)(2,1)}), bf16[32,128,128]{2,1,0:T(8,128)(2,1)S(1)}, u32[]{:S(2)}, u32[]{:S(2)}) async-start(bf16[32,128,128]{2,1,0:T(8,128)(2,1)} %bitcast.10), calls=%async_computation | async-start | bytes 2097152 | tf_op jit(solution)/shard_map/all_to_all | solution.py:268
  55.1 1.0 slice.42
  56.1 1.2 slice.43
  57.3 2.0 %collective-permute-start.4 = (bf16[20,2,128,128]{3,2,1,0:T(8,128)(2,1)}, bf16[20,2,128,128]{3,2,1,0:T(8,128)(2,1)}, u32[]{:S(2)}, u32[]{:S(2)}) collective-permute-start(bf16[20,2,128,128]{3,2,1,0:T(8,128)(2,1)} %slice.43), channel_id=1, source_target_pairs={{0,1},{1,0},{2,3},{3,2},{4,5},{5,4},{6,7},{7,6},{8,9},{9,8},{10,11... | collective-permute-start | bytes 3932168 | tf_op jit(solution)/shard_map/ppermute | solution.py:272
  59.3 14.1 %all-to-all-done.q_hbm = bf16[32,128,128]{2,1,0:T(8,128)(2,1)S(1)} async-done(((bf16[32,128,128]{2,1,0:T(8,128)(2,1)}), bf16[32,128,128]{2,1,0:T(8,128)(2,1)S(1)}, u32[]{:S(2)}, u32[]{:S(2)}) %all-to-all-start) | async-done | bytes 1048608 | tf_op jit(solution)/shard_map/all_to_all | solution.py:268
  73.4 13.4 %shard_map.57 = (f32[33,128,128]{2,1,0:T(8,128)}, f32[33,1,128]{2,1,0:T(1,128)S(1)}, f32[33,8,128]{2,1,0:T(8,128)S(1)}) custom-call(s32[196]{0:T(256)S(1)} %pad_add_fusion.1.chunks, s32[1584]{0:T(1024)S(1)} %reshape.162.lists, s32[33]{0:T(128)S(1)} %pad.21.counts, bf16[32,128,128]{2,1,0:T(8,128)(2,1)S(1)} %all-to-all-done.q_hbm, ...), custom_call_target="tpu_custom_call" | custom-call | flops 1000000 | bytes 1 | tf_op jit(solution)/shard_map/pallas_call | solution.py:220
  86.9 2.5 %collective-permute-done.3.other_hbm = bf16[12,2,128,128]{3,2,1,0:T(8,128)(2,1)S(1)} collective-permute-done((bf16[12,2,128,128]{3,2,1,0:T(8,128)(2,1)}, bf16[12,2,128,128]{3,2,1,0:T(8,128)(2,1)S(1)}, u32[]{:S(2)}, u32[]{:S(2)}) %collective-permute-start.3) | collective-permute-done | bytes 786464 | tf_op jit(solution)/shard_map/ppermute | solution.py:271
  89.4 7.4 %shard_map.58 = (f32[33,128,128]{2,1,0:T(8,128)S(1)}, f32[33,1,128]{2,1,0:T(1,128)S(1)}, f32[33,8,128]{2,1,0:T(8,128)S(1)}) custom-call(s32[196]{0:T(256)S(1)} %pad_add_fusion.2.chunks, s32[1584]{0:T(1024)S(1)} %reshape.163.lists, s32[33]{0:T(128)S(1)} %pad.23.counts, bf16[32,128,128]{2,1,0:T(8,128)(2,1)S(1)} %all-to-all-done.q_hbm, ...), custom_call_target="tpu_custom_call" | custom-call | flops 1000000 | bytes 1 | tf_op jit(solution)/shard_map/pallas_call | solution.py:220
  96.9 1.3 copy-done
  98.2 6.0 %collective-permute-done.4.own_hbm = bf16[20,2,128,128]{3,2,1,0:T(8,128)(2,1)} collective-permute-done((bf16[20,2,128,128]{3,2,1,0:T(8,128)(2,1)}, bf16[20,2,128,128]{3,2,1,0:T(8,128)(2,1)}, u32[]{:S(2)}, u32[]{:S(2)}) %collective-permute-start.4) | collective-permute-done | bytes 1310752 | tf_op jit(solution)/shard_map/ppermute | solution.py:272
  104.2 3.2 %collective-permute-done.5.other_hbm = bf16[20,2,128,128]{3,2,1,0:T(8,128)(2,1)S(1)} collective-permute-done((bf16[20,2,128,128]{3,2,1,0:T(8,128)(2,1)}, bf16[20,2,128,128]{3,2,1,0:T(8,128)(2,1)S(1)}, u32[]{:S(2)}, u32[]{:S(2)}) %collective-permute-start.5) | collective-permute-done | bytes 1310752 | tf_op jit(solution)/shard_map/ppermute | solution.py:271
  107.4 9.5 %shard_map.59 = bf16[32,128,128]{2,1,0:T(8,128)(2,1)S(1)} custom-call(s32[196]{0:T(256)S(1)} %pad_add_fusion.3.chunks, s32[1584]{0:T(1024)S(1)} %reshape.164.lists, s32[33]{0:T(128)S(1)} %pad.25.counts, bf16[32,128,128]{2,1,0:T(8,128)(2,1)S(1)} %all-to-all-done.q_hbm, bf16[20,2,128,128]{3,2,1,0:T(8,128)(2,1)} %collective-permute-done.4.own_hbm, ...), custom_call_target="tpu_custom_call" | custom-call | flops 1000000 | bytes 1 | tf_op jit(solution)/shard_map/pallas_call | solution.py:220
  116.9 33.9 %all_to_all.15 = bf16[32,128,128]{2,1,0:T(8,128)(2,1)} all-to-all(bf16[32,128,128]{2,1,0:T(8,128)(2,1)S(1)} %shard_map.59), channel_id=1, replica_groups={{0,8,16,24,32,40,48,56,64,72,80,88,96,104,112,120,3,11,19,27,35,43,51,5..., dimensions={0} | all-to-all | bytes 2097152 | tf_op jit(solution)/shard_map/all_to_all | solution.py:268
  150.8 3.5 %shard_map.60 = bf16[128,4096]{1,0:T(8,128)(2,1)} custom-call(bf16[2,16,128,128]{3,2,1,0:T(8,128)(2,1)} %bitcast.11), custom_call_target="tpu_custom_call" | custom-call | tf_op jit(solution)/shard_map/pallas_call | solution.py:63
  (46 shorter events, 4.6 us)
Async XLA Ops:
  0.9 18.3 %collective-permute-start = (s32[128,49]{1,0:T(8,128)S(1)}, s32[128,49]{1,0:T(8,128)S(1)}, u32[]{:S(2)}, u32[]{:S(2)}) collective-permute-start(s32[128,49]{1,0:T(8,128)S(1)} %copy.19), channel_id=1, source_target_pairs={{0,4},{4,0},{8,12},{12,8},{16,20},{20,16},{24,28},{28,24},{32,36},... | collective-permute-start | bytes 75272 | tf_op jit(solution)/shard_map/ppermute | solution.py:271
  5.0 41.6 %all-to-all-start.1 = ((bf16[32,2,128,128]{3,2,1,0:T(8,128)(2,1)}), bf16[32,2,128,128]{3,2,1,0:T(8,128)(2,1)S(1)}, u32[]{:S(2)}, u32[]{:S(2)}) async-start(bf16[32,2,128,128]{3,2,1,0:T(8,128)(2,1)} %bitcast.9), calls=%async_computation.1 | async-start | bytes 4194304 | tf_op jit(solution)/shard_map/all_to_all | solution.py:268
  46.6 26.8 %collective-permute-start.1 = (bf16[32,2,128,128]{3,2,1,0:T(8,128)(2,1)S(1)}, bf16[32,2,128,128]{3,2,1,0:T(8,128)(2,1)}, u32[]{:S(2)}, u32[]{:S(2)}) collective-permute-start(bf16[32,2,128,128]{3,2,1,0:T(8,128)(2,1)S(1)} %all-to-all-done.1.own_hbm), channel_id=1, source_target_pairs={{0,4},{4,0},{8,12},{12,8},{16,20},{20,16},{24,28},{28,24},{32,36},... | collective-permute-start | bytes 6291464 | tf_op jit(solution)/shard_map/ppermute | solution.py:271
  49.0 24.4 %all-to-all-start = ((bf16[32,128,128]{2,1,0:T(8,128)(2,1)}), bf16[32,128,128]{2,1,0:T(8,128)(2,1)S(1)}, u32[]{:S(2)}, u32[]{:S(2)}) async-start(bf16[32,128,128]{2,1,0:T(8,128)(2,1)} %bitcast.10), calls=%async_computation | async-start | bytes 2097152 | tf_op jit(solution)/shard_map/all_to_all | solution.py:268
  56.1 30.7 %collective-permute-start.2 = (bf16[12,2,128,128]{3,2,1,0:T(8,128)(2,1)}, bf16[12,2,128,128]{3,2,1,0:T(8,128)(2,1)}, u32[]{:S(2)}, u32[]{:S(2)}) collective-permute-start(bf16[12,2,128,128]{3,2,1,0:T(8,128)(2,1)} %slice.42), channel_id=1, source_target_pairs={{0,1},{1,0},{2,3},{3,2},{4,5},{5,4},{6,7},{7,6},{8,9},{9,8},{10,11... | collective-permute-start | bytes 2359304 | tf_op jit(solution)/shard_map/ppermute | solution.py:272
  57.3 46.9 %collective-permute-start.4 = (bf16[20,2,128,128]{3,2,1,0:T(8,128)(2,1)}, bf16[20,2,128,128]{3,2,1,0:T(8,128)(2,1)}, u32[]{:S(2)}, u32[]{:S(2)}) collective-permute-start(bf16[20,2,128,128]{3,2,1,0:T(8,128)(2,1)} %slice.43), channel_id=1, source_target_pairs={{0,1},{1,0},{2,3},{3,2},{4,5},{5,4},{6,7},{7,6},{8,9},{9,8},{10,11... | collective-permute-start | bytes 3932168 | tf_op jit(solution)/shard_map/ppermute | solution.py:272
  86.8 2.6 %collective-permute-start.3 = (bf16[12,2,128,128]{3,2,1,0:T(8,128)(2,1)}, bf16[12,2,128,128]{3,2,1,0:T(8,128)(2,1)S(1)}, u32[]{:S(2)}, u32[]{:S(2)}) collective-permute-start(bf16[12,2,128,128]{3,2,1,0:T(8,128)(2,1)} %collective-permute-done.2.own_hbm), channel_id=1, source_target_pairs={{0,4},{4,0},{8,12},{12,8},{16,20},{20,16},{24,28},{28,24},{32,36},... | collective-permute-start | bytes 2359304 | tf_op jit(solution)/shard_map/ppermute | solution.py:271
  96.8 1.4 copy-start
  104.2 3.2 %collective-permute-start.5 = (bf16[20,2,128,128]{3,2,1,0:T(8,128)(2,1)}, bf16[20,2,128,128]{3,2,1,0:T(8,128)(2,1)S(1)}, u32[]{:S(2)}, u32[]{:S(2)}) collective-permute-start(bf16[20,2,128,128]{3,2,1,0:T(8,128)(2,1)} %collective-permute-done.4.own_hbm), channel_id=1, source_target_pairs={{0,4},{4,0},{8,12},{12,8},{16,20},{20,16},{24,28},{28,24},{32,36},... | collective-permute-start | bytes 3932168 | tf_op jit(solution)/shard_map/ppermute | solution.py:271

commit v4 on v3

--- a/solution.py
+++ b/solution.py
@@ -34,7 +34,6 @@
 
 
 STEP = 4
-CUT = 12
 FLAT = pl.BlockSpec((BLOCK, 2 * STEP * HDIM), lambda i: (0, i))
 PACKED = pl.BlockSpec((2, STEP, BLOCK, HDIM), lambda i: (0, i, 0, 0))
 
@@ -164,21 +163,21 @@
     def body(i, carry):
         b0, shrink0, b1, c1, largest1, top, total = carry[:7]
         places0, places1 = list(carry[7 : 7 + GROUP]), list(carry[7 + GROUP :])
-        for u in range(2):
-            b2, c2 = where(2 * i + u + 2)
+        for u in range(4):
+            b2, c2 = where(4 * i + u + 2)
             places2 = places(b2, c2)
-            largest2 = scores(b2, places2, score_bufs[u])
+            largest2 = scores(b2, places2, score_bufs[u % 2])
             top, total, shrink1 = weights(
-                b1, c1, largest1, score_bufs[1 - u], weight_bufs[1 - u], top, total
+                b1, c1, largest1, score_bufs[1 - u % 2], weight_bufs[1 - u % 2], top, total
             )
-            weighted(b0, places0, shrink0, weight_bufs[u])
+            weighted(b0, places0, shrink0, weight_bufs[u % 2])
             b0, shrink0, places0 = b1, shrink1, places1
             b1, c1, largest1, places1 = b2, c2, largest2, places2
         return (b0, shrink0, b1, c1, largest1, top, total, *places0, *places1)
 
     lax.fori_loop(
         0,
-        (steps + 1) // 2,
+        (steps + 3) // 4,
         body,
         (b0, shrink0, b1, c1, largest1, top, total, *places0, *places1),
     )
@@ -245,7 +244,7 @@
     steps = (counts + GROUP - 1) // GROUP
     row = jnp.arange(nq, dtype=jnp.int32)
     ends = jnp.sum(jnp.where(row[:, None] <= row[None, :], steps[:, None], 0), axis=0)
-    t = jnp.arange(nq * ((most + GROUP - 1) // GROUP) + 3, dtype=jnp.int32)
+    t = jnp.arange(nq * ((most + GROUP - 1) // GROUP) + 6, dtype=jnp.int32)
     b = jnp.sum((t[:, None] >= ends[None, :]).astype(jnp.int32), axis=1)
     start = jnp.sum(jnp.where(row[None, :] < b[:, None], steps[None, :], 0), axis=1)
     c = jnp.where(b < nq, t - start, 0)
@@ -284,27 +283,19 @@
     block_core = (blocks % 2) ^ core
     block_place = (blocks // 2) % PLACES
     near = ((block_y == 0) | (block_y == 3)) == outer
-    block_at = (block_y // 2) * PLACES + block_place
-    size = 2 * PLACES
-    near_tables = make_tables(active & near, block_core * size + block_at)
-    far_tables = [
-        make_tables(active & ~near & (block_at < CUT), block_core * CUT + block_at),
-        make_tables(
-            active & ~near & (block_at >= CUT), block_core * (size - CUT) + block_at - CUT
-        ),
-    ]
+    block_at = (block_core * 2 + block_y // 2) * PLACES + block_place
+    near_tables = make_tables(active & near, block_at)
+    far_tables = make_tables(active & ~near, block_at)
 
     kv = swap(pack_kv(keys, values).reshape(2 * PLACES, 2, BLOCK, HDIM))
-    kv_far = [to_pair(kv[:CUT]), to_pair(kv[CUT:])]
+    kv_far = to_pair(kv)
     q, near_tables, far_tables = lax.optimization_barrier(
         (pack_q(queries), near_tables, far_tables)
     )
     q = swap(q.reshape(2 * PLACES, BLOCK, HDIM))
     state = attention(near_tables, q, kv, to_core(kv), None, False)
-    state, far = lax.optimization_barrier((state, kv_far[0]))
-    state = attention(far_tables[0], q, far, to_core(far), state, False)
-    state, far = lax.optimization_barrier((state, kv_far[1]))
-    out = attention(far_tables[1], q, far, to_core(far), state, True)
+    state, kv_far = lax.optimization_barrier((state, kv_far))
+    out = attention(far_tables, q, kv_far, to_core(kv_far), state, True)
     return unpack(swap(out).reshape(2, PLACES, BLOCK, HDIM))
 
 

time: 154 us -> 143 us (0.929)
  blocking collectives: 33.9 us -> 51.5 us
  waiting for transfers between devices: 46.2 us -> 35.5 us
  starting transfers between devices: 19 us -> 10.8 us
  Pallas kernels: 41.3 us -> 36.9 us
  local copies, waits for them, and re-layouts: 5.9 us -> 3.03 us
  other arithmetic: 7.69 us -> 5.26 us
    all_to_all x1 -> x2, blocking collectives: 33.9 us -> 51.5 us  [local(): lax.all_to_all(a, ('seq', 'head'), 0, 0, axis_index_groups=groups, tiled=...]
    all_to_all x2 -> x1, waiting for transfers between devices: 34.5 us -> 23 us  [local(): lax.all_to_all(a, ('seq', 'head'), 0, 0, axis_index_groups=groups, tiled=...]
    all_to_all x2 -> x1, starting transfers between devices: 16.8 us -> 10.7 us  [local(): lax.all_to_all(a, ('seq', 'head'), 0, 0, axis_index_groups=groups, tiled=...]
    pallas_call x3 -> x2, Pallas kernels: 30.4 us -> 25.9 us  [attention(): pl.pallas_call(functools.partial(attention_kernel, first, last), grid_spe...]
    ppermute x2 -> x1, waiting for transfers between devices: 5.96 us -> 8.35 us  [local(): lax.ppermute(a, 'head', [(i, i ^ 1) for i in range(head_count)])]
    slice x2 -> x0, local copies, waits for them, and re-layouts: 2.16 us -> none  [local(): kv_far = [to_pair(kv[:CUT]), to_pair(kv[CUT:])]]
    ppermute x2 -> x1, starting transfers between devices: 2.03 us -> 0.01 us  [local(): lax.ppermute(a, 'head', [(i, i ^ 1) for i in range(head_count)])]
    ppermute x4 -> x3, waiting for transfers between devices: 5.73 us -> 4.16 us  [local(): lax.ppermute(a, 'seq', [(i, i ^ 1) for i in range(seq_count)])]
  transfers between devices with their start and end apart: 8 -> 5, of which waited for: 5 -> 3; matrix products, arithmetic and copies ran while one was open for 7% -> 4% of each run, Pallas kernels for 18% -> 15%
where the time goes in v4:
time: 143 us
  blocking collectives  51.5 us (36%)
  Pallas kernels  36.9 us (26%)
  waiting for transfers between devices  35.5 us (25%)
  starting transfers between devices  10.8 us (8%)
  other arithmetic  5.26 us (4%)
  local copies, waits for them, and re-layouts  3.03 us (2%)
    all_to_all x2, blocking collectives, local(): lax.all_to_all(a, ('seq', 'head'), 0, 0, axis_index_groups=groups, tiled=...  51.5 us
    pallas_call x2, Pallas kernels, attention(): pl.pallas_call(functools.partial(attention_kernel, first, last), grid_spe...  25.9 us
    all_to_all x1, waiting for transfers between devices, local(): lax.all_to_all(a, ('seq', 'head'), 0, 0, axis_index_groups=groups, tiled=...  23 us
    all_to_all x1, starting transfers between devices, local(): lax.all_to_all(a, ('seq', 'head'), 0, 0, axis_index_groups=groups, tiled=...  10.7 us
    ppermute x1, waiting for transfers between devices, local(): lax.ppermute(a, 'head', [(i, i ^ 1) for i in range(head_count)])  8.35 us
    ppermute x3, waiting for transfers between devices, local(): lax.ppermute(a, 'seq', [(i, i ^ 1) for i in range(seq_count)])  4.16 us
    pallas_call x1, Pallas kernels, pack_kv(): pl.pallas_call(pack_kv_kernel, grid=(PLACES // STEP,), in_specs=[FLAT, FL...  4.05 us
    pallas_call x1, Pallas kernels, unpack(): pl.pallas_call(unpack_kernel, grid=(PLACES // STEP,), in_specs=[PACKED],...  3.46 us
  transfers between devices with their start and end apart: 5, of which 3 were waited for; matrix products, arithmetic and copies ran while one was open for 4% of the time, Pallas kernels for 15%

profile of v4, /device:TPU:0, one launch (start us, length us, event | category | flops | bytes accessed | tf_op | source)
XLA Modules:
  0.0 143.1 jit_solution(2078687258568352445)
XLA Ops:
  0.0 0.8 pad_add_fusion
  0.8 0.1 copy.16
  1.0 4.1 %shard_map.56 = bf16[2,16,2,128,128]{4,3,2,1,0:T(8,128)(2,1)} custom-call(bf16[128,4096]{1,0:T(8,128)(2,1)} %k_ref.1, bf16[128,4096]{1,0:T(8,128)(2,1)} %v_ref.1), custom_call_target="tpu_custom_call" | custom-call | tf_op jit(solution)/shard_map/pallas_call | solution.py:42
  5.0 10.7 %all-to-all-start.1 = ((bf16[32,2,128,128]{3,2,1,0:T(8,128)(2,1)}), bf16[32,2,128,128]{3,2,1,0:T(8,128)(2,1)S(1)}, u32[]{:S(2)}, u32[]{:S(2)}) async-start(bf16[32,2,128,128]{3,2,1,0:T(8,128)(2,1)} %bitcast.9), calls=%async_computation.1 | async-start | bytes 4194304 | tf_op jit(solution)/shard_map/all_to_all | solution.py:267
  15.7 3.4 %shard_map.55 = bf16[2,16,128,128]{3,2,1,0:T(8,128)(2,1)} custom-call(bf16[128,4096]{1,0:T(8,128)(2,1)} %q_ref.1), custom_call_target="tpu_custom_call" | custom-call | tf_op jit(solution)/shard_map/pallas_call | solution.py:52
  19.3 0.2 slice_reduce_fusion
  19.5 0.2 convert_reduce_fusion.4
  19.7 0.2 convert_reduce_fusion.5
  20.0 0.6 slice.27
  20.6 0.6 convert_reduce_fusion
  21.2 1.5 %select_reduce_fusion = (s32[32,48]{1,0:T(8,128)S(1)}, s32[32,48]{1,0:T(8,128)S(1)}) fusion(s32[32,48]{1,0:T(8,128)S(1)} %get-tuple-element.35, s32[32,48]{1,0:T(8,128)S(1)} %fusion.7, pred[32,48]{1,0:T(8,128)(4,1)S(1)} %get-tuple-element.38, pred[32,48]{1,0:T(8,128)(4,1)S(1)} %get-tuple-element.42, s32[32,48]{1,0:T(8,128)S(1)} %get-tuple-element.36), kind=kLoop, calls=%fused_computation | loop fusion | flops 586752 | bytes 33792 | tf_op jit(solution)/shard_map/reduce_sum | solution.py:242
  23.0 0.6 slice.26
  23.6 23.0 %all-to-all-done.1.own_hbm = bf16[32,2,128,128]{3,2,1,0:T(8,128)(2,1)S(1)} async-done(((bf16[32,2,128,128]{3,2,1,0:T(8,128)(2,1)}), bf16[32,2,128,128]{3,2,1,0:T(8,128)(2,1)S(1)}, u32[]{:S(2)}, u32[]{:S(2)}) %all-to-all-start.1) | async-done | bytes 2097184 | tf_op jit(solution)/shard_map/all_to_all | solution.py:267
  46.7 0.1 select_reduce_fusion.2
  46.8 0.7 pad_add_fusion.2.chunks
  47.7 0.7 pad_add_fusion.1.chunks
  48.4 24.4 %all_to_all.15.q_hbm = bf16[32,128,128]{2,1,0:T(8,128)(2,1)S(1)} all-to-all(bf16[32,128,128]{2,1,0:T(8,128)(2,1)} %bitcast.10), channel_id=1, replica_groups={{0,8,16,24,32,40,48,56,64,72,80,88,96,104,112,120,3,11,19,27,35,43,51,5..., dimensions={0} | all-to-all | bytes 2097152 | tf_op jit(solution)/shard_map/all_to_all | solution.py:267
  72.8 13.5 %shard_map.57 = (f32[33,128,128]{2,1,0:T(8,128)}, f32[33,1,128]{2,1,0:T(1,128)S(1)}, f32[33,8,128]{2,1,0:T(8,128)S(1)}) custom-call(s32[199]{0:T(256)S(1)} %pad_add_fusion.1.chunks, s32[1584]{0:T(1024)S(1)} %reshape.117.lists, s32[33]{0:T(128)S(1)} %pad.15.counts, bf16[32,128,128]{2,1,0:T(8,128)(2,1)S(1)} %all_to_all.15.q_hbm, ...), custom_call_target="tpu_custom_call" | custom-call | flops 1000000 | bytes 1 | tf_op jit(solution)/shard_map/pallas_call | solution.py:219
  86.3 8.3 %collective-permute-done.2.own_hbm = bf16[32,2,128,128]{3,2,1,0:T(8,128)(2,1)S(1)} collective-permute-done((bf16[32,2,128,128]{3,2,1,0:T(8,128)(2,1)S(1)}, bf16[32,2,128,128]{3,2,1,0:T(8,128)(2,1)S(1)}, u32[]{:S(2)}, u32[]{:S(2)}) %collective-permute-start.2) | collective-permute-done | bytes 2097184 | tf_op jit(solution)/shard_map/ppermute | solution.py:271
  94.7 4.2 %collective-permute-done.3.other_hbm = bf16[32,2,128,128]{3,2,1,0:T(8,128)(2,1)S(1)} collective-permute-done((bf16[32,2,128,128]{3,2,1,0:T(8,128)(2,1)S(1)}, bf16[32,2,128,128]{3,2,1,0:T(8,128)(2,1)S(1)}, u32[]{:S(2)}, u32[]{:S(2)}) %collective-permute-start.3) | collective-permute-done | bytes 2097184 | tf_op jit(solution)/shard_map/ppermute | solution.py:270
  98.8 1.3 copy-done
  100.1 12.4 %shard_map.58 = bf16[32,128,128]{2,1,0:T(8,128)(2,1)S(1)} custom-call(s32[199]{0:T(256)S(1)} %pad_add_fusion.2.chunks, s32[1584]{0:T(1024)S(1)} %reshape.118.lists, s32[33]{0:T(128)S(1)} %pad.17.counts, bf16[32,128,128]{2,1,0:T(8,128)(2,1)S(1)} %all_to_all.15.q_hbm, bf16[32,2,128,128]{3,2,1,0:T(8,128)(2,1)S(1)} %collective-permute-done.2.own_hbm, ...), custom_call_target="tpu_custom_call" | custom-call | flops 1000000 | bytes 1 | tf_op jit(solution)/shard_map/pallas_call | solution.py:219
  112.5 27.1 %all_to_all.16 = bf16[32,128,128]{2,1,0:T(8,128)(2,1)} all-to-all(bf16[32,128,128]{2,1,0:T(8,128)(2,1)S(1)} %shard_map.58), channel_id=1, replica_groups={{0,8,16,24,32,40,48,56,64,72,80,88,96,104,112,120,3,11,19,27,35,43,51,5..., dimensions={0} | all-to-all | bytes 2097152 | tf_op jit(solution)/shard_map/all_to_all | solution.py:267
  139.7 3.5 %shard_map.59 = bf16[128,4096]{1,0:T(8,128)(2,1)} custom-call(bf16[2,16,128,128]{3,2,1,0:T(8,128)(2,1)} %bitcast.11), custom_call_target="tpu_custom_call" | custom-call | tf_op jit(solution)/shard_map/pallas_call | solution.py:62
  (27 shorter events, 0.9 us)
Async XLA Ops:
  0.9 18.3 %collective-permute-start = (s32[128,49]{1,0:T(8,128)S(1)}, s32[128,49]{1,0:T(8,128)S(1)}, u32[]{:S(2)}, u32[]{:S(2)}) collective-permute-start(s32[128,49]{1,0:T(8,128)S(1)} %copy.16), channel_id=1, source_target_pairs={{0,4},{4,0},{8,12},{12,8},{16,20},{20,16},{24,28},{28,24},{32,36},... | collective-permute-start | bytes 75272 | tf_op jit(solution)/shard_map/ppermute | solution.py:270
  5.0 41.6 %all-to-all-start.1 = ((bf16[32,2,128,128]{3,2,1,0:T(8,128)(2,1)}), bf16[32,2,128,128]{3,2,1,0:T(8,128)(2,1)S(1)}, u32[]{:S(2)}, u32[]{:S(2)}) async-start(bf16[32,2,128,128]{3,2,1,0:T(8,128)(2,1)} %bitcast.9), calls=%async_computation.1 | async-start | bytes 4194304 | tf_op jit(solution)/shard_map/all_to_all | solution.py:267
  46.6 26.2 %collective-permute-start.1 = (bf16[32,2,128,128]{3,2,1,0:T(8,128)(2,1)S(1)}, bf16[32,2,128,128]{3,2,1,0:T(8,128)(2,1)S(1)}, u32[]{:S(2)}, u32[]{:S(2)}) collective-permute-start(bf16[32,2,128,128]{3,2,1,0:T(8,128)(2,1)S(1)} %all-to-all-done.1.own_hbm), channel_id=1, source_target_pairs={{0,4},{4,0},{8,12},{12,8},{16,20},{20,16},{24,28},{28,24},{32,36},... | collective-permute-start | bytes 6291464 | tf_op jit(solution)/shard_map/ppermute | solution.py:270
  46.6 48.0 %collective-permute-start.2 = (bf16[32,2,128,128]{3,2,1,0:T(8,128)(2,1)S(1)}, bf16[32,2,128,128]{3,2,1,0:T(8,128)(2,1)S(1)}, u32[]{:S(2)}, u32[]{:S(2)}) collective-permute-start(bf16[32,2,128,128]{3,2,1,0:T(8,128)(2,1)S(1)} %all-to-all-done.1.own_hbm), channel_id=1, source_target_pairs={{0,1},{1,0},{2,3},{3,2},{4,5},{5,4},{6,7},{7,6},{8,9},{9,8},{10,11... | collective-permute-start | bytes 6291464 | tf_op jit(solution)/shard_map/ppermute | solution.py:271
  94.7 4.2 %collective-permute-start.3 = (bf16[32,2,128,128]{3,2,1,0:T(8,128)(2,1)S(1)}, bf16[32,2,128,128]{3,2,1,0:T(8,128)(2,1)S(1)}, u32[]{:S(2)}, u32[]{:S(2)}) collective-permute-start(bf16[32,2,128,128]{3,2,1,0:T(8,128)(2,1)S(1)} %collective-permute-done.2.own_hbm), channel_id=1, source_target_pairs={{0,4},{4,0},{8,12},{12,8},{16,20},{20,16},{24,28},{28,24},{32,36},... | collective-permute-start | bytes 6291464 | tf_op jit(solution)/shard_map/ppermute | solution.py:270
  98.8 1.3 copy-start

commit v5 on v4

--- a/solution.py
+++ b/solution.py
@@ -13,7 +13,7 @@
 FACTOR = LOG2E / HDIM**0.5
 GROUP = 8
 PLACES = 16
-VMEM = 48 << 20
+VMEM = 24 << 20
 
 
 def pack_kv_kernel(k_ref, v_ref, o_ref):
@@ -33,7 +33,7 @@
         o_ref[:, h * HDIM : (h + 1) * HDIM] = x_ref[h % 2, h // 2]
 
 
-STEP = 4
+STEP = 8
 FLAT = pl.BlockSpec((BLOCK, 2 * STEP * HDIM), lambda i: (0, i))
 PACKED = pl.BlockSpec((2, STEP, BLOCK, HDIM), lambda i: (0, i, 0, 0))
 
@@ -270,6 +270,9 @@
     to_core = lambda a: lax.ppermute(a, "seq", [(i, i ^ 1) for i in range(seq_count)])
     to_pair = lambda a: lax.ppermute(a, "head", [(i, i ^ 1) for i in range(head_count)])
 
+    kv = pack_kv(keys, values)
+    kv, key_blocks, key_count = lax.optimization_barrier((kv, key_blocks, key_count))
+
     odd = (y >= 2).astype(jnp.int32)
     mine = jnp.concatenate([key_blocks[0], key_count[0][:, None]], axis=1)
     mine = jnp.where(core == odd, mine, to_core(mine))
@@ -287,11 +290,15 @@
     near_tables = make_tables(active & near, block_at)
     far_tables = make_tables(active & ~near, block_at)
 
-    kv = swap(pack_kv(keys, values).reshape(2 * PLACES, 2, BLOCK, HDIM))
+    kv, q, near_tables, far_tables = lax.optimization_barrier(
+        (
+            swap(kv.reshape(2 * PLACES, 2, BLOCK, HDIM)),
+            pack_q(queries),
+            near_tables,
+            far_tables,
+        )
+    )
     kv_far = to_pair(kv)
-    q, near_tables, far_tables = lax.optimization_barrier(
-        (pack_q(queries), near_tables, far_tables)
-    )
     q = swap(q.reshape(2 * PLACES, BLOCK, HDIM))
     state = attention(near_tables, q, kv, to_core(kv), None, False)
     state, kv_far = lax.optimization_barrier((state, kv_far))

time: 143 us -> 138 us (0.965)
  Pallas kernels: 36.9 us -> 31.8 us
  waiting for transfers between devices: 35.5 us -> 37.3 us
    ppermute x1, waiting for transfers between devices: 8.35 us -> 10.6 us  [local(): lax.ppermute(a, 'head', [(i, i ^ 1) for i in range(head_count)])]
  transfers between devices with their start and end apart: 5 -> 5, of which waited for: 3 -> 3; matrix products, arithmetic and copies ran while one was open for 4% -> 4% of each run, Pallas kernels for 15% -> 11%
where the time goes in v5:
time: 138 us
  blocking collectives  51.6 us (37%)
  waiting for transfers between devices  37.3 us (27%)
  Pallas kernels  31.8 us (23%)
  starting transfers between devices  10.8 us (8%)
  other arithmetic  4.51 us (3%)
  local copies, waits for them, and re-layouts  1.73 us (1%)
    all_to_all x2, blocking collectives, local(): lax.all_to_all(a, ('seq', 'head'), 0, 0, axis_index_groups=groups, tiled=...  51.6 us
    pallas_call x2, Pallas kernels, attention(): pl.pallas_call(functools.partial(attention_kernel, first, last), grid_spe...  24.6 us
    all_to_all x1, waiting for transfers between devices, local(): lax.all_to_all(a, ('seq', 'head'), 0, 0, axis_index_groups=groups, tiled=...  22.5 us
    all_to_all x1, starting transfers between devices, local(): lax.all_to_all(a, ('seq', 'head'), 0, 0, axis_index_groups=groups, tiled=...  10.7 us
    ppermute x1, waiting for transfers between devices, local(): lax.ppermute(a, 'head', [(i, i ^ 1) for i in range(head_count)])  10.6 us
    ppermute x3, waiting for transfers between devices, local(): lax.ppermute(a, 'seq', [(i, i ^ 1) for i in range(seq_count)])  4.16 us
    pallas_call x1, Pallas kernels, pack_kv(): pl.pallas_call(pack_kv_kernel, grid=(PLACES // STEP,), in_specs=[FLAT, FL...  2.85 us
  transfers between devices with their start and end apart: 5, of which 3 were waited for; matrix products, arithmetic and copies ran while one was open for 4% of the time, Pallas kernels for 11%

profile of v5, /device:TPU:0, one launch (start us, length us, event | category | flops | bytes accessed | tf_op | source)
XLA Modules:
  0.0 137.8 jit_solution(6879182108817768865)
XLA Ops:
  0.0 2.8 %shard_map.55 = bf16[2,16,2,128,128]{4,3,2,1,0:T(8,128)(2,1)} custom-call(bf16[128,4096]{1,0:T(8,128)(2,1)} %k_ref.1, bf16[128,4096]{1,0:T(8,128)(2,1)} %v_ref.1), custom_call_target="tpu_custom_call" | custom-call | tf_op jit(solution)/shard_map/pallas_call | solution.py:42
  2.9 0.1 copy.16
  3.1 10.7 %all-to-all-start = ((bf16[32,2,128,128]{3,2,1,0:T(8,128)(2,1)}), bf16[32,2,128,128]{3,2,1,0:T(8,128)(2,1)S(1)}, u32[]{:S(2)}, u32[]{:S(2)}) async-start(bf16[32,2,128,128]{3,2,1,0:T(8,128)(2,1)} %bitcast.9), calls=%async_computation | async-start | bytes 4194304 | tf_op jit(solution)/shard_map/all_to_all | solution.py:267
  13.8 2.1 %shard_map.56 = bf16[2,16,128,128]{3,2,1,0:T(8,128)(2,1)} custom-call(bf16[128,4096]{1,0:T(8,128)(2,1)} %q_ref.1), custom_call_target="tpu_custom_call" | custom-call | tf_op jit(solution)/shard_map/pallas_call | solution.py:52
  16.0 0.2 slice_reduce_fusion
  16.2 0.2 convert_reduce_fusion.4
  16.4 0.2 convert_reduce_fusion.5
  16.6 0.1 select_reduce_fusion.4
  16.7 0.6 slice.27
  17.3 0.6 convert_reduce_fusion
  18.0 1.5 %select_reduce_fusion = (s32[32,48]{1,0:T(8,128)S(1)}, s32[32,48]{1,0:T(8,128)S(1)}) fusion(s32[32,48]{1,0:T(8,128)S(1)} %get-tuple-element.43, s32[32,48]{1,0:T(8,128)S(1)} %fusion.7, pred[32,48]{1,0:T(8,128)(4,1)S(1)} %get-tuple-element.46, pred[32,48]{1,0:T(8,128)(4,1)S(1)} %get-tuple-element.50, s32[32,48]{1,0:T(8,128)S(1)} %get-tuple-element.44), kind=kLoop, calls=%fused_computation | loop fusion | flops 586752 | bytes 33792 | tf_op jit(solution)/shard_map/reduce_sum | solution.py:242
  19.8 0.6 slice.26
  20.5 0.1 select_reduce_fusion.2
  20.6 0.7 pad_add_fusion.2.chunks
  21.4 0.1 select_reduce_fusion.3
  21.5 0.7 pad_add_fusion.1.chunks
  22.1 22.5 %all-to-all-done.own_hbm = bf16[32,2,128,128]{3,2,1,0:T(8,128)(2,1)S(1)} async-done(((bf16[32,2,128,128]{3,2,1,0:T(8,128)(2,1)}), bf16[32,2,128,128]{3,2,1,0:T(8,128)(2,1)S(1)}, u32[]{:S(2)}, u32[]{:S(2)}) %all-to-all-start) | async-done | bytes 2097184 | tf_op jit(solution)/shard_map/all_to_all | solution.py:267
  44.7 24.4 %all_to_all.15.q_hbm = bf16[32,128,128]{2,1,0:T(8,128)(2,1)S(1)} all-to-all(bf16[32,128,128]{2,1,0:T(8,128)(2,1)} %bitcast.10), channel_id=1, replica_groups={{0,8,16,24,32,40,48,56,64,72,80,88,96,104,112,120,3,11,19,27,35,43,51,5..., dimensions={0} | all-to-all | bytes 2097152 | tf_op jit(solution)/shard_map/all_to_all | solution.py:267
  69.1 13.0 %shard_map.57 = (f32[33,128,128]{2,1,0:T(8,128)S(1)}, f32[33,1,128]{2,1,0:T(1,128)S(1)}, f32[33,8,128]{2,1,0:T(8,128)S(1)}) custom-call(s32[199]{0:T(256)S(1)} %pad_add_fusion.1.chunks, s32[1584]{0:T(1024)S(1)} %reshape.118.lists, s32[33]{0:T(128)S(1)} %pad.15.counts, bf16[32,128,128]{2,1,0:T(8,128)(2,1)S(1)} %all_to_all.15.q_hbm, ...), custom_call_target="tpu_custom_call" | custom-call | flops 1000000 | bytes 1 | tf_op jit(solution)/shard_map/pallas_call | solution.py:219
  82.1 10.6 %collective-permute-done.2.own_hbm = bf16[32,2,128,128]{3,2,1,0:T(8,128)(2,1)S(1)} collective-permute-done((bf16[32,2,128,128]{3,2,1,0:T(8,128)(2,1)S(1)}, bf16[32,2,128,128]{3,2,1,0:T(8,128)(2,1)S(1)}, u32[]{:S(2)}, u32[]{:S(2)}) %collective-permute-start.2) | collective-permute-done | bytes 2097184 | tf_op jit(solution)/shard_map/ppermute | solution.py:271
  92.7 4.2 %collective-permute-done.3.other_hbm = bf16[32,2,128,128]{3,2,1,0:T(8,128)(2,1)S(1)} collective-permute-done((bf16[32,2,128,128]{3,2,1,0:T(8,128)(2,1)S(1)}, bf16[32,2,128,128]{3,2,1,0:T(8,128)(2,1)S(1)}, u32[]{:S(2)}, u32[]{:S(2)}) %collective-permute-start.3) | collective-permute-done | bytes 2097184 | tf_op jit(solution)/shard_map/ppermute | solution.py:270
  96.9 11.6 %shard_map.58 = bf16[32,128,128]{2,1,0:T(8,128)(2,1)S(1)} custom-call(s32[199]{0:T(256)S(1)} %pad_add_fusion.2.chunks, s32[1584]{0:T(1024)S(1)} %reshape.119.lists, s32[33]{0:T(128)S(1)} %pad.17.counts, bf16[32,128,128]{2,1,0:T(8,128)(2,1)S(1)} %all_to_all.15.q_hbm, bf16[32,2,128,128]{3,2,1,0:T(8,128)(2,1)S(1)} %collective-permute-done.2.own_hbm, ...), custom_call_target="tpu_custom_call" | custom-call | flops 1000000 | bytes 1 | tf_op jit(solution)/shard_map/pallas_call | solution.py:219
  108.5 27.2 %all_to_all.16 = bf16[32,128,128]{2,1,0:T(8,128)(2,1)} all-to-all(bf16[32,128,128]{2,1,0:T(8,128)(2,1)S(1)} %shard_map.58), channel_id=1, replica_groups={{0,8,16,24,32,40,48,56,64,72,80,88,96,104,112,120,3,11,19,27,35,43,51,5..., dimensions={0} | all-to-all | bytes 2097152 | tf_op jit(solution)/shard_map/all_to_all | solution.py:267
  135.7 2.1 %shard_map.59 = bf16[128,4096]{1,0:T(8,128)(2,1)} custom-call(bf16[2,16,128,128]{3,2,1,0:T(8,128)(2,1)} %bitcast.11), custom_call_target="tpu_custom_call" | custom-call | tf_op jit(solution)/shard_map/pallas_call | solution.py:62
  (29 shorter events, 0.7 us)
Async XLA Ops:
  0.0 2.9 %copy-start = (s32[1,128,48]{1,2,0:T(8,128)S(1)}, s32[1,128,48]{1,2,0:T(8,128)}, u32[]{:S(2)}) copy-start(s32[1,128,48]{1,2,0:T(8,128)} %param.8) | copy-start | bytes 73732
  0.0 2.9 %copy-start.1 = (s32[1,128]{1,0:T(1,128)S(1)}, s32[1,128]{1,0:T(1,128)}, u32[]{:S(2)}) copy-start(s32[1,128]{1,0:T(1,128)} %param.9) | copy-start | bytes 1540
  3.0 13.0 %collective-permute-start = (s32[128,49]{1,0:T(8,128)S(1)}, s32[128,49]{1,0:T(8,128)S(1)}, u32[]{:S(2)}, u32[]{:S(2)}) collective-permute-start(s32[128,49]{1,0:T(8,128)S(1)} %copy.16), channel_id=1, source_target_pairs={{0,4},{4,0},{8,12},{12,8},{16,20},{20,16},{24,28},{28,24},{32,36},... | collective-permute-start | bytes 75272 | tf_op jit(solution)/shard_map/ppermute | solution.py:270
  3.1 41.6 %all-to-all-start = ((bf16[32,2,128,128]{3,2,1,0:T(8,128)(2,1)}), bf16[32,2,128,128]{3,2,1,0:T(8,128)(2,1)S(1)}, u32[]{:S(2)}, u32[]{:S(2)}) async-start(bf16[32,2,128,128]{3,2,1,0:T(8,128)(2,1)} %bitcast.9), calls=%async_computation | async-start | bytes 4194304 | tf_op jit(solution)/shard_map/all_to_all | solution.py:267
  44.7 24.4 %collective-permute-start.1 = (bf16[32,2,128,128]{3,2,1,0:T(8,128)(2,1)S(1)}, bf16[32,2,128,128]{3,2,1,0:T(8,128)(2,1)S(1)}, u32[]{:S(2)}, u32[]{:S(2)}) collective-permute-start(bf16[32,2,128,128]{3,2,1,0:T(8,128)(2,1)S(1)} %all-to-all-done.own_hbm), channel_id=1, source_target_pairs={{0,4},{4,0},{8,12},{12,8},{16,20},{20,16},{24,28},{28,24},{32,36},... | collective-permute-start | bytes 6291464 | tf_op jit(solution)/shard_map/ppermute | solution.py:270
  44.7 48.0 %collective-permute-start.2 = (bf16[32,2,128,128]{3,2,1,0:T(8,128)(2,1)S(1)}, bf16[32,2,128,128]{3,2,1,0:T(8,128)(2,1)S(1)}, u32[]{:S(2)}, u32[]{:S(2)}) collective-permute-start(bf16[32,2,128,128]{3,2,1,0:T(8,128)(2,1)S(1)} %all-to-all-done.own_hbm), channel_id=1, source_target_pairs={{0,1},{1,0},{2,3},{3,2},{4,5},{5,4},{6,7},{7,6},{8,9},{9,8},{10,11... | collective-permute-start | bytes 6291464 | tf_op jit(solution)/shard_map/ppermute | solution.py:271
  92.7 4.2 %collective-permute-start.3 = (bf16[32,2,128,128]{3,2,1,0:T(8,128)(2,1)S(1)}, bf16[32,2,128,128]{3,2,1,0:T(8,128)(2,1)S(1)}, u32[]{:S(2)}, u32[]{:S(2)}) collective-permute-start(bf16[32,2,128,128]{3,2,1,0:T(8,128)(2,1)S(1)} %collective-permute-done.2.own_hbm), channel_id=1, source_target_pairs={{0,4},{4,0},{8,12},{12,8},{16,20},{20,16},{24,28},{28,24},{32,36},... | collective-permute-start | bytes 6291464 | tf_op jit(solution)/shard_map/ppermute | solution.py:270

commit v6 on v5

--- a/solution.py
+++ b/solution.py
@@ -11,7 +11,9 @@
 HDIM = 128
 LOG2E = 1.4426950408889634
 FACTOR = LOG2E / HDIM**0.5
+CUT = 12
 GROUP = 8
+UNROLLS = (16, 4, 2)
 PLACES = 16
 VMEM = 24 << 20
 
@@ -69,9 +71,10 @@
 
 
 def attention_kernel(
-    first, last, chunks, lists, counts, q_hbm, own_hbm, other_hbm, *rest
+    first, last, parts, chunks, lists, counts, q_hbm, *rest
 ):
     rest = list(rest)
+    kv_hbm = [rest.pop(0) for _ in range(parts)]
     if not first:
         acc_in, top_in, total_in = (rest.pop(0) for _ in range(3))
     if last:
@@ -82,14 +85,13 @@
     s0, s1, p0, p1, q_ref, kv_ref = rest[:6]
     sems = rest[-1]
     nq = q_hbm.shape[0]
-    half = own_hbm.shape[0]
     most = lists.shape[0] // (nq + 1)
 
-    copies = [
-        (q_hbm, q_ref),
-        (own_hbm, kv_ref.at[pl.ds(0, half)]),
-        (other_hbm, kv_ref.at[pl.ds(half, half)]),
-    ]
+    copies = [(q_hbm, q_ref)]
+    at = 0
+    for part in kv_hbm:
+        copies.append((part, kv_ref.at[pl.ds(at, part.shape[0])]))
+        at += part.shape[0]
     if not first:
         copies += [(acc_in, acc_ref), (top_in, top_ref), (total_in, total_ref)]
     copies = [
@@ -123,13 +125,13 @@
         count = counts[b]
         top = jnp.where(c == 0, top_ref[b], top)
         total = jnp.where(c == 0, total_ref[b], total)
-        new_top = jnp.maximum(top, jnp.max(largest, axis=0, keepdims=True) * FACTOR)
-        shrink = jnp.exp2(top - new_top)
+        new_top = jnp.maximum(top, jnp.max(largest, axis=0, keepdims=True))
+        shrink = jnp.exp2((top - new_top) * FACTOR)
         total = total * shrink
         for g in range(GROUP):
             rows = slice(g * BLOCK, (g + 1) * BLOCK)
             base = jnp.where(c * GROUP + g < count, new_top, jnp.inf)
-            weight = jnp.exp2(src[rows, :] * FACTOR - base)
+            weight = jnp.exp2((src[rows, :] - base) * FACTOR)
             total = total + jnp.sum(weight.reshape(BLOCK // 8, 8, BLOCK), axis=0)
             dst[rows, :] = weight.astype(jnp.bfloat16)
         top_ref[b] = new_top
@@ -160,27 +162,31 @@
         jnp.zeros((8, BLOCK), jnp.float32),
     )
 
-    def body(i, carry):
-        b0, shrink0, b1, c1, largest1, top, total = carry[:7]
-        places0, places1 = list(carry[7 : 7 + GROUP]), list(carry[7 + GROUP :])
-        for u in range(4):
-            b2, c2 = where(4 * i + u + 2)
-            places2 = places(b2, c2)
-            largest2 = scores(b2, places2, score_bufs[u % 2])
-            top, total, shrink1 = weights(
-                b1, c1, largest1, score_bufs[1 - u % 2], weight_bufs[1 - u % 2], top, total
-            )
-            weighted(b0, places0, shrink0, weight_bufs[u % 2])
-            b0, shrink0, places0 = b1, shrink1, places1
-            b1, c1, largest1, places1 = b2, c2, largest2, places2
-        return (b0, shrink0, b1, c1, largest1, top, total, *places0, *places1)
-
-    lax.fori_loop(
-        0,
-        (steps + 3) // 4,
-        body,
-        (b0, shrink0, b1, c1, largest1, top, total, *places0, *places1),
-    )
+    def body(start, unroll):
+        def run(i, carry):
+            b0, shrink0, b1, c1, largest1, top, total = carry[:7]
+            places0, places1 = list(carry[7 : 7 + GROUP]), list(carry[7 + GROUP :])
+            for u in range(unroll):
+                b2, c2 = where(start + unroll * i + u + 2)
+                places2 = places(b2, c2)
+                largest2 = scores(b2, places2, score_bufs[u % 2])
+                top, total, shrink1 = weights(
+                    b1, c1, largest1, score_bufs[1 - u % 2], weight_bufs[1 - u % 2], top, total
+                )
+                weighted(b0, places0, shrink0, weight_bufs[u % 2])
+                b0, shrink0, places0 = b1, shrink1, places1
+                b1, c1, largest1, places1 = b2, c2, largest2, places2
+            return (b0, shrink0, b1, c1, largest1, top, total, *places0, *places1)
+
+        return run
+
+    state = (b0, shrink0, b1, c1, largest1, top, total, *places0, *places1)
+    done = 0
+    for unroll in UNROLLS:
+        extra = 1 if unroll == UNROLLS[-1] else 0
+        rounds = (steps - done + extra) // unroll
+        state = lax.fori_loop(0, rounds, body(done, unroll), state)
+        done = done + rounds * unroll
 
     if last:
 
@@ -192,7 +198,7 @@
         lax.fori_loop(0, nq, finish, 0, unroll=4)
 
 
-def attention(tables, q, own, other, state, last):
+def attention(tables, q, kv, state, last):
     chunks, lists, counts = tables
     nq = q.shape[0]
     first = state is None
@@ -205,7 +211,7 @@
         pltpu.VMEM((GROUP * BLOCK, BLOCK), jnp.bfloat16),
         pltpu.VMEM((GROUP * BLOCK, BLOCK), jnp.bfloat16),
         pltpu.VMEM(q.shape, q.dtype),
-        pltpu.VMEM((2 * own.shape[0],) + own.shape[1:], own.dtype),
+        pltpu.VMEM((sum(a.shape[0] for a in kv),) + kv[0].shape[1:], kv[0].dtype),
     ]
     if last:
         scratch += [pltpu.VMEM(s, jnp.float32) for s in shapes]
@@ -214,10 +220,10 @@
     else:
         out_shape = [jax.ShapeDtypeStruct(s, jnp.float32) for s in shapes]
         out_specs = [whole(s) for s in shapes]
-    scratch += [pltpu.SemaphoreType.DMA((6,))]
-    args = [q, own, other] + ([] if first else list(state))
+    scratch += [pltpu.SemaphoreType.DMA((8,))]
+    args = [q, *kv] + ([] if first else list(state))
     return pl.pallas_call(
-        functools.partial(attention_kernel, first, last),
+        functools.partial(attention_kernel, first, last, len(kv)),
         grid_spec=pltpu.PrefetchScalarGridSpec(
             num_scalar_prefetch=3,
             grid=(1,),
@@ -244,7 +250,7 @@
     steps = (counts + GROUP - 1) // GROUP
     row = jnp.arange(nq, dtype=jnp.int32)
     ends = jnp.sum(jnp.where(row[:, None] <= row[None, :], steps[:, None], 0), axis=0)
-    t = jnp.arange(nq * ((most + GROUP - 1) // GROUP) + 6, dtype=jnp.int32)
+    t = jnp.arange(nq * ((most + GROUP - 1) // GROUP) + 4, dtype=jnp.int32)
     b = jnp.sum((t[:, None] >= ends[None, :]).astype(jnp.int32), axis=1)
     start = jnp.sum(jnp.where(row[None, :] < b[:, None], steps[None, :], 0), axis=1)
     c = jnp.where(b < nq, t - start, 0)
@@ -286,23 +292,29 @@
     block_core = (blocks % 2) ^ core
     block_place = (blocks // 2) % PLACES
     near = ((block_y == 0) | (block_y == 3)) == outer
-    block_at = (block_core * 2 + block_y // 2) * PLACES + block_place
-    near_tables = make_tables(active & near, block_at)
-    far_tables = make_tables(active & ~near, block_at)
-
-    kv, q, near_tables, far_tables = lax.optimization_barrier(
+    block_at = (block_y // 2) * PLACES + block_place
+    size = 2 * PLACES
+    early = near | (block_at < CUT)
+    early_place = jnp.where(
+        near, block_core * size + block_at, 2 * size + block_core * CUT + block_at
+    )
+    late_place = block_core * (size - CUT) + block_at - CUT
+    early_tables = make_tables(active & early, early_place)
+    late_tables = make_tables(active & ~early, late_place)
+
+    kv, q, early_tables, late_tables = lax.optimization_barrier(
         (
             swap(kv.reshape(2 * PLACES, 2, BLOCK, HDIM)),
             pack_q(queries),
-            near_tables,
-            far_tables,
+            early_tables,
+            late_tables,
         )
     )
-    kv_far = to_pair(kv)
+    far, far_late = to_pair(kv[:CUT]), to_pair(kv[CUT:])
     q = swap(q.reshape(2 * PLACES, BLOCK, HDIM))
-    state = attention(near_tables, q, kv, to_core(kv), None, False)
-    state, kv_far = lax.optimization_barrier((state, kv_far))
-    out = attention(far_tables, q, kv_far, to_core(kv_far), state, True)
+    state = attention(early_tables, q, [kv, to_core(kv), far, to_core(far)], None, False)
+    state, far_late = lax.optimization_barrier((state, far_late))
+    out = attention(late_tables, q, [far_late, to_core(far_late)], state, True)
     return unpack(swap(out).reshape(2, PLACES, BLOCK, HDIM))
 
 

time: 138 us -> 132 us (0.957)
  blocking collectives: 51.6 us -> 26.7 us
  waiting for transfers between devices: 37.3 us -> 51.4 us
  starting transfers between devices: 10.8 us -> 19.3 us
  Pallas kernels: 31.8 us -> 26 us
  local copies, waits for them, and re-layouts: 1.73 us -> 3.96 us
    all_to_all x2 -> x1, blocking collectives: 51.6 us -> 26.7 us  [local(): lax.all_to_all(a, ('seq', 'head'), 0, 0, axis_index_groups=groups, tiled=...]
    ppermute x1 -> x2, waiting for transfers between devices: 10.6 us -> 21 us  [local(): lax.ppermute(a, 'head', [(i, i ^ 1) for i in range(head_count)])]
    all_to_all x1 -> x2, starting transfers between devices: 10.7 us -> 17.2 us  [local(): lax.all_to_all(a, ('seq', 'head'), 0, 0, axis_index_groups=groups, tiled=...]
    pallas_call x2, Pallas kernels: 24.6 us -> 18.9 us  [attention(): pl.pallas_call(functools.partial(attention_kernel, first, last, len(kv)),...]
    all_to_all x1 -> x2, waiting for transfers between devices: 22.5 us -> 27.2 us  [local(): lax.all_to_all(a, ('seq', 'head'), 0, 0, axis_index_groups=groups, tiled=...]
    slice x0 -> x2, local copies, waits for them, and re-layouts: none -> 2.22 us  [local(): far, far_late = (to_pair(kv[:CUT]), to_pair(kv[CUT:]))]
    ppermute x1 -> x2, starting transfers between devices: 0.01 us -> 2.03 us  [local(): lax.ppermute(a, 'head', [(i, i ^ 1) for i in range(head_count)])]
    ppermute x3 -> x4, waiting for transfers between devices: 4.16 us -> 3.25 us  [local(): lax.ppermute(a, 'seq', [(i, i ^ 1) for i in range(seq_count)])]
  transfers between devices with their start and end apart: 5 -> 8, of which waited for: 3 -> 5; matrix products, arithmetic and copies ran while one was open for 4% -> 7% of each run, Pallas kernels for 11% -> 10%
where the time goes in v6:
time: 132 us
  waiting for transfers between devices  51.4 us (39%)
  blocking collectives  26.7 us (20%)
  Pallas kernels  26 us (20%)
  starting transfers between devices  19.3 us (15%)
  other arithmetic  4.76 us (4%)
  local copies, waits for them, and re-layouts  3.96 us (3%)
    all_to_all x2, waiting for transfers between devices, local(): lax.all_to_all(a, ('seq', 'head'), 0, 0, axis_index_groups=groups, tiled=...  27.2 us
    all_to_all x1, blocking collectives, local(): lax.all_to_all(a, ('seq', 'head'), 0, 0, axis_index_groups=groups, tiled=...  26.7 us
    ppermute x2, waiting for transfers between devices, local(): lax.ppermute(a, 'head', [(i, i ^ 1) for i in range(head_count)])  21 us
    pallas_call x2, Pallas kernels, attention(): pl.pallas_call(functools.partial(attention_kernel, first, last, len(kv)),...  18.9 us
    all_to_all x2, starting transfers between devices, local(): lax.all_to_all(a, ('seq', 'head'), 0, 0, axis_index_groups=groups, tiled=...  17.2 us
    ppermute x4, waiting for transfers between devices, local(): lax.ppermute(a, 'seq', [(i, i ^ 1) for i in range(seq_count)])  3.25 us
    pallas_call x1, Pallas kernels, pack_kv(): pl.pallas_call(pack_kv_kernel, grid=(PLACES // STEP,), in_specs=[FLAT, FL...  2.82 us
  transfers between devices with their start and end apart: 8, of which 5 were waited for; matrix products, arithmetic and copies ran while one was open for 7% of the time, Pallas kernels for 10%

profile of v6, /device:TPU:0, one launch (start us, length us, event | category | flops | bytes accessed | tf_op | source)
XLA Modules:
  0.0 132.3 jit_solution(4546157675076186209)
XLA Ops:
  0.0 2.8 %shard_map.55 = bf16[2,16,2,128,128]{4,3,2,1,0:T(8,128)(2,1)} custom-call(bf16[128,4096]{1,0:T(8,128)(2,1)} %k_ref.1, bf16[128,4096]{1,0:T(8,128)(2,1)} %v_ref.1), custom_call_target="tpu_custom_call" | custom-call | tf_op jit(solution)/shard_map/pallas_call | solution.py:44
  2.8 10.8 %all-to-all-start = ((bf16[32,2,128,128]{3,2,1,0:T(8,128)(2,1)}), bf16[32,2,128,128]{3,2,1,0:T(8,128)(2,1)S(1)}, u32[]{:S(2)}, u32[]{:S(2)}) async-start(bf16[32,2,128,128]{3,2,1,0:T(8,128)(2,1)} %bitcast.9), calls=%async_computation | async-start | bytes 4194304 | tf_op jit(solution)/shard_map/all_to_all | solution.py:273
  13.9 2.1 %shard_map.56 = bf16[2,16,128,128]{3,2,1,0:T(8,128)(2,1)} custom-call(bf16[128,4096]{1,0:T(8,128)(2,1)} %q_ref.1), custom_call_target="tpu_custom_call" | custom-call | tf_op jit(solution)/shard_map/pallas_call | solution.py:54
  16.4 0.2 convert_reduce_fusion.4
  16.6 0.2 convert_reduce_fusion.5
  16.9 0.6 slice.32
  17.5 0.6 convert_reduce_fusion
  18.1 1.7 %select_reduce_fusion = (s32[32,48]{1,0:T(8,128)S(1)}, s32[32,48]{1,0:T(8,128)S(1)}) fusion(s32[32,48]{1,0:T(8,128)S(1)} %get-tuple-element.43, s32[32,48]{1,0:T(8,128)S(1)} %get-tuple-element.41, pred[32,48]{1,0:T(8,128)(4,1)S(1)} %get-tuple-element.48, s32[32,48]{1,0:T(8,128)S(1)} %add_select_fusion.5, pred[32,48]{1,0:T(8,128)(4,1)S(1)} %get-tuple-element.52, ...), kind=kLoop, calls=%fused_computation | loop fusion | flops 586752 | bytes 39936 | tf_op jit(solution)/shard_map/reduce_sum | solution.py:248
  20.1 0.6 slice.33
  20.9 0.7 pad_add_fusion.1.chunks
  21.8 0.7 pad_add_fusion.2.chunks
  22.5 20.5 %all-to-all-done.rest_0_ = bf16[32,2,128,128]{3,2,1,0:T(8,128)(2,1)S(1)} async-done(((bf16[32,2,128,128]{3,2,1,0:T(8,128)(2,1)}), bf16[32,2,128,128]{3,2,1,0:T(8,128)(2,1)S(1)}, u32[]{:S(2)}, u32[]{:S(2)}) %all-to-all-start) | async-done | bytes 2097184 | tf_op jit(solution)/shard_map/all_to_all | solution.py:273
  43.0 1.0 slice.34
  44.1 1.2 slice.35
  45.3 2.0 %collective-permute-start.4 = (bf16[20,2,128,128]{3,2,1,0:T(8,128)(2,1)}, bf16[20,2,128,128]{3,2,1,0:T(8,128)(2,1)}, u32[]{:S(2)}, u32[]{:S(2)}) collective-permute-start(bf16[20,2,128,128]{3,2,1,0:T(8,128)(2,1)} %slice.35), channel_id=1, source_target_pairs={{0,1},{1,0},{2,3},{3,2},{4,5},{5,4},{6,7},{7,6},{8,9},{9,8},{10,11... | collective-permute-start | bytes 3932168 | tf_op jit(solution)/shard_map/ppermute | solution.py:277
  47.3 6.4 %all-to-all-start.1 = ((bf16[32,128,128]{2,1,0:T(8,128)(2,1)}), bf16[32,128,128]{2,1,0:T(8,128)(2,1)S(1)}, u32[]{:S(2)}, u32[]{:S(2)}) async-start(bf16[32,128,128]{2,1,0:T(8,128)(2,1)} %bitcast.10), calls=%async_computation.1 | async-start | bytes 2097152 | tf_op jit(solution)/shard_map/all_to_all | solution.py:273
  53.7 11.0 %collective-permute-done.2.rest_2_ = bf16[12,2,128,128]{3,2,1,0:T(8,128)(2,1)} collective-permute-done((bf16[12,2,128,128]{3,2,1,0:T(8,128)(2,1)}, bf16[12,2,128,128]{3,2,1,0:T(8,128)(2,1)}, u32[]{:S(2)}, u32[]{:S(2)}) %collective-permute-start.2) | collective-permute-done | bytes 786464 | tf_op jit(solution)/shard_map/ppermute | solution.py:277
  64.7 6.6 %all-to-all-done.1.q_hbm = bf16[32,128,128]{2,1,0:T(8,128)(2,1)S(1)} async-done(((bf16[32,128,128]{2,1,0:T(8,128)(2,1)}), bf16[32,128,128]{2,1,0:T(8,128)(2,1)S(1)}, u32[]{:S(2)}, u32[]{:S(2)}) %all-to-all-start.1) | async-done | bytes 1048608 | tf_op jit(solution)/shard_map/all_to_all | solution.py:273
  71.4 11.1 %shard_map.57 = (f32[33,128,128]{2,1,0:T(8,128)S(1)}, f32[33,1,128]{2,1,0:T(1,128)S(1)}, f32[33,8,128]{2,1,0:T(8,128)S(1)}) custom-call(s32[197]{0:T(256)S(1)} %pad_add_fusion.1.chunks, s32[1584]{0:T(1024)S(1)} %reshape.119.lists, s32[33]{0:T(128)S(1)} %pad.15.counts, bf16[32,128,128]{2,1,0:T(8,128)(2,1)S(1)} %all-to-all-done.1.q_hbm, ...), custom_call_target="tpu_custom_call" | custom-call | flops 1000000 | bytes 1 | tf_op jit(solution)/shard_map/pallas_call | solution.py:225
  82.5 10.0 %collective-permute-done.4.rest_0_ = bf16[20,2,128,128]{3,2,1,0:T(8,128)(2,1)} collective-permute-done((bf16[20,2,128,128]{3,2,1,0:T(8,128)(2,1)}, bf16[20,2,128,128]{3,2,1,0:T(8,128)(2,1)}, u32[]{:S(2)}, u32[]{:S(2)}) %collective-permute-start.4) | collective-permute-done | bytes 1310752 | tf_op jit(solution)/shard_map/ppermute | solution.py:277
  92.4 3.2 %collective-permute-done.5.rest_1_ = bf16[20,2,128,128]{3,2,1,0:T(8,128)(2,1)S(1)} collective-permute-done((bf16[20,2,128,128]{3,2,1,0:T(8,128)(2,1)}, bf16[20,2,128,128]{3,2,1,0:T(8,128)(2,1)S(1)}, u32[]{:S(2)}, u32[]{:S(2)}) %collective-permute-start.5) | collective-permute-done | bytes 1310752 | tf_op jit(solution)/shard_map/ppermute | solution.py:276
  95.7 7.8 %shard_map.58 = bf16[32,128,128]{2,1,0:T(8,128)(2,1)S(1)} custom-call(s32[197]{0:T(256)S(1)} %pad_add_fusion.2.chunks, s32[1584]{0:T(1024)S(1)} %reshape.120.lists, s32[33]{0:T(128)S(1)} %pad.17.counts, bf16[32,128,128]{2,1,0:T(8,128)(2,1)S(1)} %all-to-all-done.1.q_hbm, bf16[20,2,128,128]{3,2,1,0:T(8,128)(2,1)} %collective-permute-done.4.rest_0_, ...), custom_call_target="tpu_custom_call" | custom-call | flops 1000000 | bytes 1 | tf_op jit(solution)/shard_map/pallas_call | solution.py:225
  103.5 26.7 %all_to_all.15 = bf16[32,128,128]{2,1,0:T(8,128)(2,1)} all-to-all(bf16[32,128,128]{2,1,0:T(8,128)(2,1)S(1)} %shard_map.58), channel_id=1, replica_groups={{0,8,16,24,32,40,48,56,64,72,80,88,96,104,112,120,3,11,19,27,35,43,51,5..., dimensions={0} | all-to-all | bytes 2097152 | tf_op jit(solution)/shard_map/all_to_all | solution.py:273
  130.2 2.1 %shard_map.59 = bf16[128,4096]{1,0:T(8,128)(2,1)} custom-call(bf16[2,16,128,128]{3,2,1,0:T(8,128)(2,1)} %bitcast.11), custom_call_target="tpu_custom_call" | custom-call | tf_op jit(solution)/shard_map/pallas_call | solution.py:64
  (37 shorter events, 1.3 us)
Async XLA Ops:
  2.8 10.8 %copy-start = (s32[1,128,48]{1,2,0:T(8,128)S(1)}, s32[1,128,48]{1,2,0:T(8,128)}, u32[]{:S(2)}) copy-start(s32[1,128,48]{1,2,0:T(8,128)} %param.8) | copy-start | bytes 73732
  2.8 10.8 %copy-start.1 = (s32[1,128]{1,0:T(1,128)S(1)}, s32[1,128]{1,0:T(1,128)}, u32[]{:S(2)}) copy-start(s32[1,128]{1,0:T(1,128)} %param.9) | copy-start | bytes 1540
  2.8 40.2 %all-to-all-start = ((bf16[32,2,128,128]{3,2,1,0:T(8,128)(2,1)}), bf16[32,2,128,128]{3,2,1,0:T(8,128)(2,1)S(1)}, u32[]{:S(2)}, u32[]{:S(2)}) async-start(bf16[32,2,128,128]{3,2,1,0:T(8,128)(2,1)} %bitcast.9), calls=%async_computation | async-start | bytes 4194304 | tf_op jit(solution)/shard_map/all_to_all | solution.py:273
  13.8 2.2 %collective-permute-start = (s32[128,49]{1,0:T(8,128)S(1)}, s32[128,49]{1,0:T(8,128)S(1)}, u32[]{:S(2)}, u32[]{:S(2)}) collective-permute-start(s32[128,49]{1,0:T(8,128)S(1)} %copy.17), channel_id=1, source_target_pairs={{0,4},{4,0},{8,12},{12,8},{16,20},{20,16},{24,28},{28,24},{32,36},... | collective-permute-start | bytes 75272 | tf_op jit(solution)/shard_map/ppermute | solution.py:276
  43.0 28.3 %collective-permute-start.1 = (bf16[32,2,128,128]{3,2,1,0:T(8,128)(2,1)S(1)}, bf16[32,2,128,128]{3,2,1,0:T(8,128)(2,1)}, u32[]{:S(2)}, u32[]{:S(2)}) collective-permute-start(bf16[32,2,128,128]{3,2,1,0:T(8,128)(2,1)S(1)} %all-to-all-done.rest_0_), channel_id=1, source_target_pairs={{0,4},{4,0},{8,12},{12,8},{16,20},{20,16},{24,28},{28,24},{32,36},... | collective-permute-start | bytes 6291464 | tf_op jit(solution)/shard_map/ppermute | solution.py:276
  44.1 20.7 %collective-permute-start.2 = (bf16[12,2,128,128]{3,2,1,0:T(8,128)(2,1)}, bf16[12,2,128,128]{3,2,1,0:T(8,128)(2,1)}, u32[]{:S(2)}, u32[]{:S(2)}) collective-permute-start(bf16[12,2,128,128]{3,2,1,0:T(8,128)(2,1)} %slice.34), channel_id=1, source_target_pairs={{0,1},{1,0},{2,3},{3,2},{4,5},{5,4},{6,7},{7,6},{8,9},{9,8},{10,11... | collective-permute-start | bytes 2359304 | tf_op jit(solution)/shard_map/ppermute | solution.py:277
  45.3 47.1 %collective-permute-start.4 = (bf16[20,2,128,128]{3,2,1,0:T(8,128)(2,1)}, bf16[20,2,128,128]{3,2,1,0:T(8,128)(2,1)}, u32[]{:S(2)}, u32[]{:S(2)}) collective-permute-start(bf16[20,2,128,128]{3,2,1,0:T(8,128)(2,1)} %slice.35), channel_id=1, source_target_pairs={{0,1},{1,0},{2,3},{3,2},{4,5},{5,4},{6,7},{7,6},{8,9},{9,8},{10,11... | collective-permute-start | bytes 3932168 | tf_op jit(solution)/shard_map/ppermute | solution.py:277
  47.3 24.1 %all-to-all-start.1 = ((bf16[32,128,128]{2,1,0:T(8,128)(2,1)}), bf16[32,128,128]{2,1,0:T(8,128)(2,1)S(1)}, u32[]{:S(2)}, u32[]{:S(2)}) async-start(bf16[32,128,128]{2,1,0:T(8,128)(2,1)} %bitcast.10), calls=%async_computation.1 | async-start | bytes 2097152 | tf_op jit(solution)/shard_map/all_to_all | solution.py:273
  64.7 6.6 %collective-permute-start.3 = (bf16[12,2,128,128]{3,2,1,0:T(8,128)(2,1)}, bf16[12,2,128,128]{3,2,1,0:T(8,128)(2,1)}, u32[]{:S(2)}, u32[]{:S(2)}) collective-permute-start(bf16[12,2,128,128]{3,2,1,0:T(8,128)(2,1)} %collective-permute-done.2.rest_2_), channel_id=1, source_target_pairs={{0,4},{4,0},{8,12},{12,8},{16,20},{20,16},{24,28},{28,24},{32,36},... | collective-permute-start | bytes 2359304 | tf_op jit(solution)/shard_map/ppermute | solution.py:276
  92.4 3.2 %collective-permute-start.5 = (bf16[20,2,128,128]{3,2,1,0:T(8,128)(2,1)}, bf16[20,2,128,128]{3,2,1,0:T(8,128)(2,1)S(1)}, u32[]{:S(2)}, u32[]{:S(2)}) collective-permute-start(bf16[20,2,128,128]{3,2,1,0:T(8,128)(2,1)} %collective-permute-done.4.rest_0_), channel_id=1, source_target_pairs={{0,4},{4,0},{8,12},{12,8},{16,20},{20,16},{24,28},{28,24},{32,36},... | collective-permute-start | bytes 3932168 | tf_op jit(solution)/shard_map/ppermute | solution.py:276

commit v7 on v6

--- a/solution.py
+++ b/solution.py
@@ -11,9 +11,9 @@
 HDIM = 128
 LOG2E = 1.4426950408889634
 FACTOR = LOG2E / HDIM**0.5
-CUT = 12
-GROUP = 8
-UNROLLS = (16, 4, 2)
+CUT = 14
+GROUP = 4
+UNROLLS = (32, 8, 2)
 PLACES = 16
 VMEM = 24 << 20
 
@@ -71,7 +71,7 @@
 
 
 def attention_kernel(
-    first, last, parts, chunks, lists, counts, q_hbm, *rest
+    first, last, parts, chunks, lists, counts, q_ref, *rest
 ):
     rest = list(rest)
     kv_hbm = [rest.pop(0) for _ in range(parts)]
@@ -79,21 +79,19 @@
         acc_in, top_in, total_in = (rest.pop(0) for _ in range(3))
     if last:
         o_ref = rest.pop(0)
-        acc_ref, top_ref, total_ref = rest[6:9]
+        acc_ref, top_ref, total_ref = rest[5:8]
     else:
         acc_ref, top_ref, total_ref = (rest.pop(0) for _ in range(3))
-    s0, s1, p0, p1, q_ref, kv_ref = rest[:6]
+    s0, s1, p0, p1, kv_ref = rest[:5]
     sems = rest[-1]
-    nq = q_hbm.shape[0]
+    nq = q_ref.shape[0]
     most = lists.shape[0] // (nq + 1)
 
-    copies = [(q_hbm, q_ref)]
+    copies = []
     at = 0
     for part in kv_hbm:
         copies.append((part, kv_ref.at[pl.ds(at, part.shape[0])]))
         at += part.shape[0]
-    if not first:
-        copies += [(acc_in, acc_ref), (top_in, top_ref), (total_in, total_ref)]
     copies = [
         pltpu.make_async_copy(src, dst, sems.at[i]) for i, (src, dst) in enumerate(copies)
     ]
@@ -103,12 +101,16 @@
         acc_ref[...] = jnp.zeros_like(acc_ref)
         top_ref[...] = jnp.full_like(top_ref, -jnp.inf)
         total_ref[...] = jnp.zeros_like(total_ref)
+    else:
+        acc_ref[...] = acc_in[...]
+        top_ref[...] = top_in[...]
+        total_ref[...] = total_in[...]
     for copy in copies:
         copy.wait()
 
     def where(t):
         code = chunks[t + 1]
-        return code // 8, code % 8
+        return code // 16, code % 16
 
     def places(b, c):
         end = jnp.maximum(counts[b] - 1, 0)
@@ -204,30 +206,29 @@
     first = state is None
     hbm = pl.BlockSpec(memory_space=pl.ANY)
     shapes = [(nq + 1, HDIM, BLOCK), (nq + 1, 1, BLOCK), (nq + 1, 8, BLOCK)]
-    whole = lambda s: pl.BlockSpec(s, lambda i, *_: (0, 0, 0))
+    vmem = pl.BlockSpec(memory_space=pltpu.VMEM)
     scratch = [
         pltpu.VMEM((GROUP * BLOCK, BLOCK), jnp.float32),
         pltpu.VMEM((GROUP * BLOCK, BLOCK), jnp.float32),
         pltpu.VMEM((GROUP * BLOCK, BLOCK), jnp.bfloat16),
         pltpu.VMEM((GROUP * BLOCK, BLOCK), jnp.bfloat16),
-        pltpu.VMEM(q.shape, q.dtype),
         pltpu.VMEM((sum(a.shape[0] for a in kv),) + kv[0].shape[1:], kv[0].dtype),
     ]
     if last:
         scratch += [pltpu.VMEM(s, jnp.float32) for s in shapes]
         out_shape = jax.ShapeDtypeStruct(q.shape, jnp.bfloat16)
-        out_specs = whole(q.shape)
+        out_specs = vmem
     else:
         out_shape = [jax.ShapeDtypeStruct(s, jnp.float32) for s in shapes]
-        out_specs = [whole(s) for s in shapes]
-    scratch += [pltpu.SemaphoreType.DMA((8,))]
+        out_specs = [vmem for s in shapes]
+    scratch += [pltpu.SemaphoreType.DMA((len(kv),))]
     args = [q, *kv] + ([] if first else list(state))
     return pl.pallas_call(
         functools.partial(attention_kernel, first, last, len(kv)),
         grid_spec=pltpu.PrefetchScalarGridSpec(
             num_scalar_prefetch=3,
             grid=(1,),
-            in_specs=[hbm] * len(args),
+            in_specs=[vmem] + [hbm] * len(kv) + [vmem] * (len(args) - 1 - len(kv)),
             out_specs=out_specs,
             scratch_shapes=scratch,
         ),
@@ -254,7 +255,7 @@
     b = jnp.sum((t[:, None] >= ends[None, :]).astype(jnp.int32), axis=1)
     start = jnp.sum(jnp.where(row[None, :] < b[:, None], steps[None, :], 0), axis=1)
     c = jnp.where(b < nq, t - start, 0)
-    chunks = jnp.concatenate([ends[-1:], b * 8 + c])
+    chunks = jnp.concatenate([ends[-1:], b * 16 + c])
     lists = jnp.pad(lists, ((0, 1), (0, 0))).reshape(-1)
     return chunks, lists, jnp.pad(counts, (0, 1))
 
@@ -310,7 +311,9 @@
             late_tables,
         )
     )
-    far, far_late = to_pair(kv[:CUT]), to_pair(kv[CUT:])
+    far, far_late = kv[:CUT], kv[CUT:]
+    kv, far_late = lax.optimization_barrier((kv, far_late))
+    far, far_late = to_pair(far), to_pair(far_late)
     q = swap(q.reshape(2 * PLACES, BLOCK, HDIM))
     state = attention(early_tables, q, [kv, to_core(kv), far, to_core(far)], None, False)
     state, far_late = lax.optimization_barrier((state, far_late))

time: 132 us -> 131 us (level)
  Pallas kernels: 26 us -> 35.3 us
  waiting for transfers between devices: 51.4 us -> 45.2 us
  blocking collectives: 26.7 us -> 22.3 us
    pallas_call x2, Pallas kernels: 18.9 us -> 28.2 us  [attention(): pl.pallas_call(functools.partial(attention_kernel, first, last, len(kv)),...]
    all_to_all x1, blocking collectives: 26.7 us -> 22.3 us  [local(): lax.all_to_all(a, ('seq', 'head'), 0, 0, axis_index_groups=groups, tiled=...]
    all_to_all x2, waiting for transfers between devices: 27.2 us -> 23.1 us  [local(): lax.all_to_all(a, ('seq', 'head'), 0, 0, axis_index_groups=groups, tiled=...]
    ppermute x2, waiting for transfers between devices: 21 us -> 18.8 us  [local(): lax.ppermute(a, 'head', [(i, i ^ 1) for i in range(head_count)])]
  transfers between devices with their start and end apart: 8 -> 8, of which waited for: 5 -> 6; matrix products, arithmetic and copies ran while one was open for 7% -> 6% of each run, Pallas kernels for 10% -> 16%
where the time goes in v7:
time: 131 us
  waiting for transfers between devices  45.2 us (35%)
  Pallas kernels  35.3 us (27%)
  blocking collectives  22.3 us (17%)
  starting transfers between devices  19.3 us (15%)
  other arithmetic  4.76 us (4%)
  local copies, waits for them, and re-layouts  3.97 us (3%)
    pallas_call x2, Pallas kernels, attention(): pl.pallas_call(functools.partial(attention_kernel, first, last, len(kv)),...  28.2 us
    all_to_all x2, waiting for transfers between devices, local(): lax.all_to_all(a, ('seq', 'head'), 0, 0, axis_index_groups=groups, tiled=...  23.1 us
    all_to_all x1, blocking collectives, local(): lax.all_to_all(a, ('seq', 'head'), 0, 0, axis_index_groups=groups, tiled=...  22.3 us
    ppermute x2, waiting for transfers between devices, local(): lax.ppermute(a, 'head', [(i, i ^ 1) for i in range(head_count)])  18.8 us
    all_to_all x2, starting transfers between devices, local(): lax.all_to_all(a, ('seq', 'head'), 0, 0, axis_index_groups=groups, tiled=...  17.2 us
    ppermute x4, waiting for transfers between devices, local(): lax.ppermute(a, 'seq', [(i, i ^ 1) for i in range(seq_count)])  3.26 us
    pallas_call x1, Pallas kernels, pack_kv(): pl.pallas_call(pack_kv_kernel, grid=(PLACES // STEP,), in_specs=[FLAT, FL...  2.82 us
  transfers between devices with their start and end apart: 8, of which 6 were waited for; matrix products, arithmetic and copies ran while one was open for 6% of the time, Pallas kernels for 16%

profile of v7, /device:TPU:0, one launch (start us, length us, event | category | flops | bytes accessed | tf_op | source)
XLA Modules:
  0.0 131.0 jit_solution(1623277538273191782)
XLA Ops:
  0.0 2.8 %shard_map.55 = bf16[2,16,2,128,128]{4,3,2,1,0:T(8,128)(2,1)} custom-call(bf16[128,4096]{1,0:T(8,128)(2,1)} %k_ref.1, bf16[128,4096]{1,0:T(8,128)(2,1)} %v_ref.1), custom_call_target="tpu_custom_call" | custom-call | tf_op jit(solution)/shard_map/pallas_call | solution.py:44
  2.8 10.8 %all-to-all-start = ((bf16[32,2,128,128]{3,2,1,0:T(8,128)(2,1)}), bf16[32,2,128,128]{3,2,1,0:T(8,128)(2,1)S(1)}, u32[]{:S(2)}, u32[]{:S(2)}) async-start(bf16[32,2,128,128]{3,2,1,0:T(8,128)(2,1)} %bitcast.9), calls=%async_computation | async-start | bytes 4194304 | tf_op jit(solution)/shard_map/all_to_all | solution.py:274
  13.9 2.1 %shard_map.56 = bf16[2,16,128,128]{3,2,1,0:T(8,128)(2,1)} custom-call(bf16[128,4096]{1,0:T(8,128)(2,1)} %q_ref.1), custom_call_target="tpu_custom_call" | custom-call | tf_op jit(solution)/shard_map/pallas_call | solution.py:54
  16.4 0.2 convert_reduce_fusion.4
  16.9 0.6 slice.33
  17.6 0.6 slice.32
  18.2 0.6 convert_reduce_fusion
  18.8 1.7 %select_reduce_fusion = (s32[32,48]{1,0:T(8,128)S(1)}, s32[32,48]{1,0:T(8,128)S(1)}) fusion(s32[32,48]{1,0:T(8,128)S(1)} %get-tuple-element.47, s32[32,48]{1,0:T(8,128)S(1)} %get-tuple-element.45, pred[32,48]{1,0:T(8,128)(4,1)S(1)} %get-tuple-element.52, s32[32,48]{1,0:T(8,128)S(1)} %add_select_fusion.5, pred[32,48]{1,0:T(8,128)(4,1)S(1)} %get-tuple-element.56, ...), kind=kLoop, calls=%fused_computation | loop fusion | flops 586752 | bytes 39936 | tf_op jit(solution)/shard_map/reduce_sum | solution.py:249
  20.9 0.7 pad_add_fusion.2.chunks
  21.8 0.7 pad_add_fusion.1.chunks
  22.5 20.5 %all-to-all-done.rest_0_ = bf16[32,2,128,128]{3,2,1,0:T(8,128)(2,1)S(1)} async-done(((bf16[32,2,128,128]{3,2,1,0:T(8,128)(2,1)}), bf16[32,2,128,128]{3,2,1,0:T(8,128)(2,1)S(1)}, u32[]{:S(2)}, u32[]{:S(2)}) %all-to-all-start) | async-done | bytes 2097184 | tf_op jit(solution)/shard_map/all_to_all | solution.py:274
  43.0 1.2 slice.34
  44.2 1.1 slice.35
  45.3 2.0 %collective-permute-start.4 = (bf16[18,2,128,128]{3,2,1,0:T(8,128)(2,1)}, bf16[18,2,128,128]{3,2,1,0:T(8,128)(2,1)}, u32[]{:S(2)}, u32[]{:S(2)}) collective-permute-start(bf16[18,2,128,128]{3,2,1,0:T(8,128)(2,1)} %slice.34), channel_id=1, source_target_pairs={{0,1},{1,0},{2,3},{3,2},{4,5},{5,4},{6,7},{7,6},{8,9},{9,8},{10,11... | collective-permute-start | bytes 3538952 | tf_op jit(solution)/shard_map/ppermute | solution.py:278
  47.3 6.4 %all-to-all-start.1 = ((bf16[32,128,128]{2,1,0:T(8,128)(2,1)}), bf16[32,128,128]{2,1,0:T(8,128)(2,1)S(1)}, u32[]{:S(2)}, u32[]{:S(2)}) async-start(bf16[32,128,128]{2,1,0:T(8,128)(2,1)} %bitcast.10), calls=%async_computation.1 | async-start | bytes 2097152 | tf_op jit(solution)/shard_map/all_to_all | solution.py:274
  53.7 15.1 %collective-permute-done.2.rest_2_ = bf16[14,2,128,128]{3,2,1,0:T(8,128)(2,1)} collective-permute-done((bf16[14,2,128,128]{3,2,1,0:T(8,128)(2,1)}, bf16[14,2,128,128]{3,2,1,0:T(8,128)(2,1)}, u32[]{:S(2)}, u32[]{:S(2)}) %collective-permute-start.2) | collective-permute-done | bytes 917536 | tf_op jit(solution)/shard_map/ppermute | solution.py:278
  68.8 2.6 %all-to-all-done.1.q_ref = bf16[32,128,128]{2,1,0:T(8,128)(2,1)S(1)} async-done(((bf16[32,128,128]{2,1,0:T(8,128)(2,1)}), bf16[32,128,128]{2,1,0:T(8,128)(2,1)S(1)}, u32[]{:S(2)}, u32[]{:S(2)}) %all-to-all-start.1) | async-done | bytes 1048608 | tf_op jit(solution)/shard_map/all_to_all | solution.py:274
  71.4 0.2 collective-permute-done.3.rest_3_
  71.6 18.3 %shard_map.57 = (f32[33,128,128]{2,1,0:T(8,128)S(1)}, f32[33,1,128]{2,1,0:T(1,128)S(1)}, f32[33,8,128]{2,1,0:T(8,128)S(1)}) custom-call(s32[389]{0:T(512)S(1)} %pad_add_fusion.1.chunks, s32[1584]{0:T(1024)S(1)} %reshape.119.lists, s32[33]{0:T(128)S(1)} %pad.15.counts, bf16[32,128,128]{2,1,0:T(8,128)(2,1)S(1)} %all-to-all-done.1.q_ref, ...), custom_call_target="tpu_custom_call" | custom-call | flops 1000000 | bytes 1 | tf_op jit(solution)/shard_map/pallas_call | solution.py:226
  89.9 3.8 %collective-permute-done.4.rest_0_ = bf16[18,2,128,128]{3,2,1,0:T(8,128)(2,1)} collective-permute-done((bf16[18,2,128,128]{3,2,1,0:T(8,128)(2,1)}, bf16[18,2,128,128]{3,2,1,0:T(8,128)(2,1)}, u32[]{:S(2)}, u32[]{:S(2)}) %collective-permute-start.4) | collective-permute-done | bytes 1179680 | tf_op jit(solution)/shard_map/ppermute | solution.py:278
  93.7 3.1 %collective-permute-done.5.rest_1_ = bf16[18,2,128,128]{3,2,1,0:T(8,128)(2,1)S(1)} collective-permute-done((bf16[18,2,128,128]{3,2,1,0:T(8,128)(2,1)}, bf16[18,2,128,128]{3,2,1,0:T(8,128)(2,1)S(1)}, u32[]{:S(2)}, u32[]{:S(2)}) %collective-permute-start.5) | collective-permute-done | bytes 1179680 | tf_op jit(solution)/shard_map/ppermute | solution.py:277
  96.7 9.9 %shard_map.58 = bf16[32,128,128]{2,1,0:T(8,128)(2,1)S(1)} custom-call(s32[389]{0:T(512)S(1)} %pad_add_fusion.2.chunks, s32[1584]{0:T(1024)S(1)} %reshape.120.lists, s32[33]{0:T(128)S(1)} %pad.17.counts, bf16[32,128,128]{2,1,0:T(8,128)(2,1)S(1)} %all-to-all-done.1.q_ref, bf16[18,2,128,128]{3,2,1,0:T(8,128)(2,1)} %collective-permute-done.4.rest_0_, ...), custom_call_target="tpu_custom_call" | custom-call | flops 1000000 | bytes 1 | tf_op jit(solution)/shard_map/pallas_call | solution.py:226
  106.6 22.3 %all_to_all.15 = bf16[32,128,128]{2,1,0:T(8,128)(2,1)} all-to-all(bf16[32,128,128]{2,1,0:T(8,128)(2,1)S(1)} %shard_map.58), channel_id=1, replica_groups={{0,8,16,24,32,40,48,56,64,72,80,88,96,104,112,120,3,11,19,27,35,43,51,5..., dimensions={0} | all-to-all | bytes 2097152 | tf_op jit(solution)/shard_map/all_to_all | solution.py:274
  128.9 2.1 %shard_map.59 = bf16[128,4096]{1,0:T(8,128)(2,1)} custom-call(bf16[2,16,128,128]{3,2,1,0:T(8,128)(2,1)} %bitcast.11), custom_call_target="tpu_custom_call" | custom-call | tf_op jit(solution)/shard_map/pallas_call | solution.py:64
  (37 shorter events, 1.5 us)
Async XLA Ops:
  2.8 10.8 %copy-start = (s32[1,128,48]{1,2,0:T(8,128)S(1)}, s32[1,128,48]{1,2,0:T(8,128)}, u32[]{:S(2)}) copy-start(s32[1,128,48]{1,2,0:T(8,128)} %param.8) | copy-start | bytes 73732
  2.8 10.8 %copy-start.1 = (s32[1,128]{1,0:T(1,128)S(1)}, s32[1,128]{1,0:T(1,128)}, u32[]{:S(2)}) copy-start(s32[1,128]{1,0:T(1,128)} %param.9) | copy-start | bytes 1540
  2.8 40.2 %all-to-all-start = ((bf16[32,2,128,128]{3,2,1,0:T(8,128)(2,1)}), bf16[32,2,128,128]{3,2,1,0:T(8,128)(2,1)S(1)}, u32[]{:S(2)}, u32[]{:S(2)}) async-start(bf16[32,2,128,128]{3,2,1,0:T(8,128)(2,1)} %bitcast.9), calls=%async_computation | async-start | bytes 4194304 | tf_op jit(solution)/shard_map/all_to_all | solution.py:274
  13.8 2.2 %collective-permute-start = (s32[128,49]{1,0:T(8,128)S(1)}, s32[128,49]{1,0:T(8,128)S(1)}, u32[]{:S(2)}, u32[]{:S(2)}) collective-permute-start(s32[128,49]{1,0:T(8,128)S(1)} %copy.17), channel_id=1, source_target_pairs={{0,4},{4,0},{8,12},{12,8},{16,20},{20,16},{24,28},{28,24},{32,36},... | collective-permute-start | bytes 75272 | tf_op jit(solution)/shard_map/ppermute | solution.py:277
  44.2 27.4 %collective-permute-start.1 = (bf16[32,2,128,128]{3,2,1,0:T(8,128)(2,1)S(1)}, bf16[32,2,128,128]{3,2,1,0:T(8,128)(2,1)}, u32[]{:S(2)}, u32[]{:S(2)}) collective-permute-start(bf16[32,2,128,128]{3,2,1,0:T(8,128)(2,1)S(1)} %all-to-all-done.rest_0_), channel_id=1, source_target_pairs={{0,4},{4,0},{8,12},{12,8},{16,20},{20,16},{24,28},{28,24},{32,36},... | collective-permute-start | bytes 6291464 | tf_op jit(solution)/shard_map/ppermute | solution.py:277
  45.3 23.5 %collective-permute-start.2 = (bf16[14,2,128,128]{3,2,1,0:T(8,128)(2,1)}, bf16[14,2,128,128]{3,2,1,0:T(8,128)(2,1)}, u32[]{:S(2)}, u32[]{:S(2)}) collective-permute-start(bf16[14,2,128,128]{3,2,1,0:T(8,128)(2,1)} %slice.35), channel_id=1, source_target_pairs={{0,1},{1,0},{2,3},{3,2},{4,5},{5,4},{6,7},{7,6},{8,9},{9,8},{10,11... | collective-permute-start | bytes 2752520 | tf_op jit(solution)/shard_map/ppermute | solution.py:278
  45.3 48.4 %collective-permute-start.4 = (bf16[18,2,128,128]{3,2,1,0:T(8,128)(2,1)}, bf16[18,2,128,128]{3,2,1,0:T(8,128)(2,1)}, u32[]{:S(2)}, u32[]{:S(2)}) collective-permute-start(bf16[18,2,128,128]{3,2,1,0:T(8,128)(2,1)} %slice.34), channel_id=1, source_target_pairs={{0,1},{1,0},{2,3},{3,2},{4,5},{5,4},{6,7},{7,6},{8,9},{9,8},{10,11... | collective-permute-start | bytes 3538952 | tf_op jit(solution)/shard_map/ppermute | solution.py:278
  47.3 24.1 %all-to-all-start.1 = ((bf16[32,128,128]{2,1,0:T(8,128)(2,1)}), bf16[32,128,128]{2,1,0:T(8,128)(2,1)S(1)}, u32[]{:S(2)}, u32[]{:S(2)}) async-start(bf16[32,128,128]{2,1,0:T(8,128)(2,1)} %bitcast.10), calls=%async_computation.1 | async-start | bytes 2097152 | tf_op jit(solution)/shard_map/all_to_all | solution.py:274
  68.8 2.8 %collective-permute-start.3 = (bf16[14,2,128,128]{3,2,1,0:T(8,128)(2,1)}, bf16[14,2,128,128]{3,2,1,0:T(8,128)(2,1)}, u32[]{:S(2)}, u32[]{:S(2)}) collective-permute-start(bf16[14,2,128,128]{3,2,1,0:T(8,128)(2,1)} %collective-permute-done.2.rest_2_), channel_id=1, source_target_pairs={{0,4},{4,0},{8,12},{12,8},{16,20},{20,16},{24,28},{28,24},{32,36},... | collective-permute-start | bytes 2752520 | tf_op jit(solution)/shard_map/ppermute | solution.py:277
  93.6 3.1 %collective-permute-start.5 = (bf16[18,2,128,128]{3,2,1,0:T(8,128)(2,1)}, bf16[18,2,128,128]{3,2,1,0:T(8,128)(2,1)S(1)}, u32[]{:S(2)}, u32[]{:S(2)}) collective-permute-start(bf16[18,2,128,128]{3,2,1,0:T(8,128)(2,1)} %collective-permute-done.4.rest_0_), channel_id=1, source_target_pairs={{0,4},{4,0},{8,12},{12,8},{16,20},{20,16},{24,28},{28,24},{32,36},... | collective-permute-start | bytes 3538952 | tf_op jit(solution)/shard_map/ppermute | solution.py:277

commit v8 on v7

--- a/solution.py
+++ b/solution.py
@@ -11,7 +11,7 @@
 HDIM = 128
 LOG2E = 1.4426950408889634
 FACTOR = LOG2E / HDIM**0.5
-CUT = 14
+CUT = 16
 GROUP = 4
 UNROLLS = (32, 8, 2)
 PLACES = 16
@@ -235,7 +235,7 @@
         out_shape=out_shape,
         compiler_params=pltpu.CompilerParams(vmem_limit_bytes=VMEM),
         cost_estimate=pl.CostEstimate(
-            flops=1_000_000, bytes_accessed=1, transcendentals=0
+            flops=3_000_000_000, bytes_accessed=1, transcendentals=0
         ),
     )(chunks, lists, counts, *args)
 

time: 131 us -> 150 us (1.15)
  waiting for transfers between devices: 45.2 us -> 65.1 us
  Pallas kernels: 35.3 us -> 26.3 us
  blocking collectives: 22.3 us -> 30.8 us
    all_to_all x2, waiting for transfers between devices: 23.1 us -> 38.7 us  [local(): lax.all_to_all(a, ('seq', 'head'), 0, 0, axis_index_groups=groups, tiled=...]
    pallas_call x2, Pallas kernels: 28.2 us -> 19.2 us  [attention(): pl.pallas_call(functools.partial(attention_kernel, first, last, len(kv)),...]
    all_to_all x1, blocking collectives: 22.3 us -> 30.8 us  [local(): lax.all_to_all(a, ('seq', 'head'), 0, 0, axis_index_groups=groups, tiled=...]
    ppermute x2, waiting for transfers between devices: 18.8 us -> 23.9 us  [local(): lax.ppermute(a, 'head', [(i, i ^ 1) for i in range(head_count)])]
    ppermute x2, starting transfers between devices: 2.03 us -> 0.09 us  [local(): lax.ppermute(a, 'head', [(i, i ^ 1) for i in range(head_count)])]
  transfers between devices with their start and end apart: 8 -> 8, of which waited for: 6 -> 4; matrix products, arithmetic and copies ran while one was open for 6% -> 4% of each run, Pallas kernels for 16% -> 10%
where the time goes in v8:
time: 150 us; the launch traced here: 149 us
  waiting for transfers between devices  65.1 us (43%)
  blocking collectives  30.8 us (21%)
  Pallas kernels  26.3 us (18%)
  starting transfers between devices  18.6 us (12%)
  other arithmetic  4.76 us (3%)
  local copies, waits for them, and re-layouts  2.89 us (2%)
    all_to_all x2, waiting for transfers between devices, local(): lax.all_to_all(a, ('seq', 'head'), 0, 0, axis_index_groups=groups, tiled=...  38.7 us
    all_to_all x1, blocking collectives, local(): lax.all_to_all(a, ('seq', 'head'), 0, 0, axis_index_groups=groups, tiled=...  30.8 us
    ppermute x2, waiting for transfers between devices, local(): lax.ppermute(a, 'head', [(i, i ^ 1) for i in range(head_count)])  23.9 us
    pallas_call x2, Pallas kernels, attention(): pl.pallas_call(functools.partial(attention_kernel, first, last, len(kv)),...  19.2 us
    all_to_all x2, starting transfers between devices, local(): lax.all_to_all(a, ('seq', 'head'), 0, 0, axis_index_groups=groups, tiled=...  17.1 us
  transfers between devices with their start and end apart: 8, of which 4 were waited for; matrix products, arithmetic and copies ran while one was open for 4% of the time, Pallas kernels for 10%

profile of v8, /device:TPU:0, one launch (start us, length us, event | category | flops | bytes accessed | tf_op | source)
XLA Modules:
  0.0 148.6 jit_solution(5497248675264159337)
XLA Ops:
  0.0 2.8 %shard_map.55 = bf16[2,16,2,128,128]{4,3,2,1,0:T(8,128)(2,1)} custom-call(bf16[128,4096]{1,0:T(8,128)(2,1)} %k_ref.1, bf16[128,4096]{1,0:T(8,128)(2,1)} %v_ref.1), custom_call_target="tpu_custom_call" | custom-call | tf_op jit(solution)/shard_map/pallas_call | solution.py:44
  2.8 10.8 %all-to-all-start = ((bf16[32,2,128,128]{3,2,1,0:T(8,128)(2,1)}), bf16[32,2,128,128]{3,2,1,0:T(8,128)(2,1)S(1)}, u32[]{:S(2)}, u32[]{:S(2)}) async-start(bf16[32,2,128,128]{3,2,1,0:T(8,128)(2,1)} %bitcast.9), calls=%async_computation | async-start | bytes 4194304 | tf_op jit(solution)/shard_map/all_to_all | solution.py:274
  13.7 0.1 copy.17
  13.9 2.1 %shard_map.56 = bf16[2,16,128,128]{3,2,1,0:T(8,128)(2,1)} custom-call(bf16[128,4096]{1,0:T(8,128)(2,1)} %q_ref.1), custom_call_target="tpu_custom_call" | custom-call | tf_op jit(solution)/shard_map/pallas_call | solution.py:54
  16.2 0.2 slice_reduce_fusion
  16.4 0.2 convert_reduce_fusion.4
  16.6 0.2 convert_reduce_fusion.5
  16.9 0.6 slice.33
  17.6 0.6 slice.32
  18.2 0.6 convert_reduce_fusion
  18.8 1.7 %select_reduce_fusion = (s32[32,48]{1,0:T(8,128)S(1)}, s32[32,48]{1,0:T(8,128)S(1)}) fusion(s32[32,48]{1,0:T(8,128)S(1)} %get-tuple-element.47, s32[32,48]{1,0:T(8,128)S(1)} %get-tuple-element.45, pred[32,48]{1,0:T(8,128)(4,1)S(1)} %get-tuple-element.52, s32[32,48]{1,0:T(8,128)S(1)} %add_select_fusion.5, pred[32,48]{1,0:T(8,128)(4,1)S(1)} %get-tuple-element.56, ...), kind=kLoop, calls=%fused_computation | loop fusion | flops 586752 | bytes 39936 | tf_op jit(solution)/shard_map/reduce_sum | solution.py:249
  20.9 0.7 pad_add_fusion.2.chunks
  21.8 0.7 pad_add_fusion.1.chunks
  22.5 20.5 %all-to-all-done.rest_0_ = bf16[32,2,128,128]{3,2,1,0:T(8,128)(2,1)S(1)} async-done(((bf16[32,2,128,128]{3,2,1,0:T(8,128)(2,1)}), bf16[32,2,128,128]{3,2,1,0:T(8,128)(2,1)S(1)}, u32[]{:S(2)}, u32[]{:S(2)}) %all-to-all-start) | async-done | bytes 2097184 | tf_op jit(solution)/shard_map/all_to_all | solution.py:274
  43.0 1.2 fusion.17
  44.2 23.9 %collective-permute-done.2.rest_2_ = bf16[16,2,128,128]{3,2,1,0:T(8,128)(2,1)} collective-permute-done((bf16[16,2,128,128]{3,2,1,0:T(8,128)(2,1)S(1)}, bf16[16,2,128,128]{3,2,1,0:T(8,128)(2,1)}, u32[]{:S(2)}, u32[]{:S(2)}) %collective-permute-start.2) | collective-permute-done | bytes 1048608 | tf_op jit(solution)/shard_map/ppermute | solution.py:278
  68.1 6.2 %all-to-all-start.1 = ((bf16[32,128,128]{2,1,0:T(8,128)(2,1)}), bf16[32,128,128]{2,1,0:T(8,128)(2,1)S(1)}, u32[]{:S(2)}, u32[]{:S(2)}) async-start(bf16[32,128,128]{2,1,0:T(8,128)(2,1)} %bitcast.10), calls=%async_computation.1 | async-start | bytes 2097152 | tf_op jit(solution)/shard_map/all_to_all | solution.py:274
  74.5 18.2 %all-to-all-done.1.q_ref = bf16[32,128,128]{2,1,0:T(8,128)(2,1)S(1)} async-done(((bf16[32,128,128]{2,1,0:T(8,128)(2,1)}), bf16[32,128,128]{2,1,0:T(8,128)(2,1)S(1)}, u32[]{:S(2)}, u32[]{:S(2)}) %all-to-all-start.1) | async-done | bytes 1048608 | tf_op jit(solution)/shard_map/all_to_all | solution.py:274
  92.7 12.6 %shard_map.57 = (f32[33,128,128]{2,1,0:T(8,128)S(1)}, f32[33,1,128]{2,1,0:T(1,128)S(1)}, f32[33,8,128]{2,1,0:T(8,128)S(1)}) custom-call(s32[389]{0:T(512)S(1)} %pad_add_fusion.1.chunks, s32[1584]{0:T(1024)S(1)} %reshape.119.lists, s32[33]{0:T(128)S(1)} %pad.15.counts, bf16[32,128,128]{2,1,0:T(8,128)(2,1)S(1)} %all-to-all-done.1.q_ref, ...), custom_call_target="tpu_custom_call" | custom-call | flops 3000000000 | bytes 1 | tf_op jit(solution)/shard_map/pallas_call | solution.py:226
  105.2 1.3 collective-permute-start.5
  106.5 2.5 %collective-permute-done.5.rest_1_ = bf16[16,2,128,128]{3,2,1,0:T(8,128)(2,1)S(1)} collective-permute-done((bf16[16,2,128,128]{3,2,1,0:T(8,128)(2,1)}, bf16[16,2,128,128]{3,2,1,0:T(8,128)(2,1)S(1)}, u32[]{:S(2)}, u32[]{:S(2)}) %collective-permute-start.5) | collective-permute-done | bytes 1048608 | tf_op jit(solution)/shard_map/ppermute | solution.py:277
  109.0 6.7 %shard_map.58 = bf16[32,128,128]{2,1,0:T(8,128)(2,1)S(1)} custom-call(s32[389]{0:T(512)S(1)} %pad_add_fusion.2.chunks, s32[1584]{0:T(1024)S(1)} %reshape.120.lists, s32[33]{0:T(128)S(1)} %pad.17.counts, bf16[32,128,128]{2,1,0:T(8,128)(2,1)S(1)} %all-to-all-done.1.q_ref, bf16[16,2,128,128]{3,2,1,0:T(8,128)(2,1)} %collective-permute-done.4.rest_0_, ...), custom_call_target="tpu_custom_call" | custom-call | flops 3000000000 | bytes 1 | tf_op jit(solution)/shard_map/pallas_call | solution.py:226
  115.7 30.8 %all_to_all.15 = bf16[32,128,128]{2,1,0:T(8,128)(2,1)} all-to-all(bf16[32,128,128]{2,1,0:T(8,128)(2,1)S(1)} %shard_map.58), channel_id=1, replica_groups={{0,8,16,24,32,40,48,56,64,72,80,88,96,104,112,120,3,11,19,27,35,43,51,5..., dimensions={0} | all-to-all | bytes 2097152 | tf_op jit(solution)/shard_map/all_to_all | solution.py:274
  146.5 2.1 %shard_map.59 = bf16[128,4096]{1,0:T(8,128)(2,1)} custom-call(bf16[2,16,128,128]{3,2,1,0:T(8,128)(2,1)} %bitcast.11), custom_call_target="tpu_custom_call" | custom-call | tf_op jit(solution)/shard_map/pallas_call | solution.py:64
  (36 shorter events, 1.1 us)
Async XLA Ops:
  2.8 10.8 %copy-start = (s32[1,128,48]{1,2,0:T(8,128)S(1)}, s32[1,128,48]{1,2,0:T(8,128)}, u32[]{:S(2)}) copy-start(s32[1,128,48]{1,2,0:T(8,128)} %param.8) | copy-start | bytes 73732
  2.8 10.8 %copy-start.1 = (s32[1,128]{1,0:T(1,128)S(1)}, s32[1,128]{1,0:T(1,128)}, u32[]{:S(2)}) copy-start(s32[1,128]{1,0:T(1,128)} %param.9) | copy-start | bytes 1540
  2.8 40.2 %all-to-all-start = ((bf16[32,2,128,128]{3,2,1,0:T(8,128)(2,1)}), bf16[32,2,128,128]{3,2,1,0:T(8,128)(2,1)S(1)}, u32[]{:S(2)}, u32[]{:S(2)}) async-start(bf16[32,2,128,128]{3,2,1,0:T(8,128)(2,1)} %bitcast.9), calls=%async_computation | async-start | bytes 4194304 | tf_op jit(solution)/shard_map/all_to_all | solution.py:274
  13.8 2.2 %collective-permute-start = (s32[128,49]{1,0:T(8,128)S(1)}, s32[128,49]{1,0:T(8,128)S(1)}, u32[]{:S(2)}, u32[]{:S(2)}) collective-permute-start(s32[128,49]{1,0:T(8,128)S(1)} %copy.17), channel_id=1, source_target_pairs={{0,4},{4,0},{8,12},{12,8},{16,20},{20,16},{24,28},{28,24},{32,36},... | collective-permute-start | bytes 75272 | tf_op jit(solution)/shard_map/ppermute | solution.py:277
  44.2 23.9 %collective-permute-start.2 = (bf16[16,2,128,128]{3,2,1,0:T(8,128)(2,1)S(1)}, bf16[16,2,128,128]{3,2,1,0:T(8,128)(2,1)}, u32[]{:S(2)}, u32[]{:S(2)}) collective-permute-start(bf16[16,2,128,128]{3,2,1,0:T(8,128)(2,1)S(1)} %get-tuple-element.57), channel_id=1, source_target_pairs={{0,1},{1,0},{2,3},{3,2},{4,5},{5,4},{6,7},{7,6},{8,9},{9,8},{10,11... | collective-permute-start | bytes 3145736 | tf_op jit(solution)/shard_map/ppermute | solution.py:278
  44.2 48.4 %collective-permute-start.1 = (bf16[32,2,128,128]{3,2,1,0:T(8,128)(2,1)S(1)}, bf16[32,2,128,128]{3,2,1,0:T(8,128)(2,1)}, u32[]{:S(2)}, u32[]{:S(2)}) collective-permute-start(bf16[32,2,128,128]{3,2,1,0:T(8,128)(2,1)S(1)} %all-to-all-done.rest_0_), channel_id=1, source_target_pairs={{0,4},{4,0},{8,12},{12,8},{16,20},{20,16},{24,28},{28,24},{32,36},... | collective-permute-start | bytes 6291464 | tf_op jit(solution)/shard_map/ppermute | solution.py:277
  68.1 24.5 %collective-permute-start.3 = (bf16[16,2,128,128]{3,2,1,0:T(8,128)(2,1)}, bf16[16,2,128,128]{3,2,1,0:T(8,128)(2,1)}, u32[]{:S(2)}, u32[]{:S(2)}) collective-permute-start(bf16[16,2,128,128]{3,2,1,0:T(8,128)(2,1)} %collective-permute-done.2.rest_2_), channel_id=1, source_target_pairs={{0,4},{4,0},{8,12},{12,8},{16,20},{20,16},{24,28},{28,24},{32,36},... | collective-permute-start | bytes 3145736 | tf_op jit(solution)/shard_map/ppermute | solution.py:277
  68.1 24.5 %all-to-all-start.1 = ((bf16[32,128,128]{2,1,0:T(8,128)(2,1)}), bf16[32,128,128]{2,1,0:T(8,128)(2,1)S(1)}, u32[]{:S(2)}, u32[]{:S(2)}) async-start(bf16[32,128,128]{2,1,0:T(8,128)(2,1)} %bitcast.10), calls=%async_computation.1 | async-start | bytes 2097152 | tf_op jit(solution)/shard_map/all_to_all | solution.py:274
  74.4 30.8 %collective-permute-start.4 = (bf16[16,2,128,128]{3,2,1,0:T(8,128)(2,1)}, bf16[16,2,128,128]{3,2,1,0:T(8,128)(2,1)}, u32[]{:S(2)}, u32[]{:S(2)}) collective-permute-start(bf16[16,2,128,128]{3,2,1,0:T(8,128)(2,1)} %get-tuple-element.40), channel_id=1, source_target_pairs={{0,1},{1,0},{2,3},{3,2},{4,5},{5,4},{6,7},{7,6},{8,9},{9,8},{10,11... | collective-permute-start | bytes 3145736 | tf_op jit(solution)/shard_map/ppermute | solution.py:278
  105.2 3.8 %collective-permute-start.5 = (bf16[16,2,128,128]{3,2,1,0:T(8,128)(2,1)}, bf16[16,2,128,128]{3,2,1,0:T(8,128)(2,1)S(1)}, u32[]{:S(2)}, u32[]{:S(2)}) collective-permute-start(bf16[16,2,128,128]{3,2,1,0:T(8,128)(2,1)} %collective-permute-done.4.rest_0_), channel_id=1, source_target_pairs={{0,4},{4,0},{8,12},{12,8},{16,20},{20,16},{24,28},{28,24},{32,36},... | collective-permute-start | bytes 3145736 | tf_op jit(solution)/shard_map/ppermute | solution.py:277

commit v9 on v8

--- a/solution.py
+++ b/solution.py
@@ -11,7 +11,7 @@
 HDIM = 128
 LOG2E = 1.4426950408889634
 FACTOR = LOG2E / HDIM**0.5
-CUT = 16
+CUT = 15
 GROUP = 4
 UNROLLS = (32, 8, 2)
 PLACES = 16
@@ -235,7 +235,7 @@
         out_shape=out_shape,
         compiler_params=pltpu.CompilerParams(vmem_limit_bytes=VMEM),
         cost_estimate=pl.CostEstimate(
-            flops=3_000_000_000, bytes_accessed=1, transcendentals=0
+            flops=5_000_000_000, bytes_accessed=1, transcendentals=0
         ),
     )(chunks, lists, counts, *args)
 

time: 150 us -> 135 us (0.900)
  waiting for transfers between devices: 65.1 us -> 57.2 us
  blocking collectives: 30.8 us -> 25.8 us
    all_to_all x2, waiting for transfers between devices: 38.7 us -> 20.5 us  [local(): lax.all_to_all(a, ('seq', 'head'), 0, 0, axis_index_groups=groups, tiled=...]
    ppermute x2, waiting for transfers between devices: 23.9 us -> 31.1 us  [local(): lax.ppermute(a, 'head', [(i, i ^ 1) for i in range(head_count)])]
    all_to_all x1, blocking collectives: 30.8 us -> 25.8 us  [local(): lax.all_to_all(a, ('seq', 'head'), 0, 0, axis_index_groups=groups, tiled=...]
    ppermute x4, waiting for transfers between devices: 2.51 us -> 5.59 us  [local(): lax.ppermute(a, 'seq', [(i, i ^ 1) for i in range(seq_count)])]
  transfers between devices with their start and end apart: 8 -> 8, of which waited for: 4 -> 5; matrix products, arithmetic and copies ran while one was open for 4% -> 6% of each run, Pallas kernels for 10% -> 10%
where the time goes in v9:
time: 135 us
  waiting for transfers between devices  57.2 us (42%)
  blocking collectives  25.8 us (19%)
  Pallas kernels  25.1 us (19%)
  starting transfers between devices  17.6 us (13%)
  other arithmetic  4.76 us (4%)
  local copies, waits for them, and re-layouts  3.94 us (3%)
    ppermute x2, waiting for transfers between devices, local(): lax.ppermute(a, 'head', [(i, i ^ 1) for i in range(head_count)])  31.1 us
    all_to_all x1, blocking collectives, local(): lax.all_to_all(a, ('seq', 'head'), 0, 0, axis_index_groups=groups, tiled=...  25.8 us
    all_to_all x2, waiting for transfers between devices, local(): lax.all_to_all(a, ('seq', 'head'), 0, 0, axis_index_groups=groups, tiled=...  20.5 us
    pallas_call x2, Pallas kernels, attention(): pl.pallas_call(functools.partial(attention_kernel, first, last, len(kv)),...  18.1 us
    all_to_all x2, starting transfers between devices, local(): lax.all_to_all(a, ('seq', 'head'), 0, 0, axis_index_groups=groups, tiled=...  17.2 us
    ppermute x4, waiting for transfers between devices, local(): lax.ppermute(a, 'seq', [(i, i ^ 1) for i in range(seq_count)])  5.59 us
    pallas_call x1, Pallas kernels, pack_kv(): pl.pallas_call(pack_kv_kernel, grid=(PLACES // STEP,), in_specs=[FLAT, FL...  2.82 us
  transfers between devices with their start and end apart: 8, of which 5 were waited for; matrix products, arithmetic and copies ran while one was open for 6% of the time, Pallas kernels for 10%

profile of v9, /device:TPU:0, one launch (start us, length us, event | category | flops | bytes accessed | tf_op | source)
XLA Modules:
  0.0 134.6 jit_solution(4238067763891885041)
XLA Ops:
  0.0 2.8 %shard_map.55 = bf16[2,16,2,128,128]{4,3,2,1,0:T(8,128)(2,1)} custom-call(bf16[128,4096]{1,0:T(8,128)(2,1)} %k_ref.1, bf16[128,4096]{1,0:T(8,128)(2,1)} %v_ref.1), custom_call_target="tpu_custom_call" | custom-call | tf_op jit(solution)/shard_map/pallas_call | solution.py:44
  2.8 10.8 %all-to-all-start = ((bf16[32,2,128,128]{3,2,1,0:T(8,128)(2,1)}), bf16[32,2,128,128]{3,2,1,0:T(8,128)(2,1)S(1)}, u32[]{:S(2)}, u32[]{:S(2)}) async-start(bf16[32,2,128,128]{3,2,1,0:T(8,128)(2,1)} %bitcast.9), calls=%async_computation | async-start | bytes 4194304 | tf_op jit(solution)/shard_map/all_to_all | solution.py:274
  13.9 2.1 %shard_map.56 = bf16[2,16,128,128]{3,2,1,0:T(8,128)(2,1)} custom-call(bf16[128,4096]{1,0:T(8,128)(2,1)} %q_ref.1), custom_call_target="tpu_custom_call" | custom-call | tf_op jit(solution)/shard_map/pallas_call | solution.py:54
  16.4 0.2 convert_reduce_fusion.4
  16.6 0.2 convert_reduce_fusion.5
  16.9 0.6 slice.33
  17.6 0.6 slice.32
  18.2 0.6 convert_reduce_fusion
  18.8 1.7 %select_reduce_fusion = (s32[32,48]{1,0:T(8,128)S(1)}, s32[32,48]{1,0:T(8,128)S(1)}) fusion(s32[32,48]{1,0:T(8,128)S(1)} %get-tuple-element.47, s32[32,48]{1,0:T(8,128)S(1)} %get-tuple-element.45, pred[32,48]{1,0:T(8,128)(4,1)S(1)} %get-tuple-element.52, s32[32,48]{1,0:T(8,128)S(1)} %add_select_fusion.5, pred[32,48]{1,0:T(8,128)(4,1)S(1)} %get-tuple-element.56, ...), kind=kLoop, calls=%fused_computation | loop fusion | flops 586752 | bytes 39936 | tf_op jit(solution)/shard_map/reduce_sum | solution.py:249
  20.9 0.7 pad_add_fusion.2.chunks
  21.8 0.7 pad_add_fusion.1.chunks
  22.5 20.5 %all-to-all-done.rest_0_ = bf16[32,2,128,128]{3,2,1,0:T(8,128)(2,1)S(1)} async-done(((bf16[32,2,128,128]{3,2,1,0:T(8,128)(2,1)}), bf16[32,2,128,128]{3,2,1,0:T(8,128)(2,1)S(1)}, u32[]{:S(2)}, u32[]{:S(2)}) %all-to-all-start) | async-done | bytes 2097184 | tf_op jit(solution)/shard_map/all_to_all | solution.py:274
  43.0 1.1 slice.34
  44.2 1.1 slice.35
  45.3 6.4 %all-to-all-start.1 = ((bf16[32,128,128]{2,1,0:T(8,128)(2,1)}), bf16[32,128,128]{2,1,0:T(8,128)(2,1)S(1)}, u32[]{:S(2)}, u32[]{:S(2)}) async-start(bf16[32,128,128]{2,1,0:T(8,128)(2,1)} %bitcast.10), calls=%async_computation.1 | async-start | bytes 2097152 | tf_op jit(solution)/shard_map/all_to_all | solution.py:274
  51.6 18.1 %collective-permute-done.2.rest_2_ = bf16[15,2,128,128]{3,2,1,0:T(8,128)(2,1)} collective-permute-done((bf16[15,2,128,128]{3,2,1,0:T(8,128)(2,1)}, bf16[15,2,128,128]{3,2,1,0:T(8,128)(2,1)}, u32[]{:S(2)}, u32[]{:S(2)}) %collective-permute-start.2) | collective-permute-done | bytes 983072 | tf_op jit(solution)/shard_map/ppermute | solution.py:278
  69.7 0.3 collective-permute-start.4
  70.0 2.6 %collective-permute-done.3.rest_3_ = bf16[15,2,128,128]{3,2,1,0:T(8,128)(2,1)} collective-permute-done((bf16[15,2,128,128]{3,2,1,0:T(8,128)(2,1)}, bf16[15,2,128,128]{3,2,1,0:T(8,128)(2,1)}, u32[]{:S(2)}, u32[]{:S(2)}) %collective-permute-start.3) | collective-permute-done | bytes 983072 | tf_op jit(solution)/shard_map/ppermute | solution.py:277
  72.7 11.4 %shard_map.57 = (f32[33,128,128]{2,1,0:T(8,128)S(1)}, f32[33,1,128]{2,1,0:T(1,128)S(1)}, f32[33,8,128]{2,1,0:T(8,128)S(1)}) custom-call(s32[389]{0:T(512)S(1)} %pad_add_fusion.1.chunks, s32[1584]{0:T(1024)S(1)} %reshape.119.lists, s32[33]{0:T(128)S(1)} %pad.15.counts, bf16[32,128,128]{2,1,0:T(8,128)(2,1)S(1)} %all-to-all-done.1.q_ref, ...), custom_call_target="tpu_custom_call" | custom-call | flops 5000000000 | bytes 1 | tf_op jit(solution)/shard_map/pallas_call | solution.py:226
  84.1 13.0 %collective-permute-done.4.rest_0_ = bf16[17,2,128,128]{3,2,1,0:T(8,128)(2,1)} collective-permute-done((bf16[17,2,128,128]{3,2,1,0:T(8,128)(2,1)}, bf16[17,2,128,128]{3,2,1,0:T(8,128)(2,1)}, u32[]{:S(2)}, u32[]{:S(2)}) %collective-permute-start.4) | collective-permute-done | bytes 1114144 | tf_op jit(solution)/shard_map/ppermute | solution.py:278
  97.0 3.0 %collective-permute-done.5.rest_1_ = bf16[17,2,128,128]{3,2,1,0:T(8,128)(2,1)S(1)} collective-permute-done((bf16[17,2,128,128]{3,2,1,0:T(8,128)(2,1)}, bf16[17,2,128,128]{3,2,1,0:T(8,128)(2,1)S(1)}, u32[]{:S(2)}, u32[]{:S(2)}) %collective-permute-start.5) | collective-permute-done | bytes 1114144 | tf_op jit(solution)/shard_map/ppermute | solution.py:277
  100.0 6.7 %shard_map.58 = bf16[32,128,128]{2,1,0:T(8,128)(2,1)S(1)} custom-call(s32[389]{0:T(512)S(1)} %pad_add_fusion.2.chunks, s32[1584]{0:T(1024)S(1)} %reshape.120.lists, s32[33]{0:T(128)S(1)} %pad.17.counts, bf16[32,128,128]{2,1,0:T(8,128)(2,1)S(1)} %all-to-all-done.1.q_ref, bf16[17,2,128,128]{3,2,1,0:T(8,128)(2,1)} %collective-permute-done.4.rest_0_, ...), custom_call_target="tpu_custom_call" | custom-call | flops 5000000000 | bytes 1 | tf_op jit(solution)/shard_map/pallas_call | solution.py:226
  106.7 25.8 %all_to_all.15 = bf16[32,128,128]{2,1,0:T(8,128)(2,1)} all-to-all(bf16[32,128,128]{2,1,0:T(8,128)(2,1)S(1)} %shard_map.58), channel_id=1, replica_groups={{0,8,16,24,32,40,48,56,64,72,80,88,96,104,112,120,3,11,19,27,35,43,51,5..., dimensions={0} | all-to-all | bytes 2097152 | tf_op jit(solution)/shard_map/all_to_all | solution.py:274
  132.5 2.1 %shard_map.59 = bf16[128,4096]{1,0:T(8,128)(2,1)} custom-call(bf16[2,16,128,128]{3,2,1,0:T(8,128)(2,1)} %bitcast.11), custom_call_target="tpu_custom_call" | custom-call | tf_op jit(solution)/shard_map/pallas_call | solution.py:64
  (37 shorter events, 1.3 us)
Async XLA Ops:
  2.8 10.8 %copy-start = (s32[1,128,48]{1,2,0:T(8,128)S(1)}, s32[1,128,48]{1,2,0:T(8,128)}, u32[]{:S(2)}) copy-start(s32[1,128,48]{1,2,0:T(8,128)} %param.8) | copy-start | bytes 73732
  2.8 10.8 %copy-start.1 = (s32[1,128]{1,0:T(1,128)S(1)}, s32[1,128]{1,0:T(1,128)}, u32[]{:S(2)}) copy-start(s32[1,128]{1,0:T(1,128)} %param.9) | copy-start | bytes 1540
  2.8 40.2 %all-to-all-start = ((bf16[32,2,128,128]{3,2,1,0:T(8,128)(2,1)}), bf16[32,2,128,128]{3,2,1,0:T(8,128)(2,1)S(1)}, u32[]{:S(2)}, u32[]{:S(2)}) async-start(bf16[32,2,128,128]{3,2,1,0:T(8,128)(2,1)} %bitcast.9), calls=%async_computation | async-start | bytes 4194304 | tf_op jit(solution)/shard_map/all_to_all | solution.py:274
  13.8 2.2 %collective-permute-start = (s32[128,49]{1,0:T(8,128)S(1)}, s32[128,49]{1,0:T(8,128)S(1)}, u32[]{:S(2)}, u32[]{:S(2)}) collective-permute-start(s32[128,49]{1,0:T(8,128)S(1)} %copy.17), channel_id=1, source_target_pairs={{0,4},{4,0},{8,12},{12,8},{16,20},{20,16},{24,28},{28,24},{32,36},... | collective-permute-start | bytes 75272 | tf_op jit(solution)/shard_map/ppermute | solution.py:277
  44.2 28.5 %collective-permute-start.1 = (bf16[32,2,128,128]{3,2,1,0:T(8,128)(2,1)S(1)}, bf16[32,2,128,128]{3,2,1,0:T(8,128)(2,1)}, u32[]{:S(2)}, u32[]{:S(2)}) collective-permute-start(bf16[32,2,128,128]{3,2,1,0:T(8,128)(2,1)S(1)} %all-to-all-done.rest_0_), channel_id=1, source_target_pairs={{0,4},{4,0},{8,12},{12,8},{16,20},{20,16},{24,28},{28,24},{32,36},... | collective-permute-start | bytes 6291464 | tf_op jit(solution)/shard_map/ppermute | solution.py:277
  45.3 24.5 %collective-permute-start.2 = (bf16[15,2,128,128]{3,2,1,0:T(8,128)(2,1)}, bf16[15,2,128,128]{3,2,1,0:T(8,128)(2,1)}, u32[]{:S(2)}, u32[]{:S(2)}) collective-permute-start(bf16[15,2,128,128]{3,2,1,0:T(8,128)(2,1)} %slice.35), channel_id=1, source_target_pairs={{0,1},{1,0},{2,3},{3,2},{4,5},{5,4},{6,7},{7,6},{8,9},{9,8},{10,11... | collective-permute-start | bytes 2949128 | tf_op jit(solution)/shard_map/ppermute | solution.py:278
  45.3 24.8 %all-to-all-start.1 = ((bf16[32,128,128]{2,1,0:T(8,128)(2,1)}), bf16[32,128,128]{2,1,0:T(8,128)(2,1)S(1)}, u32[]{:S(2)}, u32[]{:S(2)}) async-start(bf16[32,128,128]{2,1,0:T(8,128)(2,1)} %bitcast.10), calls=%async_computation.1 | async-start | bytes 2097152 | tf_op jit(solution)/shard_map/all_to_all | solution.py:274
  69.7 2.9 %collective-permute-start.3 = (bf16[15,2,128,128]{3,2,1,0:T(8,128)(2,1)}, bf16[15,2,128,128]{3,2,1,0:T(8,128)(2,1)}, u32[]{:S(2)}, u32[]{:S(2)}) collective-permute-start(bf16[15,2,128,128]{3,2,1,0:T(8,128)(2,1)} %collective-permute-done.2.rest_2_), channel_id=1, source_target_pairs={{0,4},{4,0},{8,12},{12,8},{16,20},{20,16},{24,28},{28,24},{32,36},... | collective-permute-start | bytes 2949128 | tf_op jit(solution)/shard_map/ppermute | solution.py:277
  69.7 27.3 %collective-permute-start.4 = (bf16[17,2,128,128]{3,2,1,0:T(8,128)(2,1)}, bf16[17,2,128,128]{3,2,1,0:T(8,128)(2,1)}, u32[]{:S(2)}, u32[]{:S(2)}) collective-permute-start(bf16[17,2,128,128]{3,2,1,0:T(8,128)(2,1)} %slice.34), channel_id=1, source_target_pairs={{0,1},{1,0},{2,3},{3,2},{4,5},{5,4},{6,7},{7,6},{8,9},{9,8},{10,11... | collective-permute-start | bytes 3342344 | tf_op jit(solution)/shard_map/ppermute | solution.py:278
  97.0 3.0 %collective-permute-start.5 = (bf16[17,2,128,128]{3,2,1,0:T(8,128)(2,1)}, bf16[17,2,128,128]{3,2,1,0:T(8,128)(2,1)S(1)}, u32[]{:S(2)}, u32[]{:S(2)}) collective-permute-start(bf16[17,2,128,128]{3,2,1,0:T(8,128)(2,1)} %collective-permute-done.4.rest_0_), channel_id=1, source_target_pairs={{0,4},{4,0},{8,12},{12,8},{16,20},{20,16},{24,28},{28,24},{32,36},... | collective-permute-start | bytes 3342344 | tf_op jit(solution)/shard_map/ppermute | solution.py:277

commit v10 on v7

--- a/solution.py
+++ b/solution.py
@@ -71,7 +71,7 @@
 
 
 def attention_kernel(
-    first, last, parts, chunks, lists, counts, q_ref, *rest
+    first, last, parts, most, table_hbm, q_ref, *rest
 ):
     rest = list(rest)
     kv_hbm = [rest.pop(0) for _ in range(parts)]
@@ -83,11 +83,10 @@
     else:
         acc_ref, top_ref, total_ref = (rest.pop(0) for _ in range(3))
     s0, s1, p0, p1, kv_ref = rest[:5]
-    sems = rest[-1]
+    table, sems = rest[-2:]
     nq = q_ref.shape[0]
-    most = lists.shape[0] // (nq + 1)
-
-    copies = []
+
+    copies = [(table_hbm, table)]
     at = 0
     for part in kv_hbm:
         copies.append((part, kv_ref.at[pl.ds(at, part.shape[0])]))
@@ -109,12 +108,12 @@
         copy.wait()
 
     def where(t):
-        code = chunks[t + 1]
+        code = table[t + (nq + 1) * (most + 1) + 1]
         return code // 16, code % 16
 
     def places(b, c):
-        end = jnp.maximum(counts[b] - 1, 0)
-        return [lists[b * most + jnp.minimum(c * GROUP + g, end)] for g in range(GROUP)]
+        end = jnp.maximum(table[b] - 1, 0)
+        return [table[(nq + 1) + b * most + jnp.minimum(c * GROUP + g, end)] for g in range(GROUP)]
 
     def scores(b, chosen, dst):
         rows = jnp.concatenate([kv_ref[i, 0] for i in chosen], axis=0)
@@ -124,7 +123,7 @@
         return jnp.max(s.reshape(GROUP * BLOCK // 8, 8, BLOCK), axis=0)
 
     def weights(b, c, largest, src, dst, top, total):
-        count = counts[b]
+        count = table[b]
         top = jnp.where(c == 0, top_ref[b], top)
         total = jnp.where(c == 0, total_ref[b], total)
         new_top = jnp.maximum(top, jnp.max(largest, axis=0, keepdims=True))
@@ -146,7 +145,7 @@
             cols, src[...], preferred_element_type=jnp.float32
         )
 
-    steps = chunks[0]
+    steps = table[(nq + 1) * (most + 1)]
     score_bufs, weight_bufs = (s0, s1), (p0, p1)
     b0, c0 = where(0)
     places0 = places(b0, c0)
@@ -193,15 +192,14 @@
     if last:
 
         def finish(b, _):
-            out = acc_ref[b] / jnp.sum(total_ref[b], axis=0, keepdims=True)
+            out = acc_ref[b] * (1.0 / jnp.sum(total_ref[b], axis=0, keepdims=True))
             o_ref[b] = out.T.astype(jnp.bfloat16)
             return 0
 
-        lax.fori_loop(0, nq, finish, 0, unroll=4)
-
-
-def attention(tables, q, kv, state, last):
-    chunks, lists, counts = tables
+        lax.fori_loop(0, nq, finish, 0, unroll=8)
+
+
+def attention(table, most, q, kv, state, last):
     nq = q.shape[0]
     first = state is None
     hbm = pl.BlockSpec(memory_space=pl.ANY)
@@ -221,26 +219,20 @@
     else:
         out_shape = [jax.ShapeDtypeStruct(s, jnp.float32) for s in shapes]
         out_specs = [vmem for s in shapes]
-    scratch += [pltpu.SemaphoreType.DMA((len(kv),))]
+    scratch += [pltpu.SMEM(table.shape, jnp.int32), pltpu.SemaphoreType.DMA((len(kv) + 1,))]
     args = [q, *kv] + ([] if first else list(state))
     return pl.pallas_call(
-        functools.partial(attention_kernel, first, last, len(kv)),
-        grid_spec=pltpu.PrefetchScalarGridSpec(
-            num_scalar_prefetch=3,
-            grid=(1,),
-            in_specs=[vmem] + [hbm] * len(kv) + [vmem] * (len(args) - 1 - len(kv)),
-            out_specs=out_specs,
-            scratch_shapes=scratch,
-        ),
+        functools.partial(attention_kernel, first, last, len(kv), most),
+        in_specs=[hbm, vmem] + [hbm] * len(kv) + [vmem] * (len(args) - 1 - len(kv)),
+        out_specs=out_specs,
+        scratch_shapes=scratch,
         out_shape=out_shape,
         compiler_params=pltpu.CompilerParams(vmem_limit_bytes=VMEM),
-        cost_estimate=pl.CostEstimate(
-            flops=1_000_000, bytes_accessed=1, transcendentals=0
-        ),
-    )(chunks, lists, counts, *args)
-
-
-def make_tables(match, place):
+        cost_estimate=pl.CostEstimate(flops=1_000_000, bytes_accessed=1, transcendentals=0),
+    )(table, *args)
+
+
+def make_table(match, place):
     nq, most = match.shape
     at = jnp.arange(most, dtype=jnp.int32)
     before = (at[:, None] < at[None, :])[None] & match[:, :, None]
@@ -255,9 +247,9 @@
     b = jnp.sum((t[:, None] >= ends[None, :]).astype(jnp.int32), axis=1)
     start = jnp.sum(jnp.where(row[None, :] < b[:, None], steps[None, :], 0), axis=1)
     c = jnp.where(b < nq, t - start, 0)
-    chunks = jnp.concatenate([ends[-1:], b * 16 + c])
     lists = jnp.pad(lists, ((0, 1), (0, 0))).reshape(-1)
-    return chunks, lists, jnp.pad(counts, (0, 1))
+    table = jnp.concatenate([jnp.pad(counts, (0, 1)), lists, ends[-1:], b * 16 + c])
+    return jnp.pad(table, (0, -table.shape[0] % 1024))
 
 
 def local(queries, keys, values, key_blocks, key_count):
@@ -294,30 +286,30 @@
     block_place = (blocks // 2) % PLACES
     near = ((block_y == 0) | (block_y == 3)) == outer
     block_at = (block_y // 2) * PLACES + block_place
-    size = 2 * PLACES
+    size, most = 2 * PLACES, blocks.shape[1]
     early = near | (block_at < CUT)
     early_place = jnp.where(
         near, block_core * size + block_at, 2 * size + block_core * CUT + block_at
     )
     late_place = block_core * (size - CUT) + block_at - CUT
-    early_tables = make_tables(active & early, early_place)
-    late_tables = make_tables(active & ~early, late_place)
-
-    kv, q, early_tables, late_tables = lax.optimization_barrier(
+    early_table = make_table(active & early, early_place)
+    late_table = make_table(active & ~early, late_place)
+
+    kv, q, early_table, late_table = lax.optimization_barrier(
         (
             swap(kv.reshape(2 * PLACES, 2, BLOCK, HDIM)),
             pack_q(queries),
-            early_tables,
-            late_tables,
+            early_table,
+            late_table,
         )
     )
     far, far_late = kv[:CUT], kv[CUT:]
     kv, far_late = lax.optimization_barrier((kv, far_late))
     far, far_late = to_pair(far), to_pair(far_late)
     q = swap(q.reshape(2 * PLACES, BLOCK, HDIM))
-    state = attention(early_tables, q, [kv, to_core(kv), far, to_core(far)], None, False)
+    state = attention(early_table, most, q, [kv, to_core(kv), far, to_core(far)], None, False)
     state, far_late = lax.optimization_barrier((state, far_late))
-    out = attention(late_tables, q, [far_late, to_core(far_late)], state, True)
+    out = attention(late_table, most, q, [far_late, to_core(far_late)], state, True)
     return unpack(swap(out).reshape(2, PLACES, BLOCK, HDIM))
 
 

time: 131 us -> 131 us (level)
  Pallas kernels: 35.3 us -> 20.6 us
  waiting for transfers between devices: 45.2 us -> 54.8 us
  blocking collectives: 22.3 us -> 26.9 us
  local copies, waits for them, and re-layouts: 3.97 us -> 5.37 us
  other arithmetic: 4.76 us -> 3.39 us
    pallas_call x2, Pallas kernels: 28.2 us -> 13.5 us  [attention(): pl.pallas_call(functools.partial(attention_kernel, first, last, len(kv),...]
    ppermute x2, waiting for transfers between devices: 18.8 us -> 28.4 us  [local(): lax.ppermute(a, 'head', [(i, i ^ 1) for i in range(head_count)])]
    all_to_all x1, blocking collectives: 22.3 us -> 26.9 us  [local(): lax.all_to_all(a, ('seq', 'head'), 0, 0, axis_index_groups=groups, tiled=...]
    concatenate x0 -> x2, local copies, waits for them, and re-layouts: none -> 1.39 us  [make_table(): jnp.concatenate([jnp.pad(counts, (0, 1)), lists, ends[-1:], b * 16 + c])]
    concatenate x2 -> x0, other arithmetic: 1.37 us -> none  [make_tables(): chunks = jnp.concatenate([ends[-1:], b * 16 + c])]
  transfers between devices with their start and end apart: 8 -> 8, of which waited for: 6 -> 6; matrix products, arithmetic and copies ran while one was open for 6% -> 6% of each run, Pallas kernels for 16% -> 8%
where the time goes in v10:
time: 131 us
  waiting for transfers between devices  54.8 us (42%)
  blocking collectives  26.9 us (21%)
  Pallas kernels  20.6 us (16%)
  starting transfers between devices  19.3 us (15%)
  local copies, waits for them, and re-layouts  5.37 us (4%)
  other arithmetic  3.39 us (3%)
    ppermute x2, waiting for transfers between devices, local(): lax.ppermute(a, 'head', [(i, i ^ 1) for i in range(head_count)])  28.4 us
    all_to_all x1, blocking collectives, local(): lax.all_to_all(a, ('seq', 'head'), 0, 0, axis_index_groups=groups, tiled=...  26.9 us
    all_to_all x2, waiting for transfers between devices, local(): lax.all_to_all(a, ('seq', 'head'), 0, 0, axis_index_groups=groups, tiled=...  23.1 us
    all_to_all x2, starting transfers between devices, local(): lax.all_to_all(a, ('seq', 'head'), 0, 0, axis_index_groups=groups, tiled=...  17.2 us
    pallas_call x2, Pallas kernels, attention(): pl.pallas_call(functools.partial(attention_kernel, first, last, len(kv),...  13.5 us
    ppermute x4, waiting for transfers between devices, local(): lax.ppermute(a, 'seq', [(i, i ^ 1) for i in range(seq_count)])  3.26 us
    pallas_call x1, Pallas kernels, pack_kv(): pl.pallas_call(pack_kv_kernel, grid=(PLACES // STEP,), in_specs=[FLAT, FL...  2.82 us
  transfers between devices with their start and end apart: 8, of which 6 were waited for; matrix products, arithmetic and copies ran while one was open for 6% of the time, Pallas kernels for 8%

profile of v10, /device:TPU:0, one launch (start us, length us, event | category | flops | bytes accessed | tf_op | source)
XLA Modules:
  0.0 130.6 jit_solution(12258532448117063050)
XLA Ops:
  0.0 2.8 %shard_map.55 = bf16[2,16,2,128,128]{4,3,2,1,0:T(8,128)(2,1)} custom-call(bf16[128,4096]{1,0:T(8,128)(2,1)} %k_ref.1, bf16[128,4096]{1,0:T(8,128)(2,1)} %v_ref.1), custom_call_target="tpu_custom_call" | custom-call | tf_op jit(solution)/shard_map/pallas_call | solution.py:44
  2.8 10.8 %all-to-all-start = ((bf16[32,2,128,128]{3,2,1,0:T(8,128)(2,1)}), bf16[32,2,128,128]{3,2,1,0:T(8,128)(2,1)S(1)}, u32[]{:S(2)}, u32[]{:S(2)}) async-start(bf16[32,2,128,128]{3,2,1,0:T(8,128)(2,1)} %bitcast.9), calls=%async_computation | async-start | bytes 4194304 | tf_op jit(solution)/shard_map/all_to_all | solution.py:266
  13.9 2.1 %shard_map.56 = bf16[2,16,128,128]{3,2,1,0:T(8,128)(2,1)} custom-call(bf16[128,4096]{1,0:T(8,128)(2,1)} %q_ref.1), custom_call_target="tpu_custom_call" | custom-call | tf_op jit(solution)/shard_map/pallas_call | solution.py:54
  16.4 0.2 convert_reduce_fusion.4
  16.9 0.6 slice.33
  17.6 0.6 slice.32
  18.2 0.6 convert_reduce_fusion
  18.8 1.7 %select_reduce_fusion = (s32[32,48]{1,0:T(8,128)S(1)}, s32[32,48]{1,0:T(8,128)S(1)}) fusion(s32[32,48]{1,0:T(8,128)S(1)} %get-tuple-element.39, s32[32,48]{1,0:T(8,128)S(1)} %get-tuple-element.37, pred[32,48]{1,0:T(8,128)(4,1)S(1)} %get-tuple-element.44, s32[32,48]{1,0:T(8,128)S(1)} %add_select_fusion.5, pred[32,48]{1,0:T(8,128)(4,1)S(1)} %get-tuple-element.48, ...), kind=kLoop, calls=%fused_computation | loop fusion | flops 586752 | bytes 39936 | tf_op jit(solution)/shard_map/reduce_sum | solution.py:241
  20.9 0.7 concatenate.11
  21.9 0.7 concatenate.10
  22.5 20.5 %all-to-all-done.rest_0_ = bf16[32,2,128,128]{3,2,1,0:T(8,128)(2,1)S(1)} async-done(((bf16[32,2,128,128]{3,2,1,0:T(8,128)(2,1)}), bf16[32,2,128,128]{3,2,1,0:T(8,128)(2,1)S(1)}, u32[]{:S(2)}, u32[]{:S(2)}) %all-to-all-start) | async-done | bytes 2097184 | tf_op jit(solution)/shard_map/all_to_all | solution.py:266
  43.0 1.2 slice.34
  44.2 1.1 slice.35
  45.3 2.0 %collective-permute-start.4 = (bf16[18,2,128,128]{3,2,1,0:T(8,128)(2,1)}, bf16[18,2,128,128]{3,2,1,0:T(8,128)(2,1)}, u32[]{:S(2)}, u32[]{:S(2)}) collective-permute-start(bf16[18,2,128,128]{3,2,1,0:T(8,128)(2,1)} %slice.34), channel_id=1, source_target_pairs={{0,1},{1,0},{2,3},{3,2},{4,5},{5,4},{6,7},{7,6},{8,9},{9,8},{10,11... | collective-permute-start | bytes 3538952 | tf_op jit(solution)/shard_map/ppermute | solution.py:270
  47.3 6.4 %all-to-all-start.1 = ((bf16[32,128,128]{2,1,0:T(8,128)(2,1)}), bf16[32,128,128]{2,1,0:T(8,128)(2,1)S(1)}, u32[]{:S(2)}, u32[]{:S(2)}) async-start(bf16[32,128,128]{2,1,0:T(8,128)(2,1)} %bitcast.10), calls=%async_computation.1 | async-start | bytes 2097152 | tf_op jit(solution)/shard_map/all_to_all | solution.py:266
  53.7 15.1 %collective-permute-done.2.rest_2_ = bf16[14,2,128,128]{3,2,1,0:T(8,128)(2,1)} collective-permute-done((bf16[14,2,128,128]{3,2,1,0:T(8,128)(2,1)}, bf16[14,2,128,128]{3,2,1,0:T(8,128)(2,1)}, u32[]{:S(2)}, u32[]{:S(2)}) %collective-permute-start.2) | collective-permute-done | bytes 917536 | tf_op jit(solution)/shard_map/ppermute | solution.py:270
  68.8 2.6 %all-to-all-done.1.q_ref = bf16[32,128,128]{2,1,0:T(8,128)(2,1)S(1)} async-done(((bf16[32,128,128]{2,1,0:T(8,128)(2,1)}), bf16[32,128,128]{2,1,0:T(8,128)(2,1)S(1)}, u32[]{:S(2)}, u32[]{:S(2)}) %all-to-all-start.1) | async-done | bytes 1048608 | tf_op jit(solution)/shard_map/all_to_all | solution.py:266
  71.4 0.2 collective-permute-done.3.rest_3_
  71.6 8.7 %shard_map.57 = (f32[33,128,128]{2,1,0:T(8,128)S(1)}, f32[33,1,128]{2,1,0:T(1,128)S(1)}, f32[33,8,128]{2,1,0:T(8,128)S(1)}) custom-call(s32[2048]{0:T(1024)S(1)} %pad.23.table_hbm, bf16[32,128,128]{2,1,0:T(8,128)(2,1)S(1)} %all-to-all-done.1.q_ref, bf16[32,2,128,128]{3,2,1,0:T(8,128)(2,1)S(1)} %all-to-all-done.rest_0_, ...), custom_call_target="tpu_custom_call" | custom-call | flops 1000000 | bytes 1 | tf_op jit(solution)/shard_map/pallas_call | solution.py:224
  80.3 13.3 %collective-permute-done.4.rest_0_ = bf16[18,2,128,128]{3,2,1,0:T(8,128)(2,1)} collective-permute-done((bf16[18,2,128,128]{3,2,1,0:T(8,128)(2,1)}, bf16[18,2,128,128]{3,2,1,0:T(8,128)(2,1)}, u32[]{:S(2)}, u32[]{:S(2)}) %collective-permute-start.4) | collective-permute-done | bytes 1179680 | tf_op jit(solution)/shard_map/ppermute | solution.py:270
  93.7 3.1 %collective-permute-done.5.rest_1_ = bf16[18,2,128,128]{3,2,1,0:T(8,128)(2,1)S(1)} collective-permute-done((bf16[18,2,128,128]{3,2,1,0:T(8,128)(2,1)}, bf16[18,2,128,128]{3,2,1,0:T(8,128)(2,1)S(1)}, u32[]{:S(2)}, u32[]{:S(2)}) %collective-permute-start.5) | collective-permute-done | bytes 1179680 | tf_op jit(solution)/shard_map/ppermute | solution.py:269
  96.7 4.8 %shard_map.58 = bf16[32,128,128]{2,1,0:T(8,128)(2,1)S(1)} custom-call(s32[2048]{0:T(1024)S(1)} %pad.26.table_hbm, bf16[32,128,128]{2,1,0:T(8,128)(2,1)S(1)} %all-to-all-done.1.q_ref, bf16[18,2,128,128]{3,2,1,0:T(8,128)(2,1)} %collective-permute-done.4.rest_0_, bf16[18,2,128,128]{3,2,1,0:T(8,128)(2,1)S(1)} %collective-permute-done.5.rest_1_, ...), custom_call_target="tpu_custom_call" | custom-call | flops 1000000 | bytes 1 | tf_op jit(solution)/shard_map/pallas_call | solution.py:224
  101.5 26.9 %all_to_all.15 = bf16[32,128,128]{2,1,0:T(8,128)(2,1)} all-to-all(bf16[32,128,128]{2,1,0:T(8,128)(2,1)S(1)} %shard_map.58), channel_id=1, replica_groups={{0,8,16,24,32,40,48,56,64,72,80,88,96,104,112,120,3,11,19,27,35,43,51,5..., dimensions={0} | all-to-all | bytes 2097152 | tf_op jit(solution)/shard_map/all_to_all | solution.py:266
  128.5 2.1 %shard_map.59 = bf16[128,4096]{1,0:T(8,128)(2,1)} custom-call(bf16[2,16,128,128]{3,2,1,0:T(8,128)(2,1)} %bitcast.11), custom_call_target="tpu_custom_call" | custom-call | tf_op jit(solution)/shard_map/pallas_call | solution.py:64
  (39 shorter events, 1.5 us)
Async XLA Ops:
  2.8 10.8 %copy-start = (s32[1,128,48]{1,2,0:T(8,128)S(1)}, s32[1,128,48]{1,2,0:T(8,128)}, u32[]{:S(2)}) copy-start(s32[1,128,48]{1,2,0:T(8,128)} %param.8) | copy-start | bytes 73732
  2.8 10.8 %copy-start.1 = (s32[1,128]{1,0:T(1,128)S(1)}, s32[1,128]{1,0:T(1,128)}, u32[]{:S(2)}) copy-start(s32[1,128]{1,0:T(1,128)} %param.9) | copy-start | bytes 1540
  2.8 40.2 %all-to-all-start = ((bf16[32,2,128,128]{3,2,1,0:T(8,128)(2,1)}), bf16[32,2,128,128]{3,2,1,0:T(8,128)(2,1)S(1)}, u32[]{:S(2)}, u32[]{:S(2)}) async-start(bf16[32,2,128,128]{3,2,1,0:T(8,128)(2,1)} %bitcast.9), calls=%async_computation | async-start | bytes 4194304 | tf_op jit(solution)/shard_map/all_to_all | solution.py:266
  13.8 2.2 %collective-permute-start = (s32[128,49]{1,0:T(8,128)S(1)}, s32[128,49]{1,0:T(8,128)S(1)}, u32[]{:S(2)}, u32[]{:S(2)}) collective-permute-start(s32[128,49]{1,0:T(8,128)S(1)} %copy.17), channel_id=1, source_target_pairs={{0,4},{4,0},{8,12},{12,8},{16,20},{20,16},{24,28},{28,24},{32,36},... | collective-permute-start | bytes 75272 | tf_op jit(solution)/shard_map/ppermute | solution.py:269
  44.2 27.4 %collective-permute-start.1 = (bf16[32,2,128,128]{3,2,1,0:T(8,128)(2,1)S(1)}, bf16[32,2,128,128]{3,2,1,0:T(8,128)(2,1)}, u32[]{:S(2)}, u32[]{:S(2)}) collective-permute-start(bf16[32,2,128,128]{3,2,1,0:T(8,128)(2,1)S(1)} %all-to-all-done.rest_0_), channel_id=1, source_target_pairs={{0,4},{4,0},{8,12},{12,8},{16,20},{20,16},{24,28},{28,24},{32,36},... | collective-permute-start | bytes 6291464 | tf_op jit(solution)/shard_map/ppermute | solution.py:269
  45.3 23.5 %collective-permute-start.2 = (bf16[14,2,128,128]{3,2,1,0:T(8,128)(2,1)}, bf16[14,2,128,128]{3,2,1,0:T(8,128)(2,1)}, u32[]{:S(2)}, u32[]{:S(2)}) collective-permute-start(bf16[14,2,128,128]{3,2,1,0:T(8,128)(2,1)} %slice.35), channel_id=1, source_target_pairs={{0,1},{1,0},{2,3},{3,2},{4,5},{5,4},{6,7},{7,6},{8,9},{9,8},{10,11... | collective-permute-start | bytes 2752520 | tf_op jit(solution)/shard_map/ppermute | solution.py:270
  45.3 48.4 %collective-permute-start.4 = (bf16[18,2,128,128]{3,2,1,0:T(8,128)(2,1)}, bf16[18,2,128,128]{3,2,1,0:T(8,128)(2,1)}, u32[]{:S(2)}, u32[]{:S(2)}) collective-permute-start(bf16[18,2,128,128]{3,2,1,0:T(8,128)(2,1)} %slice.34), channel_id=1, source_target_pairs={{0,1},{1,0},{2,3},{3,2},{4,5},{5,4},{6,7},{7,6},{8,9},{9,8},{10,11... | collective-permute-start | bytes 3538952 | tf_op jit(solution)/shard_map/ppermute | solution.py:270
  47.3 24.1 %all-to-all-start.1 = ((bf16[32,128,128]{2,1,0:T(8,128)(2,1)}), bf16[32,128,128]{2,1,0:T(8,128)(2,1)S(1)}, u32[]{:S(2)}, u32[]{:S(2)}) async-start(bf16[32,128,128]{2,1,0:T(8,128)(2,1)} %bitcast.10), calls=%async_computation.1 | async-start | bytes 2097152 | tf_op jit(solution)/shard_map/all_to_all | solution.py:266
  68.8 2.8 %collective-permute-start.3 = (bf16[14,2,128,128]{3,2,1,0:T(8,128)(2,1)}, bf16[14,2,128,128]{3,2,1,0:T(8,128)(2,1)}, u32[]{:S(2)}, u32[]{:S(2)}) collective-permute-start(bf16[14,2,128,128]{3,2,1,0:T(8,128)(2,1)} %collective-permute-done.2.rest_2_), channel_id=1, source_target_pairs={{0,4},{4,0},{8,12},{12,8},{16,20},{20,16},{24,28},{28,24},{32,36},... | collective-permute-start | bytes 2752520 | tf_op jit(solution)/shard_map/ppermute | solution.py:269
  93.6 3.1 %collective-permute-start.5 = (bf16[18,2,128,128]{3,2,1,0:T(8,128)(2,1)}, bf16[18,2,128,128]{3,2,1,0:T(8,128)(2,1)S(1)}, u32[]{:S(2)}, u32[]{:S(2)}) collective-permute-start(bf16[18,2,128,128]{3,2,1,0:T(8,128)(2,1)} %collective-permute-done.4.rest_0_), channel_id=1, source_target_pairs={{0,4},{4,0},{8,12},{12,8},{16,20},{20,16},{24,28},{28,24},{32,36},... | collective-permute-start | bytes 3538952 | tf_op jit(solution)/shard_map/ppermute | solution.py:269

commit v11 on v10

--- a/solution.py
+++ b/solution.py
@@ -18,11 +18,31 @@
 VMEM = 24 << 20
 
 
-def pack_kv_kernel(k_ref, v_ref, o_ref):
-    for h in range(o_ref.shape[0] * o_ref.shape[1]):
-        cols = slice(h * HDIM, (h + 1) * HDIM)
-        o_ref[h % 2, h // 2, 0] = k_ref[:, cols]
-        o_ref[h % 2, h // 2, 1] = v_ref[:, cols].T
+def pack_kv_kernel(k_hbm, v_hbm, o_hbm, k_ref, v_ref, o_ref, in_sems, out_sems):
+    parts = in_sems.shape[0]
+    heads = 2 * PLACES // parts
+    width = heads * HDIM
+    places = heads // 2
+    arrivals, departures = [], []
+    for i in range(parts):
+        cols = pl.ds(i * width, width)
+        for j, (src, dst) in enumerate(((k_hbm, k_ref), (v_hbm, v_ref))):
+            copy = pltpu.make_async_copy(src.at[:, cols], dst.at[:, cols], in_sems.at[i, j])
+            copy.start()
+            arrivals.append(copy)
+    for i in range(parts):
+        arrivals[2 * i].wait()
+        arrivals[2 * i + 1].wait()
+        for h in range(i * heads, (i + 1) * heads):
+            cols = slice(h * HDIM, (h + 1) * HDIM)
+            o_ref[h % 2, h // 2, 0] = k_ref[:, cols]
+            o_ref[h % 2, h // 2, 1] = v_ref[:, cols].T
+        at = pl.ds(i * places, places)
+        copy = pltpu.make_async_copy(o_ref.at[:, at], o_hbm.at[:, at], out_sems.at[i])
+        copy.start()
+        departures.append(copy)
+    for copy in departures:
+        copy.wait()
 
 
 def pack_q_kernel(q_ref, o_ref):
@@ -41,12 +61,21 @@
 
 
 def pack_kv(keys, values):
+    hbm = pl.BlockSpec(memory_space=pl.ANY)
+    shape = (2, PLACES, 2, BLOCK, HDIM)
     return pl.pallas_call(
         pack_kv_kernel,
-        grid=(PLACES // STEP,),
-        in_specs=[FLAT, FLAT],
-        out_specs=pl.BlockSpec((2, STEP, 2, BLOCK, HDIM), lambda i: (0, i, 0, 0, 0)),
-        out_shape=jax.ShapeDtypeStruct((2, PLACES, 2, BLOCK, HDIM), keys.dtype),
+        in_specs=[hbm, hbm],
+        out_specs=hbm,
+        out_shape=jax.ShapeDtypeStruct(shape, keys.dtype),
+        scratch_shapes=[
+            pltpu.VMEM(keys.shape, keys.dtype),
+            pltpu.VMEM(values.shape, values.dtype),
+            pltpu.VMEM(shape, keys.dtype),
+            pltpu.SemaphoreType.DMA((4, 2)),
+            pltpu.SemaphoreType.DMA((4,)),
+        ],
+        compiler_params=pltpu.CompilerParams(vmem_limit_bytes=VMEM),
     )(keys, values)
 
 

time: 131 us -> 134 us (1.023)
  local copies, waits for them, and re-layouts: 5.37 us -> 9.16 us
    unnamed x4 -> x10, local copies, waits for them, and re-layouts: 0.01 us -> 3.8 us
    pallas_call x1, Pallas kernels: 2.82 us -> 1.09 us  [pack_kv(): pl.pallas_call(pack_kv_kernel, in_specs=[hbm, hbm], out_specs=hbm, out_sh...]
    pallas_call x2, Pallas kernels: 13.5 us -> 15 us  [attention(): pl.pallas_call(functools.partial(attention_kernel, first, last, len(kv),...]
  transfers between devices with their start and end apart: 8 -> 8, of which waited for: 6 -> 6; matrix products, arithmetic and copies ran while one was open for 6% -> 6% of each run, Pallas kernels for 8% -> 9%
where the time goes in v11:
time: 134 us; the launch traced here: 133 us
  waiting for transfers between devices  54 us (40%)
  blocking collectives  26.3 us (20%)
  Pallas kernels  20.3 us (15%)
  starting transfers between devices  19.3 us (14%)
  local copies, waits for them, and re-layouts  9.16 us (7%)
  other arithmetic  3.39 us (3%)
    ppermute x2, waiting for transfers between devices, local(): lax.ppermute(a, 'head', [(i, i ^ 1) for i in range(head_count)])  27.7 us
    all_to_all x1, blocking collectives, local(): lax.all_to_all(a, ('seq', 'head'), 0, 0, axis_index_groups=groups, tiled=...  26.3 us
    all_to_all x2, waiting for transfers between devices, local(): lax.all_to_all(a, ('seq', 'head'), 0, 0, axis_index_groups=groups, tiled=...  23.1 us
    all_to_all x2, starting transfers between devices, local(): lax.all_to_all(a, ('seq', 'head'), 0, 0, axis_index_groups=groups, tiled=...  17.2 us
    pallas_call x2, Pallas kernels, attention(): pl.pallas_call(functools.partial(attention_kernel, first, last, len(kv),...  15 us
    unnamed x10, local copies, waits for them, and re-layouts  3.8 us
    ppermute x4, waiting for transfers between devices, local(): lax.ppermute(a, 'seq', [(i, i ^ 1) for i in range(seq_count)])  3.26 us
  transfers between devices with their start and end apart: 8, of which 6 were waited for; matrix products, arithmetic and copies ran while one was open for 6% of the time, Pallas kernels for 9%

profile of v11, /device:TPU:0, one launch (start us, length us, event | category | flops | bytes accessed | tf_op | source)
XLA Modules:
  0.0 132.7 jit_solution(4602492791271929281)
XLA Ops:
  0.0 1.2 copy-done.1
  1.2 1.2 copy-done.2
  2.5 1.1 shard_map.55
  3.6 1.3 %copy-done = bf16[2,16,2,128,128]{4,3,2,1,0:T(8,128)(2,1)} copy-done((bf16[2,16,2,128,128]{4,3,2,1,0:T(8,128)(2,1)}, bf16[2,16,2,128,128]{4,3,2,1,0:T(8,128)(2,1)S(1)}, u32[]{:S(2)}) %copy-start) | copy-done | bytes 2097176
  4.9 10.8 %all-to-all-start = ((bf16[32,2,128,128]{3,2,1,0:T(8,128)(2,1)}), bf16[32,2,128,128]{3,2,1,0:T(8,128)(2,1)S(1)}, u32[]{:S(2)}, u32[]{:S(2)}) async-start(bf16[32,2,128,128]{3,2,1,0:T(8,128)(2,1)} %bitcast.9), calls=%async_computation | async-start | bytes 4194304 | tf_op jit(solution)/shard_map/all_to_all | solution.py:295
  16.0 2.1 %shard_map.56 = bf16[2,16,128,128]{3,2,1,0:T(8,128)(2,1)} custom-call(bf16[128,4096]{1,0:T(8,128)(2,1)} %q_ref.1), custom_call_target="tpu_custom_call" | custom-call | tf_op jit(solution)/shard_map/pallas_call | solution.py:83
  19.6 0.6 slice.32
  20.3 0.6 convert_reduce_fusion
  20.9 1.7 %select_reduce_fusion = (s32[32,48]{1,0:T(8,128)S(1)}, s32[32,48]{1,0:T(8,128)S(1)}) fusion(s32[32,48]{1,0:T(8,128)S(1)} %get-tuple-element.39, s32[32,48]{1,0:T(8,128)S(1)} %get-tuple-element.37, pred[32,48]{1,0:T(8,128)(4,1)S(1)} %get-tuple-element.44, s32[32,48]{1,0:T(8,128)S(1)} %add_select_fusion.5, pred[32,48]{1,0:T(8,128)(4,1)S(1)} %get-tuple-element.48, ...), kind=kLoop, calls=%fused_computation | loop fusion | flops 586752 | bytes 39936 | tf_op jit(solution)/shard_map/reduce_sum | solution.py:270
  22.9 0.7 concatenate.11
  23.9 0.7 concatenate.10
  24.6 20.5 %all-to-all-done.rest_0_ = bf16[32,2,128,128]{3,2,1,0:T(8,128)(2,1)S(1)} async-done(((bf16[32,2,128,128]{3,2,1,0:T(8,128)(2,1)}), bf16[32,2,128,128]{3,2,1,0:T(8,128)(2,1)S(1)}, u32[]{:S(2)}, u32[]{:S(2)}) %all-to-all-start) | async-done | bytes 2097184 | tf_op jit(solution)/shard_map/all_to_all | solution.py:295
  45.1 1.2 slice.34
  46.3 1.1 slice.35
  47.4 2.0 %collective-permute-start.4 = (bf16[18,2,128,128]{3,2,1,0:T(8,128)(2,1)}, bf16[18,2,128,128]{3,2,1,0:T(8,128)(2,1)}, u32[]{:S(2)}, u32[]{:S(2)}) collective-permute-start(bf16[18,2,128,128]{3,2,1,0:T(8,128)(2,1)} %slice.34), channel_id=1, source_target_pairs={{0,1},{1,0},{2,3},{3,2},{4,5},{5,4},{6,7},{7,6},{8,9},{9,8},{10,11... | collective-permute-start | bytes 3538952 | tf_op jit(solution)/shard_map/ppermute | solution.py:299
  49.4 6.4 %all-to-all-start.1 = ((bf16[32,128,128]{2,1,0:T(8,128)(2,1)}), bf16[32,128,128]{2,1,0:T(8,128)(2,1)S(1)}, u32[]{:S(2)}, u32[]{:S(2)}) async-start(bf16[32,128,128]{2,1,0:T(8,128)(2,1)} %bitcast.10), calls=%async_computation.1 | async-start | bytes 2097152 | tf_op jit(solution)/shard_map/all_to_all | solution.py:295
  55.8 15.1 %collective-permute-done.2.rest_2_ = bf16[14,2,128,128]{3,2,1,0:T(8,128)(2,1)} collective-permute-done((bf16[14,2,128,128]{3,2,1,0:T(8,128)(2,1)}, bf16[14,2,128,128]{3,2,1,0:T(8,128)(2,1)}, u32[]{:S(2)}, u32[]{:S(2)}) %collective-permute-start.2) | collective-permute-done | bytes 917536 | tf_op jit(solution)/shard_map/ppermute | solution.py:299
  70.8 2.6 %all-to-all-done.1.q_ref = bf16[32,128,128]{2,1,0:T(8,128)(2,1)S(1)} async-done(((bf16[32,128,128]{2,1,0:T(8,128)(2,1)}), bf16[32,128,128]{2,1,0:T(8,128)(2,1)S(1)}, u32[]{:S(2)}, u32[]{:S(2)}) %all-to-all-start.1) | async-done | bytes 1048608 | tf_op jit(solution)/shard_map/all_to_all | solution.py:295
  73.6 9.5 %shard_map.57 = (f32[33,128,128]{2,1,0:T(8,128)S(1)}, f32[33,1,128]{2,1,0:T(1,128)S(1)}, f32[33,8,128]{2,1,0:T(8,128)S(1)}) custom-call(s32[2048]{0:T(1024)S(1)} %pad.23.table_hbm, bf16[32,128,128]{2,1,0:T(8,128)(2,1)S(1)} %all-to-all-done.1.q_ref, bf16[32,2,128,128]{3,2,1,0:T(8,128)(2,1)S(1)} %all-to-all-done.rest_0_, ...), custom_call_target="tpu_custom_call" | custom-call | flops 1000000 | bytes 1 | tf_op jit(solution)/shard_map/pallas_call | solution.py:253
  83.1 12.6 %collective-permute-done.4.rest_0_ = bf16[18,2,128,128]{3,2,1,0:T(8,128)(2,1)} collective-permute-done((bf16[18,2,128,128]{3,2,1,0:T(8,128)(2,1)}, bf16[18,2,128,128]{3,2,1,0:T(8,128)(2,1)}, u32[]{:S(2)}, u32[]{:S(2)}) %collective-permute-start.4) | collective-permute-done | bytes 1179680 | tf_op jit(solution)/shard_map/ppermute | solution.py:299
  95.7 3.1 %collective-permute-done.5.rest_1_ = bf16[18,2,128,128]{3,2,1,0:T(8,128)(2,1)S(1)} collective-permute-done((bf16[18,2,128,128]{3,2,1,0:T(8,128)(2,1)}, bf16[18,2,128,128]{3,2,1,0:T(8,128)(2,1)S(1)}, u32[]{:S(2)}, u32[]{:S(2)}) %collective-permute-start.5) | collective-permute-done | bytes 1179680 | tf_op jit(solution)/shard_map/ppermute | solution.py:298
  98.8 5.5 %shard_map.58 = bf16[32,128,128]{2,1,0:T(8,128)(2,1)S(1)} custom-call(s32[2048]{0:T(1024)S(1)} %pad.26.table_hbm, bf16[32,128,128]{2,1,0:T(8,128)(2,1)S(1)} %all-to-all-done.1.q_ref, bf16[18,2,128,128]{3,2,1,0:T(8,128)(2,1)} %collective-permute-done.4.rest_0_, bf16[18,2,128,128]{3,2,1,0:T(8,128)(2,1)S(1)} %collective-permute-done.5.rest_1_, ...), custom_call_target="tpu_custom_call" | custom-call | flops 1000000 | bytes 1 | tf_op jit(solution)/shard_map/pallas_call | solution.py:253
  104.3 26.3 %all_to_all.15 = bf16[32,128,128]{2,1,0:T(8,128)(2,1)} all-to-all(bf16[32,128,128]{2,1,0:T(8,128)(2,1)S(1)} %shard_map.58), channel_id=1, replica_groups={{0,8,16,24,32,40,48,56,64,72,80,88,96,104,112,120,3,11,19,27,35,43,51,5..., dimensions={0} | all-to-all | bytes 2097152 | tf_op jit(solution)/shard_map/all_to_all | solution.py:295
  130.6 2.1 %shard_map.59 = bf16[128,4096]{1,0:T(8,128)(2,1)} custom-call(bf16[2,16,128,128]{3,2,1,0:T(8,128)(2,1)} %bitcast.11), custom_call_target="tpu_custom_call" | custom-call | tf_op jit(solution)/shard_map/pallas_call | solution.py:93
  (45 shorter events, 2.5 us)
Async XLA Ops:
  0.0 1.2 copy-start.1
  1.2 1.2 copy-start.2
  3.5 1.4 %copy-start = (bf16[2,16,2,128,128]{4,3,2,1,0:T(8,128)(2,1)}, bf16[2,16,2,128,128]{4,3,2,1,0:T(8,128)(2,1)S(1)}, u32[]{:S(2)}) copy-start(bf16[2,16,2,128,128]{4,3,2,1,0:T(8,128)(2,1)S(1)} %shard_map.55) | copy-start | bytes 6291460
  4.9 10.8 %copy-start.3 = (s32[1,128,48]{1,2,0:T(8,128)S(1)}, s32[1,128,48]{1,2,0:T(8,128)}, u32[]{:S(2)}) copy-start(s32[1,128,48]{1,2,0:T(8,128)} %param.8) | copy-start | bytes 73732
  4.9 10.8 %copy-start.4 = (s32[1,128]{1,0:T(1,128)S(1)}, s32[1,128]{1,0:T(1,128)}, u32[]{:S(2)}) copy-start(s32[1,128]{1,0:T(1,128)} %param.9) | copy-start | bytes 1540
  4.9 40.2 %all-to-all-start = ((bf16[32,2,128,128]{3,2,1,0:T(8,128)(2,1)}), bf16[32,2,128,128]{3,2,1,0:T(8,128)(2,1)S(1)}, u32[]{:S(2)}, u32[]{:S(2)}) async-start(bf16[32,2,128,128]{3,2,1,0:T(8,128)(2,1)} %bitcast.9), calls=%async_computation | async-start | bytes 4194304 | tf_op jit(solution)/shard_map/all_to_all | solution.py:295
  15.9 2.2 %collective-permute-start = (s32[128,49]{1,0:T(8,128)S(1)}, s32[128,49]{1,0:T(8,128)S(1)}, u32[]{:S(2)}, u32[]{:S(2)}) collective-permute-start(s32[128,49]{1,0:T(8,128)S(1)} %copy.17), channel_id=1, source_target_pairs={{0,4},{4,0},{8,12},{12,8},{16,20},{20,16},{24,28},{28,24},{32,36},... | collective-permute-start | bytes 75272 | tf_op jit(solution)/shard_map/ppermute | solution.py:298
  46.3 27.4 %collective-permute-start.1 = (bf16[32,2,128,128]{3,2,1,0:T(8,128)(2,1)S(1)}, bf16[32,2,128,128]{3,2,1,0:T(8,128)(2,1)}, u32[]{:S(2)}, u32[]{:S(2)}) collective-permute-start(bf16[32,2,128,128]{3,2,1,0:T(8,128)(2,1)S(1)} %all-to-all-done.rest_0_), channel_id=1, source_target_pairs={{0,4},{4,0},{8,12},{12,8},{16,20},{20,16},{24,28},{28,24},{32,36},... | collective-permute-start | bytes 6291464 | tf_op jit(solution)/shard_map/ppermute | solution.py:298
  47.4 23.5 %collective-permute-start.2 = (bf16[14,2,128,128]{3,2,1,0:T(8,128)(2,1)}, bf16[14,2,128,128]{3,2,1,0:T(8,128)(2,1)}, u32[]{:S(2)}, u32[]{:S(2)}) collective-permute-start(bf16[14,2,128,128]{3,2,1,0:T(8,128)(2,1)} %slice.35), channel_id=1, source_target_pairs={{0,1},{1,0},{2,3},{3,2},{4,5},{5,4},{6,7},{7,6},{8,9},{9,8},{10,11... | collective-permute-start | bytes 2752520 | tf_op jit(solution)/shard_map/ppermute | solution.py:299
  47.4 48.4 %collective-permute-start.4 = (bf16[18,2,128,128]{3,2,1,0:T(8,128)(2,1)}, bf16[18,2,128,128]{3,2,1,0:T(8,128)(2,1)}, u32[]{:S(2)}, u32[]{:S(2)}) collective-permute-start(bf16[18,2,128,128]{3,2,1,0:T(8,128)(2,1)} %slice.34), channel_id=1, source_target_pairs={{0,1},{1,0},{2,3},{3,2},{4,5},{5,4},{6,7},{7,6},{8,9},{9,8},{10,11... | collective-permute-start | bytes 3538952 | tf_op jit(solution)/shard_map/ppermute | solution.py:299
  49.4 24.1 %all-to-all-start.1 = ((bf16[32,128,128]{2,1,0:T(8,128)(2,1)}), bf16[32,128,128]{2,1,0:T(8,128)(2,1)S(1)}, u32[]{:S(2)}, u32[]{:S(2)}) async-start(bf16[32,128,128]{2,1,0:T(8,128)(2,1)} %bitcast.10), calls=%async_computation.1 | async-start | bytes 2097152 | tf_op jit(solution)/shard_map/all_to_all | solution.py:295
  70.8 2.8 %collective-permute-start.3 = (bf16[14,2,128,128]{3,2,1,0:T(8,128)(2,1)}, bf16[14,2,128,128]{3,2,1,0:T(8,128)(2,1)}, u32[]{:S(2)}, u32[]{:S(2)}) collective-permute-start(bf16[14,2,128,128]{3,2,1,0:T(8,128)(2,1)} %collective-permute-done.2.rest_2_), channel_id=1, source_target_pairs={{0,4},{4,0},{8,12},{12,8},{16,20},{20,16},{24,28},{28,24},{32,36},... | collective-permute-start | bytes 2752520 | tf_op jit(solution)/shard_map/ppermute | solution.py:298
  95.7 3.1 %collective-permute-start.5 = (bf16[18,2,128,128]{3,2,1,0:T(8,128)(2,1)}, bf16[18,2,128,128]{3,2,1,0:T(8,128)(2,1)S(1)}, u32[]{:S(2)}, u32[]{:S(2)}) collective-permute-start(bf16[18,2,128,128]{3,2,1,0:T(8,128)(2,1)} %collective-permute-done.4.rest_0_), channel_id=1, source_target_pairs={{0,4},{4,0},{8,12},{12,8},{16,20},{20,16},{24,28},{28,24},{32,36},... | collective-permute-start | bytes 3538952 | tf_op jit(solution)/shard_map/ppermute | solution.py:298
